TPU v7x, 32 devices: a whole 2x2x4 slice. The times are simulated.
32 devices in a mesh: gx: 4 (over x, core), gy: 8 (over z, y).
Axes of the slice: x: 2, y: 2, z: 4, core: 2. Of those that a mesh axis runs over, the one named last changes fastest.
Arguments:
- model_state: float32 [16, 256, 528], P('gx', 'gy'), may hold values from -6 to 6
- hyper_coef: float32 [528], replicated, may hold values from 0.0001 to 0.001
- point_mass: float32 [16, 256], P('gx', 'gy'), may hold values from 0.5 to 2
- inverse_mass: float32 [16, 256], P('gx', 'gy'), may hold values from 0.2 to 0.8
- span_slot: int32 [16, 256], P('gx', 'gy'), may hold values from 0 to 511, as said below
- vert_diff: float32 [8, 48, 512], P('gy', None, 'gx'), may hold values from 0.05 to 20
- fall_rate: float32 [8, 48, 512], P('gy', None, 'gx'), may hold values from 0.1 to 10
- cloud_frac: float32 [8, 48, 512], P('gy', None, 'gx'), may hold values from 0 to 1
Outputs:
- new_state: float32 [16, 256, 528], P('gx', 'gy')
Inputs may be any that keep to these rules, and one draw needn't show every extreme that they name: `span_slot`: within the columns that share a block of 32 along the second dimension, the values form a permutation; each device's 128 columns hold exactly 32 values in each range from p * 128 to (p + 1) * 128 - 1.
All inputs are finite; a program needn't handle non-finite values.
Results may differ from a plain program's by a relative error of at most 0.0003.
Values sent between devices are 32-bit elements; how exact they have to be, the bound alone decides.
No kernel may reach another device: no remote copies, remote signals or barrier semaphores. Data moves between devices by JAX's collectives and lax.ppermute only.
A program may use at most 64 MiB of HBM per device.

v0:
```python
import functools

import jax
import jax.numpy as jnp
import numpy as np
from jax import lax
from jax.experimental import pallas as pl
from jax.experimental.pallas import tpu as pltpu
from jax.sharding import PartitionSpec as P

VMEM = pl.BlockSpec(memory_space=pltpu.VMEM)
PARAMS = pltpu.CompilerParams(vmem_limit_bytes=16 * 1024 * 1024)


def second_table():
    nodes = np.array([-1.0, -1.0 / np.sqrt(5.0), 1.0 / np.sqrt(5.0), 1.0])
    deriv = np.zeros((4, 4))
    for i in range(4):
        for j in range(4):
            if i == j:
                deriv[i, j] = sum(1.0 / (nodes[i] - nodes[k]) for k in range(4) if k != i)
            else:
                upper = np.prod([nodes[i] - nodes[k] for k in range(4) if k != i])
                lower = np.prod([nodes[j] - nodes[k] for k in range(4) if k != j])
                deriv[i, j] = upper / (lower * (nodes[i] - nodes[j]))
    return deriv @ deriv


def laplacian_tables(size_x, size_y):
    second = second_table()
    lap = np.kron(np.kron(np.eye(size_x // 4), second), np.eye(size_y))
    lap = lap + np.kron(np.eye(size_x), np.kron(np.eye(size_y // 4), second))
    partner = np.zeros_like(lap)
    for x in range(size_x):
        for y in range(size_y):
            other = y - 1 if y % 4 == 0 else y + 1 if y % 4 == 3 else -1
            if 0 <= other < size_y:
                partner[x * size_y + y] = lap[x * size_y + other]
    return np.stack([lap, partner]).astype(np.float32)


def split(value):
    high = value.astype(jnp.bfloat16)
    return high, (value - high.astype(jnp.float32)).astype(jnp.bfloat16)


def product(left, right):
    left_high, left_low = left
    right_high, right_low = right
    dot = functools.partial(jnp.dot, preferred_element_type=jnp.float32)
    return dot(left_high, right_high) + (dot(left_high, right_low) + dot(left_low, right_high))


def to_column(plane, partner=False):
    size_x, size_y = plane.shape
    row = lax.broadcasted_iota(jnp.int32, (size_y, size_y), 0)
    lane = lax.broadcasted_iota(jnp.int32, (size_y, size_y), 1)
    if partner:
        row = jnp.where(row % 4 == 0, row - 1, jnp.where(row % 4 == 3, row + 1, -1))
    pick = row == lane
    parts = [
        jnp.sum(jnp.where(pick, plane[x : x + 1, :], 0.0), axis=1, keepdims=True)
        for x in range(size_x)
    ]
    return jnp.concatenate(parts, axis=0)


def even(axis):
    return lax.rem(lax.axis_index(axis), 2) == 0


def x_rows(count, size_y):
    near = jnp.where(even("gx"), count - size_y, 0)
    far = count - size_y - near
    return tuple(pl.ds(pl.multiple_of(start, size_y), size_y) for start in (near, far))


COEF_ROWS = 32


def write_coefs(message, start, coefs):
    rows, lanes = coefs.shape
    for i, first in enumerate(range(0, rows, COEF_ROWS)):
        part = coefs[first : min(first + COEF_ROWS, rows)]
        message[start : start + part.shape[0], i * lanes : (i + 1) * lanes] = part


def read_coefs(message, start, rows, lanes):
    parts = []
    for i, first in enumerate(range(0, rows, COEF_ROWS)):
        count = min(COEF_ROWS, rows - first)
        parts.append(message[start : start + count, i * lanes : (i + 1) * lanes])
    return jnp.concatenate(parts, axis=0)


def start_kernel(
    state,
    mass,
    inverse,
    diff,
    fall,
    cloud,
    tables,
    here,
    total,
    x_near,
    x_far,
    low,
    high,
    operator,
    columns,
    coefs,
    mass_here,
    inverse_here,
    tables_here,
    sems,
):
    size_x, size_y, width = state.shape
    levels = diff.shape[1]
    pairs = [(mass, mass_here), (tables, tables_here), (inverse, inverse_here), (state, here)]
    for i, source in enumerate((diff, fall, cloud)):
        pairs.append((source.at[0], coefs.at[i * levels : (i + 1) * levels]))
    copies = [
        pltpu.make_async_copy(source, target, sems.at[i])
        for i, (source, target) in enumerate(pairs)
    ]
    for copy in copies:
        copy.start()
    for copy in copies[:3]:
        copy.wait()
    own = to_column(mass_here[...])
    lane = lax.broadcasted_iota(jnp.int32, columns.shape, 1)
    partner = to_column(mass_here[...], True)
    inverses = to_column(inverse_here[...])
    columns[...] = jnp.where(lane == 0, own, jnp.where(lane == 1, inverses, partner))
    matrix = own * tables_here[0] + partner * tables_here[1]
    operator[...] = matrix
    copies[3].wait()
    total[...] = product(split(matrix), split(here[...].reshape(size_x * size_y, width)))
    for first, message in ((0, low), (size_y - 4, high)):
        for x in range(size_x):
            for i in range(4):
                row = x * size_y + first + i
                place = i * size_x + x
                message[place : place + 1, :width] = total[row : row + 1, :]
                message[place : place + 1, width : width + 2] = columns[row : row + 1, :2]
    near, far = x_rows(size_x * size_y, size_y)
    x_near[...] = total[near]
    x_far[:size_y, :width] = total[far]
    for copy in copies[4:]:
        copy.wait()
    if x_far.shape[0] > size_y:
        write_coefs(x_far, size_y, coefs)


def edge_rows(ref, y, size_x, size_y):
    return jnp.concatenate(
        [ref[x * size_y + y : x * size_y + y + 1, :] for x in range(size_x)], axis=0
    )


def node_column(values, start, count):
    row = lax.broadcasted_iota(jnp.int32, (count, 1), 0)
    result = jnp.zeros((count, 1), jnp.float32)
    for i, value in enumerate(values):
        result = jnp.where(row == start + i, float(value), result)
    return result


def edge_weights(columns, message, size_x, size_y, width, edge, line):
    second = second_table()
    other = size_x - 1 - edge
    low = line == 3
    y, first = (0, 0) if low else (size_y - 1, size_y - 8)
    rows = slice(edge * size_y + first, edge * size_y + first + 8)
    here, there = (slice(x * size_y + y, x * size_y + y + 1) for x in (edge, other))
    mass, inverse = columns[here, 0:1], columns[here, 1:2]
    beyond = slice(line * size_x + edge, line * size_x + edge + 1)
    beyond_mass = message[beyond, width : width + 1]

    def beyond_inverse(i, x):
        return message[i * size_x + x : i * size_x + x + 1, width + 1 : width + 2]

    if low:
        own, partner = node_column(second[:, 0], 0, 8), node_column(second[3:, 0], 4, 8)
    else:
        own, partner = node_column(second[:, 3], 4, 8), node_column(second[:1, 3], 3, 8)
    along = inverse * (own * columns[rows, 0:1] + partner * columns[rows, 2:3])
    lane = lax.broadcasted_iota(jnp.int32, (8, 128), 1) - width % 128
    place = lax.broadcasted_iota(jnp.int32, (8, 128), 0)
    tile = jnp.where(lane == line, along, 0.0)
    for i in range(4):
        value = float(second[line, i]) * beyond_mass * beyond_inverse(i, edge)
        if i == line:
            across = beyond_mass * beyond_inverse(line, edge) + mass * inverse
            value = value + float(second[edge, edge]) * across
        tile = tile + jnp.where((place == y - first) & (lane == i), value, 0.0)
    across = beyond_mass * beyond_inverse(line, other) + mass * columns[there, 1:2]
    value = float(second[edge, other]) * across
    return tile + jnp.where((place == y - first) & (lane == 4), value, 0.0)


def second_kernel(
    size_x,
    total,
    columns,
    operator,
    coefs,
    from_far,
    from_near,
    low,
    high,
    out,
    x_near,
    x_far,
    line_ends,
    inner,
    work,
):
    size_y, width = from_near.shape
    second = second_table()
    near, far = x_rows(size_x * size_y, size_y)
    work[...] = total[...]
    work[near] += from_near[...]
    work[far] += from_far[:size_y, :width]
    sides = ((low, 0, 3, 0), (high, size_y - 1, 0, size_y - 8))
    beyond = []
    for message, y, line, _ in sides:
        lines = [message[i * size_x : (i + 1) * size_x, :width] for i in range(4)]
        lines[line] = lines[line] + edge_rows(work, y, size_x, size_y)
        for x in range(size_x):
            work[x * size_y + y : x * size_y + y + 1, :] = lines[line][x : x + 1]
        for i in range(4):
            inverse = message[i * size_x : (i + 1) * size_x, width + 1 : width + 2]
            lines[i] = inverse * lines[i]
        value = sum(float(second[line, i]) * lines[i] for i in range(4))
        for x in range(size_x):
            value = value + node_column(second[:, x], 0, size_x) * lines[line][x : x + 1]
        mass = message[line * size_x : (line + 1) * size_x, width : width + 1]
        beyond.append(mass * value)
    out[...] = product(split(operator[...]), split(columns[:, 1:2] * work[...]))
    for (_, y, _, _), rows in zip(sides, beyond):
        for x in range(size_x):
            out[x * size_y + y : x * size_y + y + 1, :] += rows[x : x + 1]

    first, last = 0, size_x - 1
    x_near[:size_y, :width] = out[near]
    x_far[:size_y, :width] = out[far]
    for side, (message, y, line, start) in enumerate(sides):
        tiles = {
            edge: edge_weights(columns, message, size_x, size_y, width, edge, line)
            for edge in (first, last)
        }
        behind = slice(width % 128, 128)
        rows = slice(start, start + 8)
        x_near[rows, width:] = jnp.where(even("gx"), tiles[last], tiles[first])[:, behind]
        x_far[rows, width:] = jnp.where(even("gx"), tiles[first], tiles[last])[:, behind]
        for i in range(4):
            rows = [message[i * size_x + x : i * size_x + x + 1, :width] for x in (first, last)]
            at_near = jnp.where(even("gx"), rows[1], rows[0])
            at_far = jnp.where(even("gx"), rows[0], rows[1])
            place = size_y + 4 * side + i
            x_near[place : place + 1, :width] = at_near
            x_far[place : place + 1, :width] = at_far
            if i == line:
                line_ends[2 * side : 2 * side + 1, :] = at_far
                line_ends[2 * side + 1 : 2 * side + 2, :] = at_near
        mass = message[line * size_x : (line + 1) * size_x, width : width + 1]
        own = edge_rows(columns, y, size_x, size_y)
        weights = []
        for edge in (first, last):
            inverse = message[line * size_x + edge : line * size_x + edge + 1, width + 1 : width + 2]
            across = mass * inverse + own[:, 0:1] * own[edge : edge + 1, 1:2]
            weights.append(node_column(second[:, edge], 0, size_x) * across)
        lane = lax.broadcasted_iota(jnp.int32, (size_x, 128), 1)
        from_last = jnp.where(even("gx"), 0, 1)
        inner[side * size_x : (side + 1) * size_x, :] = jnp.where(
            lane == from_last, weights[1], weights[0]
        )
    if x_near.shape[0] > size_y + 8:
        write_coefs(x_near, size_y + 8, coefs)
        x_near[size_y + 8 + COEF_ROWS :, :] = from_far[size_y:, :]


def third_kernel(
    levels,
    state,
    hyper,
    total,
    masses,
    inner,
    factors,
    to_near,
    to_far,
    from_far,
    from_near,
    ends_near,
    ends_far,
    out,
    work,
    turned,
    values,
):
    columns, width = total.shape
    size_x, size_y, _ = state.shape
    variables = width // levels
    near = jnp.where(even("gx"), columns - size_y, 0)
    sides = ((0, 0, 3, 0), (1, size_y - 1, 0, size_y - 8))
    partners = (
        (near, to_near, from_near, from_far, ends_near, 0),
        (columns - size_y - near, to_far, from_far, from_near, ends_far, 1),
    )
    work[...] = total[...]
    for start, _, theirs, _, _, _ in partners:
        work[pl.ds(pl.multiple_of(start, size_y), size_y), :] += theirs[:size_y, :width]
    for side, y, line, first in sides:
        place = size_y + 4 * side
        tile = slice(first, first + 8)
        for start, mine, theirs, others, ends, which in partners:
            terms = [
                (weights, i, rows, place + i)
                for i in range(4)
                for weights, rows in ((mine, theirs), (theirs, mine))
            ]
            terms += [(mine, 4, others, place + line), (theirs, 4, ends, 2 * side + which)]
            added = sum(
                weights[tile, width + i : width + i + 1] * rows[row : row + 1, :width]
                for weights, i, rows, row in terms
            )
            work[pl.ds(pl.multiple_of(start + first, 8), 8), :] += added
        for x in range(1, size_x - 1):
            row, weight = x * size_y + y, side * size_x + x
            work[row : row + 1, :] += (
                inner[weight : weight + 1, 0:1] * from_near[place + line : place + line + 1, :width]
                + inner[weight : weight + 1, 1:2] * from_far[place + line : place + line + 1, :width]
            )
    twice = masses[:, 1:2] * work[...]
    turned[...] = (state[...].reshape(columns, width) - hyper[...] * twice).T
    scale, down, up, keep, flow, cloud = (
        factors.at[i * levels : (i + 1) * levels] for i in range(6)
    )
    value = jnp.zeros((variables, columns), jnp.float32)
    for k in range(levels):
        rows = turned[pl.ds(k, variables, stride=levels), :]
        value = rows * scale[k : k + 1, :] + down[k : k + 1, :] * value
        values[k, :variables, :] = value
    solved = jnp.zeros((variables, columns), jnp.float32)
    for k in reversed(range(levels)):
        solved = values[k, :variables, :] + up[k : k + 1, :] * solved
        turned[pl.ds(k, variables, stride=levels), :] = solved
    heat, vapour, liquid = (turned.at[i * levels : (i + 1) * levels] for i in range(3))
    condensed = cloud[...] * 0.5 * jnp.maximum(vapour[...] - 0.3 * heat[...], 0.0)
    vapour[...] = vapour[...] - condensed
    heat[...] = heat[...] + 2.0 * condensed
    liquid[...] = (liquid[...] + condensed) * keep[...]
    settled = jnp.zeros((1, columns), jnp.float32)
    for k in range(levels):
        settled = liquid[k : k + 1, :] + flow[k : k + 1, :] * settled
        liquid[k : k + 1, :] = settled
    out[...] = turned[...].T.reshape(out.shape)


def factor_kernel(levels, span, slots, *refs):
    rows = 3 * levels
    size_x, size_y = slots.shape
    columns = size_x * size_y
    factors = refs[-1]
    if len(refs) == 4:
        own, from_far, from_near = refs[:3]
        here = lax.axis_index("gx")
        pieces = [
            (here, own[...]),
            (here ^ 3, read_coefs(from_far, size_y, rows, span)),
            (here ^ 1, read_coefs(from_near, size_y + 8, rows, span)),
            (here ^ 2, read_coefs(from_near, size_y + 8 + COEF_ROWS, rows, span)),
        ]
    else:
        pieces = [(peer, refs[0][peer]) for peer in range(refs[0].shape[0])]
    picked = jnp.zeros((rows, columns), jnp.float32)
    wanted = jnp.concatenate([slots[x : x + 1, :] for x in range(size_x)], axis=1)
    for owner, rest in pieces:
        entry = lax.broadcasted_iota(jnp.int32, (span, columns), 0) + owner * span
        choice = (entry == wanted).astype(jnp.float32).astype(jnp.bfloat16)
        for _ in range(3):
            part = rest.astype(jnp.bfloat16)
            rest = rest - part.astype(jnp.float32)
            picked = picked + jnp.dot(part, choice, preferred_element_type=jnp.float32)
    mixing, falling, covered = (picked[i * levels : (i + 1) * levels] for i in range(3))
    scale, down, up, keep, flow, cover = (
        factors.at[i * levels : (i + 1) * levels] for i in range(6)
    )
    gain = jnp.zeros((1, columns), jnp.float32)
    for k in range(levels):
        above = mixing[k : k + 1] if k else jnp.zeros_like(gain)
        below = mixing[k + 1 : k + 2] if k + 1 < levels else jnp.zeros_like(gain)
        centre = 1.0 + above + (below if k + 1 < levels else mixing[:1])
        inverse = 1.0 / (centre - above * gain)
        gain = below * inverse
        scale[k : k + 1, :] = inverse
        down[k : k + 1, :] = above * inverse
        up[k : k + 1, :] = gain
    kept = 1.0 / (1.0 + falling)
    keep[...] = kept
    flow[:1, :] = jnp.zeros((1, columns), jnp.float32)
    flow[1:, :] = falling[:-1] * kept[1:]
    cover[...] = covered


def swapped(value, axis, partner):
    return lax.ppermute(value, axis, [(i, partner(i)) for i in range(lax.axis_size(axis))])


def exchanged(near, far, axis):
    size = lax.axis_size(axis)
    from_far = swapped(far, axis, lambda i: (i + (1 if i % 2 else -1)) % size)
    from_near = swapped(near, axis, lambda i: i ^ 1)
    return from_far, from_near


def shifted(value, axis, step):
    size = lax.axis_size(axis)
    return lax.ppermute(value, axis, [(i, (i + step) % size) for i in range(size)])


def local(
    model_state, hyper_coef, point_mass, inverse_mass, span_slot, vert_diff, fall_rate, cloud_frac
):
    size_x, size_y, width = model_state.shape
    levels, span = vert_diff.shape[1:]
    columns = size_x * size_y
    hyper = hyper_coef.reshape(1, width)
    padded = -(-(width + 5) // 128) * 128
    tables = jnp.asarray(laplacian_tables(size_x, size_y))

    def array(*shape):
        return jax.ShapeDtypeStruct(shape, jnp.float32)

    def scratch(*shape):
        return pltpu.VMEM(shape, jnp.float32)

    def call(kernel, name, outs, scratches, *operands, spec=VMEM):
        return pl.pallas_call(
            kernel,
            out_shape=outs,
            in_specs=[spec] * len(operands),
            out_specs=[VMEM] * len(outs),
            scratch_shapes=scratches,
            compiler_params=PARAMS,
            name=name,
        )(*operands)

    riding = lax.axis_size("gx") == 4
    extra = COEF_ROWS if riding else 0
    whole, line = array(columns, width), array(size_y, width)
    edge = array(4 * size_x, padded)
    here, total, x_near, x_far, y_low, y_high, operator, masses, coefs = call(
        start_kernel,
        "start",
        [
            array(size_x, size_y, width),
            whole,
            line,
            array(size_y + extra, padded),
            edge,
            edge,
            array(columns, columns),
            array(columns, 128),
            array(3 * levels, span),
        ],
        [
            scratch(size_x, size_y),
            scratch(size_x, size_y),
            scratch(*tables.shape),
            pltpu.SemaphoreType.DMA((7,)),
        ],
        *(
            pltpu.with_memory_space_constraint(value, pltpu.HBM)
            for value in (
                model_state,
                point_mass,
                inverse_mass,
                vert_diff,
                fall_rate,
                cloud_frac,
                tables,
            )
        ),
        spec=pl.BlockSpec(memory_space=pltpu.HBM),
    )
    from_x = exchanged(x_near, x_far, "gx")
    total, x_near, x_far, line_ends, inner = call(
        functools.partial(second_kernel, size_x),
        "second",
        [
            whole,
            array(size_y + 8 + 2 * extra, padded),
            array(size_y + 8, padded),
            array(4, width),
            array(2 * size_x, 128),
        ],
        [scratch(columns, width)],
        total,
        masses,
        operator,
        coefs,
        *from_x,
        shifted(y_high, "gy", 1),
        shifted(y_low, "gy", -1),
    )
    last_x = exchanged(x_near, x_far, "gx")
    peers = lax.axis_size("gx")
    ends_near = swapped(line_ends, "gx", lambda i: (i + (2 if i % 2 else -2)) % peers)
    ends_far = ends_near
    if peers != 4:
        ends_far = swapped(line_ends, "gx", lambda i: (i - (2 if i % 2 else -2)) % peers)
    if riding:
        pieces = [coefs, from_x[0], last_x[1]]
    else:
        pieces = [lax.all_gather(coefs, "gx")]
    (factors,) = call(
        functools.partial(factor_kernel, levels, span),
        "factors",
        [array(6 * levels, columns)],
        [],
        span_slot,
        *pieces,
    )
    (result,) = call(
        functools.partial(third_kernel, levels),
        "third",
        [array(size_x, size_y, width)],
        [scratch(columns, width), scratch(width, columns), scratch(levels, 16, columns)],
        here,
        hyper,
        total,
        masses,
        inner,
        factors,
        x_near,
        x_far,
        *last_x,
        ends_near,
        ends_far,
    )
    return result


def solution(mesh):
    placed = (
        P("gx", "gy", None),
        P(),
        P("gx", "gy"),
        P("gx", "gy"),
        P("gx", "gy"),
        P("gy", None, "gx"),
        P("gy", None, "gx"),
        P("gy", None, "gx"),
    )
    return jax.shard_map(
        local, mesh=mesh, in_specs=placed, out_specs=P("gx", "gy", None), check_vma=False
    )
```

profile of v0, /device:TPU:0, one launch (start us, length us, event | category | flops | bytes accessed | tf_op | source)
XLA Modules:
  0.0 19.1 jit_solution(6845593094410458346)
XLA Ops:
  0.0 1.6 %start.1 = (f32[4,32,528]{2,1,0:T(8,128)S(1)}, f32[128,528]{1,0:T(8,128)S(1)}, f32[32,528]{1,0:T(8,128)S(1)}, f32[64,640]{1,0:T(8,128)S(1)}, f32[16,640]{1,0:T(8...) custom-call(f32[4,32,528]{2,1,0:T(8,128)} %state.1, ...), custom_call_target="tpu_custom_call" | custom-call | tf_op jit(solution)/shard_map/start/pallas_call | solution.py:442
  1.6 2.4 %collective-permute-start = (f32[64,640]{1,0:T(8,128)S(1)}, f32[64,640]{1,0:T(8,128)S(1)}, u32[]{:S(2)}, u32[]{:S(2)}) collective-permute-start(f32[64,640]{1,0:T(8,128)S(1)} %get-tuple-element.24), channel_id=1, source_target_pairs={{0,24},{8,16},{16,8},{24,0},{1,25},{9,17},{17,9},{25,1},{2,26},{10... | collective-permute-start | bytes 491528 | tf_op jit(solution)/shard_map/ppermute | solution.py:410
  4.1 0.7 %collective-permute-start.1 = (f32[32,528]{1,0:T(8,128)S(1)}, f32[32,528]{1,0:T(8,128)S(1)}, u32[]{:S(2)}, u32[]{:S(2)}) collective-permute-start(f32[32,528]{1,0:T(8,128)S(1)} %get-tuple-element.25), channel_id=1, source_target_pairs={{0,8},{8,0},{16,24},{24,16},{1,9},{9,1},{17,25},{25,17},{2,10},{10... | collective-permute-start | bytes 202760 | tf_op jit(solution)/shard_map/ppermute | solution.py:410
  4.8 1.5 %collective-permute-start.2 = (f32[16,640]{1,0:T(8,128)S(1)}, f32[16,640]{1,0:T(8,128)S(1)}, u32[]{:S(2)}, u32[]{:S(2)}) collective-permute-start(f32[16,640]{1,0:T(8,128)S(1)} %get-tuple-element.26), channel_id=1, source_target_pairs={{0,1},{1,2},{2,3},{3,4},{4,5},{5,6},{6,7},{7,0},{8,9},{9,10},{10,1... | collective-permute-start | bytes 122888 | tf_op jit(solution)/shard_map/ppermute | solution.py:422
  6.3 3.2 %collective-permute-start.3 = (f32[16,640]{1,0:T(8,128)S(1)}, f32[16,640]{1,0:T(8,128)S(1)}, u32[]{:S(2)}, u32[]{:S(2)}) collective-permute-start(f32[16,640]{1,0:T(8,128)S(1)} %get-tuple-element.27), channel_id=1, source_target_pairs={{0,7},{1,0},{2,1},{3,2},{4,3},{5,4},{6,5},{7,6},{8,15},{9,8},{10,9... | collective-permute-start | bytes 122888 | tf_op jit(solution)/shard_map/ppermute | solution.py:422
  9.5 2.0 %collective-permute-done.2.low = f32[16,640]{1,0:T(8,128)S(1)} collective-permute-done((f32[16,640]{1,0:T(8,128)S(1)}, f32[16,640]{1,0:T(8,128)S(1)}, u32[]{:S(2)}, u32[]{:S(2)}) %collective-permute-start.2) | collective-permute-done | bytes 40992 | tf_op jit(solution)/shard_map/ppermute | solution.py:422
  11.5 0.0 collective-permute-done.3.high
  11.5 0.0 collective-permute-done.1.from_near
  11.5 0.0 collective-permute-done.from_far.refs_1_
  11.5 0.5 %second.1 = (f32[128,528]{1,0:T(8,128)S(1)}, f32[104,640]{1,0:T(8,128)S(1)}, f32[40,640]{1,0:T(8,128)S(1)}, f32[4,528]{1,0:T(4,128)S(1)}, f32[8,128]{1,0:T(8,128)S(1)}) custom-call(f32[128,528]{1,0:T(8,128)S(1)} %get-tuple-element.20.total, f32[128,128]{1,0:T(8,128)S(1)} %get-tuple-element.21.columns.masses, f32[128,128]{1,0:T(8,128)S(1)} %get-tuple-element.22.operator, ...), custom_call_target="tpu_custom_call" | custom-call | tf_op jit(solution)/shard_map/second/pallas_call | solution.py:442
  11.9 0.0 copy-start.1
  12.0 0.1 collective-permute-start.4
  12.0 0.5 %collective-permute-start.5 = (f32[40,640]{1,0:T(8,128)S(1)}, f32[40,640]{1,0:T(8,128)S(1)}, u32[]{:S(2)}, u32[]{:S(2)}) collective-permute-start(f32[40,640]{1,0:T(8,128)S(1)} %get-tuple-element.31.to_far), channel_id=1, source_target_pairs={{0,24},{8,16},{16,8},{24,0},{1,25},{9,17},{17,9},{25,1},{2,26},{10... | collective-permute-start | bytes 307208 | tf_op jit(solution)/shard_map/ppermute | solution.py:410
  12.5 0.0 copy-start
  12.5 1.7 %collective-permute-start.6 = (f32[4,528]{1,0:T(4,128)S(1)}, f32[4,528]{1,0:T(4,128)S(1)}, u32[]{:S(2)}, u32[]{:S(2)}) collective-permute-start(f32[4,528]{1,0:T(4,128)S(1)} %get-tuple-element.32), channel_id=1, source_target_pairs={{0,16},{8,24},{16,0},{24,8},{1,17},{9,25},{17,1},{25,9},{2,18},{10... | collective-permute-start | bytes 25352 | tf_op jit(solution)/shard_map/ppermute | solution.py:410
  14.2 0.0 copy-done.1
  14.2 0.0 collective-permute-done.4.refs_2_.from_near
  14.2 0.0 copy-done
  14.2 0.9 %factors.1 = f32[288,128]{1,0:T(8,128)S(1)} custom-call(s32[4,32]{1,0:T(4,128)S(1)} %copy-done, f32[144,128]{1,0:T(8,128)S(1)} %get-tuple-element.23.coefs.refs_0_, f32[64,640]{1,0:T(8,128)S(1)} %collective-permute-done.from_far.refs_1_, f32[104,640]{1,0:T(8,128)S(1)} %collective-permute-done.4.refs_2_.from_near), custom_call_target="tpu_custom_call" | custom-call | tf_op jit(solution)/shard_map/factors/pallas_call | solution.py:442
  15.1 2.4 %collective-permute-done.6.ends_near.ends_far = f32[4,528]{1,0:T(4,128)S(1)} collective-permute-done((f32[4,528]{1,0:T(4,128)S(1)}, f32[4,528]{1,0:T(4,128)S(1)}, u32[]{:S(2)}, u32[]{:S(2)}) %collective-permute-start.6) | collective-permute-done | bytes 8480 | tf_op jit(solution)/shard_map/ppermute | solution.py:410
  17.5 0.0 collective-permute-done.5.from_far
  17.5 1.6 %third.1 = f32[4,32,528]{2,1,0:T(8,128)} custom-call(f32[4,32,528]{2,1,0:T(8,128)S(1)} %get-tuple-element.19.state, f32[1,528]{1,0:T(1,128)S(1)} %reshape.3.hyper, f32[128,528]{1,0:T(8,128)S(1)} %get-tuple-element.28.total, f32[128,128]{1,0:T(8,128)S(1)} %get-tuple-element.21.columns.masses, f32[8,128]{1,0:T(8,128)S(1)} %get-tuple-element.29.inner, ...), custom_call_target="tpu_custom_call" | custom-call | tf_op jit(solution)/shard_map/third/pallas_call | solution.py:442
  (1 shorter events, 0.0 us)
Async XLA Ops:
  1.6 9.8 %collective-permute-start = (f32[64,640]{1,0:T(8,128)S(1)}, f32[64,640]{1,0:T(8,128)S(1)}, u32[]{:S(2)}, u32[]{:S(2)}) collective-permute-start(f32[64,640]{1,0:T(8,128)S(1)} %get-tuple-element.24), channel_id=1, source_target_pairs={{0,24},{8,16},{16,8},{24,0},{1,25},{9,17},{17,9},{25,1},{2,26},{10... | collective-permute-start | bytes 491528 | tf_op jit(solution)/shard_map/ppermute | solution.py:410
  4.1 7.4 %collective-permute-start.1 = (f32[32,528]{1,0:T(8,128)S(1)}, f32[32,528]{1,0:T(8,128)S(1)}, u32[]{:S(2)}, u32[]{:S(2)}) collective-permute-start(f32[32,528]{1,0:T(8,128)S(1)} %get-tuple-element.25), channel_id=1, source_target_pairs={{0,8},{8,0},{16,24},{24,16},{1,9},{9,1},{17,25},{25,17},{2,10},{10... | collective-permute-start | bytes 202760 | tf_op jit(solution)/shard_map/ppermute | solution.py:410
  4.8 6.7 %collective-permute-start.2 = (f32[16,640]{1,0:T(8,128)S(1)}, f32[16,640]{1,0:T(8,128)S(1)}, u32[]{:S(2)}, u32[]{:S(2)}) collective-permute-start(f32[16,640]{1,0:T(8,128)S(1)} %get-tuple-element.26), channel_id=1, source_target_pairs={{0,1},{1,2},{2,3},{3,4},{4,5},{5,6},{6,7},{7,0},{8,9},{9,10},{10,1... | collective-permute-start | bytes 122888 | tf_op jit(solution)/shard_map/ppermute | solution.py:422
  6.3 5.2 %collective-permute-start.3 = (f32[16,640]{1,0:T(8,128)S(1)}, f32[16,640]{1,0:T(8,128)S(1)}, u32[]{:S(2)}, u32[]{:S(2)}) collective-permute-start(f32[16,640]{1,0:T(8,128)S(1)} %get-tuple-element.27), channel_id=1, source_target_pairs={{0,7},{1,0},{2,1},{3,2},{4,3},{5,4},{6,5},{7,6},{8,15},{9,8},{10,9... | collective-permute-start | bytes 122888 | tf_op jit(solution)/shard_map/ppermute | solution.py:422
  11.9 2.2 %copy-start.1 = (f32[528]{0:T(1024)S(1)}, f32[528]{0:T(1024)}, u32[]{:S(2)}) copy-start(f32[528]{0:T(1024)} %param.10) | copy-start | bytes 6340
  12.0 2.2 %collective-permute-start.4 = (f32[104,640]{1,0:T(8,128)S(1)}, f32[104,640]{1,0:T(8,128)S(1)}, u32[]{:S(2)}, u32[]{:S(2)}) collective-permute-start(f32[104,640]{1,0:T(8,128)S(1)} %get-tuple-element.30.to_near), channel_id=1, source_target_pairs={{0,8},{8,0},{16,24},{24,16},{1,9},{9,1},{17,25},{25,17},{2,10},{10... | collective-permute-start | bytes 798728 | tf_op jit(solution)/shard_map/ppermute | solution.py:410
  12.0 5.5 %collective-permute-start.5 = (f32[40,640]{1,0:T(8,128)S(1)}, f32[40,640]{1,0:T(8,128)S(1)}, u32[]{:S(2)}, u32[]{:S(2)}) collective-permute-start(f32[40,640]{1,0:T(8,128)S(1)} %get-tuple-element.31.to_far), channel_id=1, source_target_pairs={{0,24},{8,16},{16,8},{24,0},{1,25},{9,17},{17,9},{25,1},{2,26},{10... | collective-permute-start | bytes 307208 | tf_op jit(solution)/shard_map/ppermute | solution.py:410
  12.5 1.7 %copy-start = (s32[4,32]{1,0:T(4,128)S(1)}, s32[4,32]{1,0:T(4,128)}, u32[]{:S(2)}) copy-start(s32[4,32]{1,0:T(4,128)} %slots.1) | copy-start | bytes 1540
  12.5 5.0 %collective-permute-start.6 = (f32[4,528]{1,0:T(4,128)S(1)}, f32[4,528]{1,0:T(4,128)S(1)}, u32[]{:S(2)}, u32[]{:S(2)}) collective-permute-start(f32[4,528]{1,0:T(4,128)S(1)} %get-tuple-element.32), channel_id=1, source_target_pairs={{0,16},{8,24},{16,0},{24,8},{1,17},{9,25},{17,1},{25,9},{2,18},{10... | collective-permute-start | bytes 25352 | tf_op jit(solution)/shard_map/ppermute | solution.py:410
where the time goes:
time: 19.2 us; the launch traced here: 19.1 us
  starting transfers between devices  10.1 us (53%)
  Pallas kernels  4.52 us (24%)
  waiting for transfers between devices  4.41 us (23%)
    ppermute x5, starting transfers between devices, swapped(): lax.ppermute(value, axis, [(i, partner(i)) for i in range(lax.axis_size(a...  5.33 us
    ppermute x2, starting transfers between devices, shifted(): lax.ppermute(value, axis, [(i, (i + step) % size) for i in range(size)])  4.72 us
    pallas_call x4, Pallas kernels, call(): pl.pallas_call(kernel, out_shape=outs, in_specs=[spec] * len(operands), o...  4.52 us
    ppermute x5, waiting for transfers between devices, swapped(): lax.ppermute(value, axis, [(i, partner(i)) for i in range(lax.axis_size(a...  2.43 us
    ppermute x2, waiting for transfers between devices, shifted(): lax.ppermute(value, axis, [(i, (i + step) % size) for i in range(size)])  1.98 us
  transfers between devices with their start and end apart: 7, of which 2 were waited for; matrix products, arithmetic and copies ran while one was open for 0% of the time, Pallas kernels for 5%

commit v1 on v0

--- a/solution.py
+++ b/solution.py
@@ -9,6 +9,7 @@
 from jax.sharding import PartitionSpec as P
 
 VMEM = pl.BlockSpec(memory_space=pltpu.VMEM)
+LONG = pl.CostEstimate(flops=100_000_000_000, bytes_accessed=30_000_000, transcendentals=0)
 PARAMS = pltpu.CompilerParams(vmem_limit_bytes=16 * 1024 * 1024)
 
 
@@ -91,6 +92,12 @@
         count = min(COEF_ROWS, rows - first)
         parts.append(message[start : start + count, i * lanes : (i + 1) * lanes])
     return jnp.concatenate(parts, axis=0)
+
+
+def edge_rows(ref, y, size_x, size_y):
+    return jnp.concatenate(
+        [ref[x * size_y + y : x * size_y + y + 1, :] for x in range(size_x)], axis=0
+    )
 
 
 def start_kernel(
@@ -135,28 +142,21 @@
     columns[...] = jnp.where(lane == 0, own, jnp.where(lane == 1, inverses, partner))
     matrix = own * tables_here[0] + partner * tables_here[1]
     operator[...] = matrix
+    matrix = split(matrix)
     copies[3].wait()
-    total[...] = product(split(matrix), split(here[...].reshape(size_x * size_y, width)))
+    total[...] = product(matrix, split(here[...].reshape(size_x * size_y, width)))
+    near, far = x_rows(size_x * size_y, size_y)
+    x_near[:size_y, :width] = total[near]
+    x_far[:, :width] = total[far]
     for first, message in ((0, low), (size_y - 4, high)):
-        for x in range(size_x):
-            for i in range(4):
-                row = x * size_y + first + i
-                place = i * size_x + x
-                message[place : place + 1, :width] = total[row : row + 1, :]
-                message[place : place + 1, width : width + 2] = columns[row : row + 1, :2]
-    near, far = x_rows(size_x * size_y, size_y)
-    x_near[...] = total[near]
-    x_far[:size_y, :width] = total[far]
+        for i in range(4):
+            rows = slice(i * size_x, (i + 1) * size_x)
+            message[rows, :width] = edge_rows(total, first + i, size_x, size_y)
+            message[rows, width : width + 2] = edge_rows(columns, first + i, size_x, size_y)[:, :2]
     for copy in copies[4:]:
         copy.wait()
-    if x_far.shape[0] > size_y:
-        write_coefs(x_far, size_y, coefs)
-
-
-def edge_rows(ref, y, size_x, size_y):
-    return jnp.concatenate(
-        [ref[x * size_y + y : x * size_y + y + 1, :] for x in range(size_x)], axis=0
-    )
+    if x_near.shape[0] > size_y:
+        write_coefs(x_near, size_y, coefs)
 
 
 def node_column(values, start, count):
@@ -200,15 +200,44 @@
     return tile + jnp.where((place == y - first) & (lane == 4), value, 0.0)
 
 
+def side_weights(columns, message, size_x, size_y, width, line):
+    second = second_table()
+    first, last = 0, size_x - 1
+    tiles = [
+        edge_weights(columns, message, size_x, size_y, width, edge, line) for edge in (first, last)
+    ]
+    mass = message[line * size_x : (line + 1) * size_x, width : width + 1]
+    own = edge_rows(columns, 0 if line == 3 else size_y - 1, size_x, size_y)
+    inner = []
+    for edge in (first, last):
+        inverse = message[line * size_x + edge : line * size_x + edge + 1, width + 1 : width + 2]
+        across = mass * inverse + own[:, 0:1] * own[edge : edge + 1, 1:2]
+        inner.append(node_column(second[:, edge], 0, size_x) * across)
+    lane = lax.broadcasted_iota(jnp.int32, (size_x, 128), 1)
+    from_last = jnp.where(even("gx"), 0, 1)
+    return (
+        jnp.where(even("gx"), tiles[1], tiles[0]),
+        jnp.where(even("gx"), tiles[0], tiles[1]),
+        jnp.where(lane == from_last, inner[1], inner[0]),
+    )
+
+
+def weights_kernel(size_x, size_y, width, columns, message, out):
+    near, far, inner = side_weights(columns, message, size_x, size_y, width, 3)
+    out[0:8, :] = near
+    out[8:16, :] = far
+    out[16 : 16 + size_x, :] = inner
+
+
 def second_kernel(
     size_x,
     total,
     columns,
     operator,
-    coefs,
+    low_weights,
+    low,
     from_far,
     from_near,
-    low,
     high,
     out,
     x_near,
@@ -217,12 +246,12 @@
     inner,
     work,
 ):
-    size_y, width = from_near.shape
+    size_y, width = from_far.shape[0], total.shape[1]
     second = second_table()
     near, far = x_rows(size_x * size_y, size_y)
     work[...] = total[...]
-    work[near] += from_near[...]
-    work[far] += from_far[:size_y, :width]
+    work[near] += from_near[:size_y, :width]
+    work[far] += from_far[:, :width]
     sides = ((low, 0, 3, 0), (high, size_y - 1, 0, size_y - 8))
     beyond = []
     for message, y, line, _ in sides:
@@ -243,20 +272,19 @@
         for x in range(size_x):
             out[x * size_y + y : x * size_y + y + 1, :] += rows[x : x + 1]
 
-    first, last = 0, size_x - 1
     x_near[:size_y, :width] = out[near]
     x_far[:size_y, :width] = out[far]
+    high_weights = side_weights(columns, high, size_x, size_y, width, 0)
     for side, (message, y, line, start) in enumerate(sides):
-        tiles = {
-            edge: edge_weights(columns, message, size_x, size_y, width, edge, line)
-            for edge in (first, last)
-        }
+        weights = high_weights if side else [low_weights[i : i + 8] for i in (0, 8, 16)]
         behind = slice(width % 128, 128)
-        rows = slice(start, start + 8)
-        x_near[rows, width:] = jnp.where(even("gx"), tiles[last], tiles[first])[:, behind]
-        x_far[rows, width:] = jnp.where(even("gx"), tiles[first], tiles[last])[:, behind]
+        x_near[start : start + 8, width:] = weights[0][:, behind]
+        x_far[start : start + 8, width:] = weights[1][:, behind]
+        inner[side * size_x : (side + 1) * size_x, :] = weights[2][:size_x]
         for i in range(4):
-            rows = [message[i * size_x + x : i * size_x + x + 1, :width] for x in (first, last)]
+            rows = [
+                message[i * size_x + x : i * size_x + x + 1, :width] for x in (0, size_x - 1)
+            ]
             at_near = jnp.where(even("gx"), rows[1], rows[0])
             at_far = jnp.where(even("gx"), rows[0], rows[1])
             place = size_y + 4 * side + i
@@ -265,21 +293,6 @@
             if i == line:
                 line_ends[2 * side : 2 * side + 1, :] = at_far
                 line_ends[2 * side + 1 : 2 * side + 2, :] = at_near
-        mass = message[line * size_x : (line + 1) * size_x, width : width + 1]
-        own = edge_rows(columns, y, size_x, size_y)
-        weights = []
-        for edge in (first, last):
-            inverse = message[line * size_x + edge : line * size_x + edge + 1, width + 1 : width + 2]
-            across = mass * inverse + own[:, 0:1] * own[edge : edge + 1, 1:2]
-            weights.append(node_column(second[:, edge], 0, size_x) * across)
-        lane = lax.broadcasted_iota(jnp.int32, (size_x, 128), 1)
-        from_last = jnp.where(even("gx"), 0, 1)
-        inner[side * size_x : (side + 1) * size_x, :] = jnp.where(
-            lane == from_last, weights[1], weights[0]
-        )
-    if x_near.shape[0] > size_y + 8:
-        write_coefs(x_near, size_y + 8, coefs)
-        x_near[size_y + 8 + COEF_ROWS :, :] = from_far[size_y:, :]
 
 
 def third_kernel(
@@ -360,31 +373,39 @@
     out[...] = turned[...].T.reshape(out.shape)
 
 
-def factor_kernel(levels, span, slots, *refs):
-    rows = 3 * levels
+def pick(slots, pieces):
     size_x, size_y = slots.shape
     columns = size_x * size_y
-    factors = refs[-1]
-    if len(refs) == 4:
-        own, from_far, from_near = refs[:3]
-        here = lax.axis_index("gx")
-        pieces = [
-            (here, own[...]),
-            (here ^ 3, read_coefs(from_far, size_y, rows, span)),
-            (here ^ 1, read_coefs(from_near, size_y + 8, rows, span)),
-            (here ^ 2, read_coefs(from_near, size_y + 8 + COEF_ROWS, rows, span)),
-        ]
-    else:
-        pieces = [(peer, refs[0][peer]) for peer in range(refs[0].shape[0])]
-    picked = jnp.zeros((rows, columns), jnp.float32)
     wanted = jnp.concatenate([slots[x : x + 1, :] for x in range(size_x)], axis=1)
+    picked = 0.0
     for owner, rest in pieces:
+        span = rest.shape[1]
         entry = lax.broadcasted_iota(jnp.int32, (span, columns), 0) + owner * span
         choice = (entry == wanted).astype(jnp.float32).astype(jnp.bfloat16)
         for _ in range(3):
             part = rest.astype(jnp.bfloat16)
             rest = rest - part.astype(jnp.float32)
             picked = picked + jnp.dot(part, choice, preferred_element_type=jnp.float32)
+    return picked
+
+
+def pick_kernel(slots, own, from_near, from_far, picked, passed):
+    here = lax.axis_index("gx")
+    size_y = slots.shape[1]
+    near = read_coefs(from_near, size_y, *own.shape)
+    pieces = [(here, own[...]), (here ^ 1, near), (here ^ 3, from_far[...])]
+    passed[...] = from_far[...]
+    picked[...] = pick(slots, pieces)
+
+
+def factor_kernel(levels, slots, *refs):
+    factors = refs[-1]
+    columns = factors.shape[1]
+    if len(refs) == 3:
+        here = lax.axis_index("gx")
+        picked = refs[0][...] + pick(slots, [(here ^ 2, refs[1][...])])
+    else:
+        picked = pick(slots, [(peer, refs[0][peer]) for peer in range(refs[0].shape[0])])
     mixing, falling, covered = (picked[i * levels : (i + 1) * levels] for i in range(3))
     scale, down, up, keep, flow, cover = (
         factors.at[i * levels : (i + 1) * levels] for i in range(6)
@@ -438,7 +459,7 @@
     def scratch(*shape):
         return pltpu.VMEM(shape, jnp.float32)
 
-    def call(kernel, name, outs, scratches, *operands, spec=VMEM):
+    def call(kernel, name, outs, scratches, *operands, spec=VMEM, cost=None):
         return pl.pallas_call(
             kernel,
             out_shape=outs,
@@ -446,21 +467,21 @@
             out_specs=[VMEM] * len(outs),
             scratch_shapes=scratches,
             compiler_params=PARAMS,
+            cost_estimate=cost,
             name=name,
         )(*operands)
 
     riding = lax.axis_size("gx") == 4
-    extra = COEF_ROWS if riding else 0
-    whole, line = array(columns, width), array(size_y, width)
-    edge = array(4 * size_x, padded)
+    whole = array(columns, width)
+    edge, message = array(4 * size_x, padded), array(size_y + 8, padded)
     here, total, x_near, x_far, y_low, y_high, operator, masses, coefs = call(
         start_kernel,
         "start",
         [
             array(size_x, size_y, width),
             whole,
-            line,
-            array(size_y + extra, padded),
+            array(size_y + (COEF_ROWS if riding else 0), padded),
+            array(size_y, padded),
             edge,
             edge,
             array(columns, columns),
@@ -487,25 +508,33 @@
         ),
         spec=pl.BlockSpec(memory_space=pltpu.HBM),
     )
-    from_x = exchanged(x_near, x_far, "gx")
+    low = shifted(y_high, "gy", 1)
+    from_far, from_near = exchanged(x_near, x_far, "gx")
+    sent, y_low, _ = lax.optimization_barrier((coefs, y_low, from_near))
+    coefs_far = swapped(sent, "gx", lambda i: i ^ 3) if riding else None
+    high = shifted(y_low, "gy", -1)
+    (low_weights,) = call(
+        functools.partial(weights_kernel, size_x, size_y, width),
+        "weights",
+        [array(24, 128)],
+        [],
+        masses,
+        low,
+        cost=LONG,
+    )
     total, x_near, x_far, line_ends, inner = call(
         functools.partial(second_kernel, size_x),
         "second",
-        [
-            whole,
-            array(size_y + 8 + 2 * extra, padded),
-            array(size_y + 8, padded),
-            array(4, width),
-            array(2 * size_x, 128),
-        ],
+        [whole, message, message, array(4, width), array(2 * size_x, 128)],
         [scratch(columns, width)],
         total,
         masses,
         operator,
-        coefs,
-        *from_x,
-        shifted(y_high, "gy", 1),
-        shifted(y_low, "gy", -1),
+        low_weights,
+        low,
+        from_far,
+        from_near,
+        high,
     )
     last_x = exchanged(x_near, x_far, "gx")
     peers = lax.axis_size("gx")
@@ -514,11 +543,21 @@
     if peers != 4:
         ends_far = swapped(line_ends, "gx", lambda i: (i - (2 if i % 2 else -2)) % peers)
     if riding:
-        pieces = [coefs, from_x[0], last_x[1]]
+        picked, passed = call(
+            pick_kernel,
+            "pick",
+            [array(3 * levels, columns), array(3 * levels, span)],
+            [],
+            span_slot,
+            coefs,
+            from_near,
+            coefs_far,
+        )
+        pieces = [picked, swapped(passed, "gx", lambda i: i ^ 1)]
     else:
         pieces = [lax.all_gather(coefs, "gx")]
     (factors,) = call(
-        functools.partial(factor_kernel, levels, span),
+        functools.partial(factor_kernel, levels),
         "factors",
         [array(6 * levels, columns)],
         [],

time: 19.2 us -> 19.8 us (1.031)
  starting transfers between devices: 10.1 us -> 11.4 us
  waiting for transfers between devices: 4.41 us -> 3.13 us
  Pallas kernels: 4.52 us -> 5 us
    ppermute x2, waiting for transfers between devices: 1.98 us -> 0.64 us  [shifted(): lax.ppermute(value, axis, [(i, (i + step) % size) for i in range(size)])]
    ppermute x2, starting transfers between devices: 4.72 us -> 5.9 us  [shifted(): lax.ppermute(value, axis, [(i, (i + step) % size) for i in range(size)])]
    pallas_call x4 -> x6, Pallas kernels: 4.52 us -> 5 us  [call(): pl.pallas_call(kernel, out_shape=outs, in_specs=[spec] * len(operands), o...]
    ppermute x5 -> x7, starting transfers between devices: 5.33 us -> 5.53 us  [swapped(): lax.ppermute(value, axis, [(i, partner(i)) for i in range(lax.axis_size(a...]
    ppermute x5 -> x7, waiting for transfers between devices: 2.43 us -> 2.49 us  [swapped(): lax.ppermute(value, axis, [(i, partner(i)) for i in range(lax.axis_size(a...]
  transfers between devices with their start and end apart: 7 -> 9, of which waited for: 2 -> 3; matrix products, arithmetic and copies ran while one was open for 0% -> 0% of each run, Pallas kernels for 5% -> 9%
where the time goes in v1:
time: 19.8 us; the launch traced here: 19.6 us
  starting transfers between devices  11.4 us (58%)
  Pallas kernels  5 us (25%)
  waiting for transfers between devices  3.13 us (16%)
    ppermute x2, starting transfers between devices, shifted(): lax.ppermute(value, axis, [(i, (i + step) % size) for i in range(size)])  5.9 us
    ppermute x7, starting transfers between devices, swapped(): lax.ppermute(value, axis, [(i, partner(i)) for i in range(lax.axis_size(a...  5.53 us
    pallas_call x6, Pallas kernels, call(): pl.pallas_call(kernel, out_shape=outs, in_specs=[spec] * len(operands), o...  5 us
    ppermute x7, waiting for transfers between devices, swapped(): lax.ppermute(value, axis, [(i, partner(i)) for i in range(lax.axis_size(a...  2.49 us
    ppermute x2, waiting for transfers between devices, shifted(): lax.ppermute(value, axis, [(i, (i + step) % size) for i in range(size)])  0.64 us
  transfers between devices with their start and end apart: 9, of which 3 were waited for; matrix products, arithmetic and copies ran while one was open for 0% of the time, Pallas kernels for 9%

profile of v1, /device:TPU:0, one launch (start us, length us, event | category | flops | bytes accessed | tf_op | source)
XLA Modules:
  0.0 19.6 jit_solution(7940767860407200925)
XLA Ops:
  0.0 1.6 %start.1 = (f32[4,32,528]{2,1,0:T(8,128)S(1)}, f32[128,528]{1,0:T(8,128)S(1)}, f32[64,640]{1,0:T(8,128)S(1)}, f32[32,640]{1,0:T(8,128)S(1)}, f32[16,640]{1,0:T(8...) custom-call(f32[4,32,528]{2,1,0:T(8,128)} %state.1, ...), custom_call_target="tpu_custom_call" | custom-call | tf_op jit(solution)/shard_map/start/pallas_call | solution.py:463
  1.6 0.5 %collective-permute-start.2 = (f32[64,640]{1,0:T(8,128)S(1)}, f32[64,640]{1,0:T(8,128)S(1)}, u32[]{:S(2)}, u32[]{:S(2)}) collective-permute-start(f32[64,640]{1,0:T(8,128)S(1)} %get-tuple-element.29), channel_id=1, source_target_pairs={{0,8},{8,0},{16,24},{24,16},{1,9},{9,1},{17,25},{25,17},{2,10},{10... | collective-permute-start | bytes 491528 | tf_op jit(solution)/shard_map/ppermute | solution.py:431
  2.2 2.6 %collective-permute-start = (f32[16,640]{1,0:T(8,128)S(1)}, f32[16,640]{1,0:T(8,128)S(1)}, u32[]{:S(2)}, u32[]{:S(2)}) collective-permute-start(f32[16,640]{1,0:T(8,128)S(1)} %get-tuple-element.27), channel_id=1, source_target_pairs={{0,1},{1,2},{2,3},{3,4},{4,5},{5,6},{6,7},{7,0},{8,9},{9,10},{10,1... | collective-permute-start | bytes 122888 | tf_op jit(solution)/shard_map/ppermute | solution.py:443
  4.7 1.3 %collective-permute-start.1 = (f32[32,640]{1,0:T(8,128)S(1)}, f32[32,640]{1,0:T(8,128)S(1)}, u32[]{:S(2)}, u32[]{:S(2)}) collective-permute-start(f32[32,640]{1,0:T(8,128)S(1)} %get-tuple-element.28), channel_id=1, source_target_pairs={{0,24},{8,16},{16,8},{24,0},{1,25},{9,17},{17,9},{25,1},{2,26},{10... | collective-permute-start | bytes 245768 | tf_op jit(solution)/shard_map/ppermute | solution.py:431
  6.0 0.0 collective-permute-done.2.from_near
  6.0 3.3 %collective-permute-start.3 = (f32[16,640]{1,0:T(8,128)S(1)}, f32[16,640]{1,0:T(8,128)S(1)}, u32[]{:S(2)}, u32[]{:S(2)}) collective-permute-start(f32[16,640]{1,0:T(8,128)S(1)} %get-tuple-element.32), channel_id=1, source_target_pairs={{0,7},{1,0},{2,1},{3,2},{4,3},{5,4},{6,5},{7,6},{8,15},{9,8},{10,9... | collective-permute-start | bytes 122888 | tf_op jit(solution)/shard_map/ppermute | solution.py:443
  9.3 0.7 %collective-permute-start.4 = (f32[144,128]{1,0:T(8,128)S(1)}, f32[144,128]{1,0:T(8,128)S(1)}, u32[]{:S(2)}, u32[]{:S(2)}) collective-permute-start(f32[144,128]{1,0:T(8,128)S(1)} %get-tuple-element.35.own), channel_id=1, source_target_pairs={{0,24},{8,16},{16,8},{24,0},{1,25},{9,17},{17,9},{25,1},{2,26},{10... | collective-permute-start | bytes 221192 | tf_op jit(solution)/shard_map/ppermute | solution.py:431
  10.1 0.0 collective-permute-done.message.low
  10.1 0.3 %weights.1.low_weights = f32[24,128]{1,0:T(8,128)S(1)} custom-call(f32[128,128]{1,0:T(8,128)S(1)} %get-tuple-element.25.columns.masses, f32[16,640]{1,0:T(8,128)S(1)} %collective-permute-done.message.low), custom_call_target="tpu_custom_call" | custom-call | flops 99999997952 | bytes 30000000 | tf_op jit(solution)/shard_map/weights/pallas_call | solution.py:463
  10.4 0.0 collective-permute-done.1.from_far
  10.4 0.6 %collective-permute-done.3.high = f32[16,640]{1,0:T(8,128)S(1)} collective-permute-done((f32[16,640]{1,0:T(8,128)S(1)}, f32[16,640]{1,0:T(8,128)S(1)}, u32[]{:S(2)}, u32[]{:S(2)}) %collective-permute-start.3) | collective-permute-done | bytes 40992 | tf_op jit(solution)/shard_map/ppermute | solution.py:443
  11.0 0.4 %second.1 = (f32[128,528]{1,0:T(8,128)S(1)}, f32[40,640]{1,0:T(8,128)S(1)}, f32[40,640]{1,0:T(8,128)S(1)}, f32[4,528]{1,0:T(4,128)S(1)}, f32[8,128]{1,0:T(8,128)S(1)}) custom-call(f32[128,528]{1,0:T(8,128)S(1)} %get-tuple-element.24.total, f32[128,128]{1,0:T(8,128)S(1)} %get-tuple-element.25.columns.masses, f32[128,128]{1,0:T(8,128)S(1)} %get-tuple-element.26.operator, ...), custom_call_target="tpu_custom_call" | custom-call | tf_op jit(solution)/shard_map/second/pallas_call | solution.py:463
  11.4 0.0 copy-start
  11.5 0.1 collective-permute-start.7
  11.5 1.4 %collective-permute-start.6 = (f32[40,640]{1,0:T(8,128)S(1)}, f32[40,640]{1,0:T(8,128)S(1)}, u32[]{:S(2)}, u32[]{:S(2)}) collective-permute-start(f32[40,640]{1,0:T(8,128)S(1)} %get-tuple-element.39.to_far), channel_id=1, source_target_pairs={{0,24},{8,16},{16,8},{24,0},{1,25},{9,17},{17,9},{25,1},{2,26},{10... | collective-permute-start | bytes 307208 | tf_op jit(solution)/shard_map/ppermute | solution.py:431
  12.9 0.8 %collective-permute-done.4.from_far = f32[144,128]{1,0:T(8,128)S(1)} collective-permute-done((f32[144,128]{1,0:T(8,128)S(1)}, f32[144,128]{1,0:T(8,128)S(1)}, u32[]{:S(2)}, u32[]{:S(2)}) %collective-permute-start.4) | collective-permute-done | bytes 73760 | tf_op jit(solution)/shard_map/ppermute | solution.py:431
  13.8 0.0 copy-done
  13.8 0.0 copy-start.1
  13.8 0.4 %pick.1 = (f32[144,128]{1,0:T(8,128)S(1)}, f32[144,128]{1,0:T(8,128)S(1)}) custom-call(s32[4,32]{1,0:T(4,128)S(1)} %copy-done, f32[144,128]{1,0:T(8,128)S(1)} %get-tuple-element.35.own, f32[64,640]{1,0:T(8,128)S(1)} %collective-permute-done.2.from_near, f32[144,128]{1,0:T(8,128)S(1)} %collective-permute-done.4.from_far), custom_call_target="tpu_custom_call" | custom-call | tf_op jit(solution)/shard_map/pick/pallas_call | solution.py:463
  14.2 0.2 collective-permute-start.5
  14.4 1.4 %collective-permute-start.8 = (f32[4,528]{1,0:T(4,128)S(1)}, f32[4,528]{1,0:T(4,128)S(1)}, u32[]{:S(2)}, u32[]{:S(2)}) collective-permute-start(f32[4,528]{1,0:T(4,128)S(1)} %get-tuple-element.40), channel_id=1, source_target_pairs={{0,16},{8,24},{16,0},{24,8},{1,17},{9,25},{17,1},{25,9},{2,18},{10... | collective-permute-start | bytes 25352 | tf_op jit(solution)/shard_map/ppermute | solution.py:431
  15.7 0.0 copy-done.1
  15.7 0.0 collective-permute-done.5.refs_1_
  15.7 0.7 %factors.1 = f32[288,128]{1,0:T(8,128)S(1)} custom-call(s32[4,32]{1,0:T(4,128)S(1)} %copy-done, f32[144,128]{1,0:T(8,128)S(1)} %get-tuple-element.36.refs_0_, f32[144,128]{1,0:T(8,128)S(1)} %collective-permute-done.5.refs_1_), custom_call_target="tpu_custom_call" | custom-call | tf_op jit(solution)/shard_map/factors/pallas_call | solution.py:463
  16.4 1.6 %collective-permute-done.8.ends_near.ends_far = f32[4,528]{1,0:T(4,128)S(1)} collective-permute-done((f32[4,528]{1,0:T(4,128)S(1)}, f32[4,528]{1,0:T(4,128)S(1)}, u32[]{:S(2)}, u32[]{:S(2)}) %collective-permute-start.8) | collective-permute-done | bytes 8480 | tf_op jit(solution)/shard_map/ppermute | solution.py:431
  18.1 0.0 collective-permute-done.7.from_near
  18.1 0.0 collective-permute-done.6.from_far
  18.1 1.6 %third.1 = f32[4,32,528]{2,1,0:T(8,128)} custom-call(f32[4,32,528]{2,1,0:T(8,128)S(1)} %get-tuple-element.23.state, f32[1,528]{1,0:T(1,128)S(1)} %reshape.3.hyper, f32[128,528]{1,0:T(8,128)S(1)} %get-tuple-element.33.total, f32[128,128]{1,0:T(8,128)S(1)} %get-tuple-element.25.columns.masses, f32[8,128]{1,0:T(8,128)S(1)} %get-tuple-element.34.inner, ...), custom_call_target="tpu_custom_call" | custom-call | tf_op jit(solution)/shard_map/third/pallas_call | solution.py:463
  (1 shorter events, 0.0 us)
Async XLA Ops:
  1.6 4.4 %collective-permute-start.2 = (f32[64,640]{1,0:T(8,128)S(1)}, f32[64,640]{1,0:T(8,128)S(1)}, u32[]{:S(2)}, u32[]{:S(2)}) collective-permute-start(f32[64,640]{1,0:T(8,128)S(1)} %get-tuple-element.29), channel_id=1, source_target_pairs={{0,8},{8,0},{16,24},{24,16},{1,9},{9,1},{17,25},{25,17},{2,10},{10... | collective-permute-start | bytes 491528 | tf_op jit(solution)/shard_map/ppermute | solution.py:431
  2.2 7.9 %collective-permute-start = (f32[16,640]{1,0:T(8,128)S(1)}, f32[16,640]{1,0:T(8,128)S(1)}, u32[]{:S(2)}, u32[]{:S(2)}) collective-permute-start(f32[16,640]{1,0:T(8,128)S(1)} %get-tuple-element.27), channel_id=1, source_target_pairs={{0,1},{1,2},{2,3},{3,4},{4,5},{5,6},{6,7},{7,0},{8,9},{9,10},{10,1... | collective-permute-start | bytes 122888 | tf_op jit(solution)/shard_map/ppermute | solution.py:443
  4.7 5.6 %collective-permute-start.1 = (f32[32,640]{1,0:T(8,128)S(1)}, f32[32,640]{1,0:T(8,128)S(1)}, u32[]{:S(2)}, u32[]{:S(2)}) collective-permute-start(f32[32,640]{1,0:T(8,128)S(1)} %get-tuple-element.28), channel_id=1, source_target_pairs={{0,24},{8,16},{16,8},{24,0},{1,25},{9,17},{17,9},{25,1},{2,26},{10... | collective-permute-start | bytes 245768 | tf_op jit(solution)/shard_map/ppermute | solution.py:431
  6.0 5.0 %collective-permute-start.3 = (f32[16,640]{1,0:T(8,128)S(1)}, f32[16,640]{1,0:T(8,128)S(1)}, u32[]{:S(2)}, u32[]{:S(2)}) collective-permute-start(f32[16,640]{1,0:T(8,128)S(1)} %get-tuple-element.32), channel_id=1, source_target_pairs={{0,7},{1,0},{2,1},{3,2},{4,3},{5,4},{6,5},{7,6},{8,15},{9,8},{10,9... | collective-permute-start | bytes 122888 | tf_op jit(solution)/shard_map/ppermute | solution.py:443
  9.3 4.4 %collective-permute-start.4 = (f32[144,128]{1,0:T(8,128)S(1)}, f32[144,128]{1,0:T(8,128)S(1)}, u32[]{:S(2)}, u32[]{:S(2)}) collective-permute-start(f32[144,128]{1,0:T(8,128)S(1)} %get-tuple-element.35.own), channel_id=1, source_target_pairs={{0,24},{8,16},{16,8},{24,0},{1,25},{9,17},{17,9},{25,1},{2,26},{10... | collective-permute-start | bytes 221192 | tf_op jit(solution)/shard_map/ppermute | solution.py:431
  11.4 2.3 %copy-start = (s32[4,32]{1,0:T(4,128)S(1)}, s32[4,32]{1,0:T(4,128)}, u32[]{:S(2)}) copy-start(s32[4,32]{1,0:T(4,128)} %slots.3) | copy-start | bytes 1540
  11.5 6.6 %collective-permute-start.7 = (f32[40,640]{1,0:T(8,128)S(1)}, f32[40,640]{1,0:T(8,128)S(1)}, u32[]{:S(2)}, u32[]{:S(2)}) collective-permute-start(f32[40,640]{1,0:T(8,128)S(1)} %get-tuple-element.38.to_near), channel_id=1, source_target_pairs={{0,8},{8,0},{16,24},{24,16},{1,9},{9,1},{17,25},{25,17},{2,10},{10... | collective-permute-start | bytes 307208 | tf_op jit(solution)/shard_map/ppermute | solution.py:431
  11.5 6.5 %collective-permute-start.6 = (f32[40,640]{1,0:T(8,128)S(1)}, f32[40,640]{1,0:T(8,128)S(1)}, u32[]{:S(2)}, u32[]{:S(2)}) collective-permute-start(f32[40,640]{1,0:T(8,128)S(1)} %get-tuple-element.39.to_far), channel_id=1, source_target_pairs={{0,24},{8,16},{16,8},{24,0},{1,25},{9,17},{17,9},{25,1},{2,26},{10... | collective-permute-start | bytes 307208 | tf_op jit(solution)/shard_map/ppermute | solution.py:431
  13.8 1.9 %copy-start.1 = (f32[528]{0:T(1024)S(1)}, f32[528]{0:T(1024)}, u32[]{:S(2)}) copy-start(f32[528]{0:T(1024)} %param.10) | copy-start | bytes 6340
  14.2 1.6 %collective-permute-start.5 = (f32[144,128]{1,0:T(8,128)S(1)}, f32[144,128]{1,0:T(8,128)S(1)}, u32[]{:S(2)}, u32[]{:S(2)}) collective-permute-start(f32[144,128]{1,0:T(8,128)S(1)} %get-tuple-element.37), channel_id=1, source_target_pairs={{0,8},{8,0},{16,24},{24,16},{1,9},{9,1},{17,25},{25,17},{2,10},{10... | collective-permute-start | bytes 221192 | tf_op jit(solution)/shard_map/ppermute | solution.py:431
  14.4 3.7 %collective-permute-start.8 = (f32[4,528]{1,0:T(4,128)S(1)}, f32[4,528]{1,0:T(4,128)S(1)}, u32[]{:S(2)}, u32[]{:S(2)}) collective-permute-start(f32[4,528]{1,0:T(4,128)S(1)} %get-tuple-element.40), channel_id=1, source_target_pairs={{0,16},{8,24},{16,0},{24,8},{1,17},{9,25},{17,1},{25,9},{2,18},{10... | collective-permute-start | bytes 25352 | tf_op jit(solution)/shard_map/ppermute | solution.py:431

commit v2 on v1

--- a/solution.py
+++ b/solution.py
@@ -146,7 +146,7 @@
     copies[3].wait()
     total[...] = product(matrix, split(here[...].reshape(size_x * size_y, width)))
     near, far = x_rows(size_x * size_y, size_y)
-    x_near[:size_y, :width] = total[near]
+    x_near[:, :width] = total[near]
     x_far[:, :width] = total[far]
     for first, message in ((0, low), (size_y - 4, high)):
         for i in range(4):
@@ -155,8 +155,6 @@
             message[rows, width : width + 2] = edge_rows(columns, first + i, size_x, size_y)[:, :2]
     for copy in copies[4:]:
         copy.wait()
-    if x_near.shape[0] > size_y:
-        write_coefs(x_near, size_y, coefs)
 
 
 def node_column(values, start, count):
@@ -234,6 +232,7 @@
     total,
     columns,
     operator,
+    coefs,
     low_weights,
     low,
     from_far,
@@ -250,7 +249,7 @@
     second = second_table()
     near, far = x_rows(size_x * size_y, size_y)
     work[...] = total[...]
-    work[near] += from_near[:size_y, :width]
+    work[near] += from_near[:, :width]
     work[far] += from_far[:, :width]
     sides = ((low, 0, 3, 0), (high, size_y - 1, 0, size_y - 8))
     beyond = []
@@ -293,6 +292,8 @@
             if i == line:
                 line_ends[2 * side : 2 * side + 1, :] = at_far
                 line_ends[2 * side + 1 : 2 * side + 2, :] = at_near
+    if x_near.shape[0] > size_y + 8:
+        write_coefs(x_near, size_y + 8, coefs)
 
 
 def third_kernel(
@@ -389,23 +390,26 @@
     return picked
 
 
-def pick_kernel(slots, own, from_near, from_far, picked, passed):
-    here = lax.axis_index("gx")
-    size_y = slots.shape[1]
-    near = read_coefs(from_near, size_y, *own.shape)
-    pieces = [(here, own[...]), (here ^ 1, near), (here ^ 3, from_far[...])]
-    passed[...] = from_far[...]
-    picked[...] = pick(slots, pieces)
+def pass_kernel(arrived, passed):
+    passed[...] = arrived[...]
 
 
 def factor_kernel(levels, slots, *refs):
     factors = refs[-1]
+    if len(refs) == 5:
+        own, from_far, relayed, from_near = refs[:4]
+        here = lax.axis_index("gx")
+        near = read_coefs(from_near, slots.shape[1] + 8, *own.shape)
+        pieces = [
+            (here, own[...]),
+            (here ^ 3, from_far[...]),
+            (here ^ 2, relayed[...]),
+            (here ^ 1, near),
+        ]
+    else:
+        pieces = [(peer, refs[0][peer]) for peer in range(refs[0].shape[0])]
     columns = factors.shape[1]
-    if len(refs) == 3:
-        here = lax.axis_index("gx")
-        picked = refs[0][...] + pick(slots, [(here ^ 2, refs[1][...])])
-    else:
-        picked = pick(slots, [(peer, refs[0][peer]) for peer in range(refs[0].shape[0])])
+    picked = pick(slots, pieces)
     mixing, falling, covered = (picked[i * levels : (i + 1) * levels] for i in range(3))
     scale, down, up, keep, flow, cover = (
         factors.at[i * levels : (i + 1) * levels] for i in range(6)
@@ -473,14 +477,14 @@
 
     riding = lax.axis_size("gx") == 4
     whole = array(columns, width)
-    edge, message = array(4 * size_x, padded), array(size_y + 8, padded)
+    edge = array(4 * size_x, padded)
     here, total, x_near, x_far, y_low, y_high, operator, masses, coefs = call(
         start_kernel,
         "start",
         [
             array(size_x, size_y, width),
             whole,
-            array(size_y + (COEF_ROWS if riding else 0), padded),
+            array(size_y, padded),
             array(size_y, padded),
             edge,
             edge,
@@ -510,7 +514,8 @@
     )
     low = shifted(y_high, "gy", 1)
     from_far, from_near = exchanged(x_near, x_far, "gx")
-    sent, y_low, _ = lax.optimization_barrier((coefs, y_low, from_near))
+    y_low, _ = lax.optimization_barrier((y_low, from_near))
+    sent, _ = lax.optimization_barrier((coefs, from_near))
     coefs_far = swapped(sent, "gx", lambda i: i ^ 3) if riding else None
     high = shifted(y_low, "gy", -1)
     (low_weights,) = call(
@@ -525,11 +530,18 @@
     total, x_near, x_far, line_ends, inner = call(
         functools.partial(second_kernel, size_x),
         "second",
-        [whole, message, message, array(4, width), array(2 * size_x, 128)],
+        [
+            whole,
+            array(size_y + 8 + (COEF_ROWS if riding else 0), padded),
+            array(size_y + 8, padded),
+            array(4, width),
+            array(2 * size_x, 128),
+        ],
         [scratch(columns, width)],
         total,
         masses,
         operator,
+        coefs,
         low_weights,
         low,
         from_far,
@@ -543,17 +555,16 @@
     if peers != 4:
         ends_far = swapped(line_ends, "gx", lambda i: (i - (2 if i % 2 else -2)) % peers)
     if riding:
-        picked, passed = call(
-            pick_kernel,
-            "pick",
-            [array(3 * levels, columns), array(3 * levels, span)],
+        (passed,) = call(
+            pass_kernel,
+            "pass",
+            [array(3 * levels, span)],
             [],
-            span_slot,
-            coefs,
-            from_near,
             coefs_far,
+            cost=LONG,
         )
-        pieces = [picked, swapped(passed, "gx", lambda i: i ^ 1)]
+        relayed = swapped(passed, "gx", lambda i: i ^ 1)
+        pieces = [coefs, coefs_far, relayed, last_x[1]]
     else:
         pieces = [lax.all_gather(coefs, "gx")]
     (factors,) = call(

time: 19.8 us -> 19.4 us (0.980)
  starting transfers between devices: 11.4 us -> 11.1 us
  Pallas kernels: 5 us -> 4.79 us
    ppermute x7, starting transfers between devices: 5.53 us -> 5.19 us  [swapped(): lax.ppermute(value, axis, [(i, partner(i)) for i in range(lax.axis_size(a...]
    pallas_call x6, Pallas kernels: 5 us -> 4.79 us  [call(): pl.pallas_call(kernel, out_shape=outs, in_specs=[spec] * len(operands), o...]
  transfers between devices with their start and end apart: 9 -> 9, of which waited for: 3 -> 4; matrix products, arithmetic and copies ran while one was open for 0% -> 0% of each run, Pallas kernels for 9% -> 8%
where the time goes in v2:
time: 19.4 us; the launch traced here: 19.2 us
  starting transfers between devices  11.1 us (57%)
  Pallas kernels  4.79 us (25%)
  waiting for transfers between devices  3.28 us (17%)
    ppermute x2, starting transfers between devices, shifted(): lax.ppermute(value, axis, [(i, (i + step) % size) for i in range(size)])  5.9 us
    ppermute x7, starting transfers between devices, swapped(): lax.ppermute(value, axis, [(i, partner(i)) for i in range(lax.axis_size(a...  5.19 us
    pallas_call x6, Pallas kernels, call(): pl.pallas_call(kernel, out_shape=outs, in_specs=[spec] * len(operands), o...  4.79 us
    ppermute x7, waiting for transfers between devices, swapped(): lax.ppermute(value, axis, [(i, partner(i)) for i in range(lax.axis_size(a...  2.53 us
    ppermute x2, waiting for transfers between devices, shifted(): lax.ppermute(value, axis, [(i, (i + step) % size) for i in range(size)])  0.75 us
  transfers between devices with their start and end apart: 9, of which 4 were waited for; matrix products, arithmetic and copies ran while one was open for 0% of the time, Pallas kernels for 8%

profile of v2, /device:TPU:0, one launch (start us, length us, event | category | flops | bytes accessed | tf_op | source)
XLA Modules:
  0.0 19.2 jit_solution(2833342840657401311)
XLA Ops:
  0.0 1.6 %start.1 = (f32[4,32,528]{2,1,0:T(8,128)S(1)}, f32[128,528]{1,0:T(8,128)S(1)}, f32[32,640]{1,0:T(8,128)S(1)}, f32[32,640]{1,0:T(8,128)S(1)}, f32[16,640]{1,0:T(8...) custom-call(f32[4,32,528]{2,1,0:T(8,128)} %state.1, ...), custom_call_target="tpu_custom_call" | custom-call | tf_op jit(solution)/shard_map/start/pallas_call | solution.py:467
  1.6 0.5 %collective-permute-start.2 = (f32[32,640]{1,0:T(8,128)S(1)}, f32[32,640]{1,0:T(8,128)S(1)}, u32[]{:S(2)}, u32[]{:S(2)}) collective-permute-start(f32[32,640]{1,0:T(8,128)S(1)} %get-tuple-element.28), channel_id=1, source_target_pairs={{0,8},{8,0},{16,24},{24,16},{1,9},{9,1},{17,25},{25,17},{2,10},{10... | collective-permute-start | bytes 245768 | tf_op jit(solution)/shard_map/ppermute | solution.py:435
  2.2 2.6 %collective-permute-start = (f32[16,640]{1,0:T(8,128)S(1)}, f32[16,640]{1,0:T(8,128)S(1)}, u32[]{:S(2)}, u32[]{:S(2)}) collective-permute-start(f32[16,640]{1,0:T(8,128)S(1)} %get-tuple-element.26), channel_id=1, source_target_pairs={{0,1},{1,2},{2,3},{3,4},{4,5},{5,6},{6,7},{7,0},{8,9},{9,10},{10,1... | collective-permute-start | bytes 122888 | tf_op jit(solution)/shard_map/ppermute | solution.py:447
  4.7 1.3 %collective-permute-start.1 = (f32[32,640]{1,0:T(8,128)S(1)}, f32[32,640]{1,0:T(8,128)S(1)}, u32[]{:S(2)}, u32[]{:S(2)}) collective-permute-start(f32[32,640]{1,0:T(8,128)S(1)} %get-tuple-element.27), channel_id=1, source_target_pairs={{0,24},{8,16},{16,8},{24,0},{1,25},{9,17},{17,9},{25,1},{2,26},{10... | collective-permute-start | bytes 245768 | tf_op jit(solution)/shard_map/ppermute | solution.py:435
  6.0 0.0 collective-permute-done.2.from_near
  6.0 3.3 %collective-permute-start.3 = (f32[16,640]{1,0:T(8,128)S(1)}, f32[16,640]{1,0:T(8,128)S(1)}, u32[]{:S(2)}, u32[]{:S(2)}) collective-permute-start(f32[16,640]{1,0:T(8,128)S(1)} %get-tuple-element.30), channel_id=1, source_target_pairs={{0,7},{1,0},{2,1},{3,2},{4,3},{5,4},{6,5},{7,6},{8,15},{9,8},{10,9... | collective-permute-start | bytes 122888 | tf_op jit(solution)/shard_map/ppermute | solution.py:447
  9.3 0.6 %collective-permute-start.4 = (f32[144,128]{1,0:T(8,128)S(1)}, f32[144,128]{1,0:T(8,128)S(1)}, u32[]{:S(2)}, u32[]{:S(2)}) collective-permute-start(f32[144,128]{1,0:T(8,128)S(1)} %get-tuple-element.33.coefs.refs_0_), channel_id=1, source_target_pairs={{0,24},{8,16},{16,8},{24,0},{1,25},{9,17},{17,9},{25,1},{2,26},{10... | collective-permute-start | bytes 221192 | tf_op jit(solution)/shard_map/ppermute | solution.py:435
  10.0 0.1 collective-permute-done.message.low
  10.1 0.3 %weights.1.low_weights = f32[24,128]{1,0:T(8,128)S(1)} custom-call(f32[128,128]{1,0:T(8,128)S(1)} %get-tuple-element.23.columns.masses, f32[16,640]{1,0:T(8,128)S(1)} %collective-permute-done.message.low), custom_call_target="tpu_custom_call" | custom-call | flops 99999997952 | bytes 30000000 | tf_op jit(solution)/shard_map/weights/pallas_call | solution.py:467
  10.3 0.0 collective-permute-done.1.from_far
  10.3 0.7 %collective-permute-done.3.high = f32[16,640]{1,0:T(8,128)S(1)} collective-permute-done((f32[16,640]{1,0:T(8,128)S(1)}, f32[16,640]{1,0:T(8,128)S(1)}, u32[]{:S(2)}, u32[]{:S(2)}) %collective-permute-start.3) | collective-permute-done | bytes 40992 | tf_op jit(solution)/shard_map/ppermute | solution.py:447
  11.0 0.4 %second.1 = (f32[128,528]{1,0:T(8,128)S(1)}, f32[72,640]{1,0:T(8,128)S(1)}, f32[40,640]{1,0:T(8,128)S(1)}, f32[4,528]{1,0:T(4,128)S(1)}, f32[8,128]{1,0:T(8,128)S(1)}) custom-call(f32[128,528]{1,0:T(8,128)S(1)} %get-tuple-element.22.total, f32[128,128]{1,0:T(8,128)S(1)} %get-tuple-element.23.columns.masses, f32[128,128]{1,0:T(8,128)S(1)} %get-tuple-element.24.operator, ...), custom_call_target="tpu_custom_call" | custom-call | tf_op jit(solution)/shard_map/second/pallas_call | solution.py:467
  11.4 0.4 %collective-permute-start.7 = (f32[40,640]{1,0:T(8,128)S(1)}, f32[40,640]{1,0:T(8,128)S(1)}, u32[]{:S(2)}, u32[]{:S(2)}) collective-permute-start(f32[40,640]{1,0:T(8,128)S(1)} %get-tuple-element.35.to_far), channel_id=1, source_target_pairs={{0,24},{8,16},{16,8},{24,0},{1,25},{9,17},{17,9},{25,1},{2,26},{10... | collective-permute-start | bytes 307208 | tf_op jit(solution)/shard_map/ppermute | solution.py:435
  11.9 0.9 %collective-permute-start.6 = (f32[72,640]{1,0:T(8,128)S(1)}, f32[72,640]{1,0:T(8,128)S(1)}, u32[]{:S(2)}, u32[]{:S(2)}) collective-permute-start(f32[72,640]{1,0:T(8,128)S(1)} %get-tuple-element.34.to_near), channel_id=1, source_target_pairs={{0,8},{8,0},{16,24},{24,16},{1,9},{9,1},{17,25},{25,17},{2,10},{10... | collective-permute-start | bytes 552968 | tf_op jit(solution)/shard_map/ppermute | solution.py:435
  12.8 1.0 %collective-permute-done.4.arrived.refs_1_ = f32[144,128]{1,0:T(8,128)S(1)} collective-permute-done((f32[144,128]{1,0:T(8,128)S(1)}, f32[144,128]{1,0:T(8,128)S(1)}, u32[]{:S(2)}, u32[]{:S(2)}) %collective-permute-start.4) | collective-permute-done | bytes 73760 | tf_op jit(solution)/shard_map/ppermute | solution.py:435
  13.8 0.0 copy-start.1
  13.8 0.2 collective-permute-start.5
  14.0 0.0 copy-start
  14.0 1.3 %collective-permute-start.8 = (f32[4,528]{1,0:T(4,128)S(1)}, f32[4,528]{1,0:T(4,128)S(1)}, u32[]{:S(2)}, u32[]{:S(2)}) collective-permute-start(f32[4,528]{1,0:T(4,128)S(1)} %get-tuple-element.36), channel_id=1, source_target_pairs={{0,16},{8,24},{16,0},{24,8},{1,17},{9,25},{17,1},{25,9},{2,18},{10... | collective-permute-start | bytes 25352 | tf_op jit(solution)/shard_map/ppermute | solution.py:435
  15.2 0.0 copy-done.1
  15.2 0.0 collective-permute-done.5.refs_2_
  15.2 0.0 collective-permute-done.6.refs_3_.from_near
  15.2 0.0 copy-done
  15.3 0.9 %factors.1 = f32[288,128]{1,0:T(8,128)S(1)} custom-call(s32[4,32]{1,0:T(4,128)S(1)} %copy-done, f32[144,128]{1,0:T(8,128)S(1)} %get-tuple-element.33.coefs.refs_0_, f32[144,128]{1,0:T(8,128)S(1)} %collective-permute-done.4.arrived.refs_1_, f32[144,128]{1,0:T(8,128)S(1)} %collective-permute-done.5.refs_2_, f32[72,640]{1,0:T(8,128)S(1)} %collective-permute-done.6.refs_3_.from_near), custom_call_target="tpu_custom_call" | custom-call | tf_op jit(solution)/shard_map/factors/pallas_call | solution.py:467
  16.1 1.5 %collective-permute-done.8.ends_near.ends_far = f32[4,528]{1,0:T(4,128)S(1)} collective-permute-done((f32[4,528]{1,0:T(4,128)S(1)}, f32[4,528]{1,0:T(4,128)S(1)}, u32[]{:S(2)}, u32[]{:S(2)}) %collective-permute-start.8) | collective-permute-done | bytes 8480 | tf_op jit(solution)/shard_map/ppermute | solution.py:435
  17.7 0.0 collective-permute-done.7.from_far
  17.7 1.6 %third.1 = f32[4,32,528]{2,1,0:T(8,128)} custom-call(f32[4,32,528]{2,1,0:T(8,128)S(1)} %get-tuple-element.21.state, f32[1,528]{1,0:T(1,128)S(1)} %reshape.3.hyper, f32[128,528]{1,0:T(8,128)S(1)} %get-tuple-element.31.total, f32[128,128]{1,0:T(8,128)S(1)} %get-tuple-element.23.columns.masses, f32[8,128]{1,0:T(8,128)S(1)} %get-tuple-element.32.inner, ...), custom_call_target="tpu_custom_call" | custom-call | tf_op jit(solution)/shard_map/third/pallas_call | solution.py:467
  (2 shorter events, 0.0 us)
Async XLA Ops:
  1.6 4.4 %collective-permute-start.2 = (f32[32,640]{1,0:T(8,128)S(1)}, f32[32,640]{1,0:T(8,128)S(1)}, u32[]{:S(2)}, u32[]{:S(2)}) collective-permute-start(f32[32,640]{1,0:T(8,128)S(1)} %get-tuple-element.28), channel_id=1, source_target_pairs={{0,8},{8,0},{16,24},{24,16},{1,9},{9,1},{17,25},{25,17},{2,10},{10... | collective-permute-start | bytes 245768 | tf_op jit(solution)/shard_map/ppermute | solution.py:435
  2.2 7.9 %collective-permute-start = (f32[16,640]{1,0:T(8,128)S(1)}, f32[16,640]{1,0:T(8,128)S(1)}, u32[]{:S(2)}, u32[]{:S(2)}) collective-permute-start(f32[16,640]{1,0:T(8,128)S(1)} %get-tuple-element.26), channel_id=1, source_target_pairs={{0,1},{1,2},{2,3},{3,4},{4,5},{5,6},{6,7},{7,0},{8,9},{9,10},{10,1... | collective-permute-start | bytes 122888 | tf_op jit(solution)/shard_map/ppermute | solution.py:447
  4.7 5.6 %collective-permute-start.1 = (f32[32,640]{1,0:T(8,128)S(1)}, f32[32,640]{1,0:T(8,128)S(1)}, u32[]{:S(2)}, u32[]{:S(2)}) collective-permute-start(f32[32,640]{1,0:T(8,128)S(1)} %get-tuple-element.27), channel_id=1, source_target_pairs={{0,24},{8,16},{16,8},{24,0},{1,25},{9,17},{17,9},{25,1},{2,26},{10... | collective-permute-start | bytes 245768 | tf_op jit(solution)/shard_map/ppermute | solution.py:435
  6.0 5.0 %collective-permute-start.3 = (f32[16,640]{1,0:T(8,128)S(1)}, f32[16,640]{1,0:T(8,128)S(1)}, u32[]{:S(2)}, u32[]{:S(2)}) collective-permute-start(f32[16,640]{1,0:T(8,128)S(1)} %get-tuple-element.30), channel_id=1, source_target_pairs={{0,7},{1,0},{2,1},{3,2},{4,3},{5,4},{6,5},{7,6},{8,15},{9,8},{10,9... | collective-permute-start | bytes 122888 | tf_op jit(solution)/shard_map/ppermute | solution.py:447
  9.3 4.4 %collective-permute-start.4 = (f32[144,128]{1,0:T(8,128)S(1)}, f32[144,128]{1,0:T(8,128)S(1)}, u32[]{:S(2)}, u32[]{:S(2)}) collective-permute-start(f32[144,128]{1,0:T(8,128)S(1)} %get-tuple-element.33.coefs.refs_0_), channel_id=1, source_target_pairs={{0,24},{8,16},{16,8},{24,0},{1,25},{9,17},{17,9},{25,1},{2,26},{10... | collective-permute-start | bytes 221192 | tf_op jit(solution)/shard_map/ppermute | solution.py:435
  11.4 6.2 %collective-permute-start.7 = (f32[40,640]{1,0:T(8,128)S(1)}, f32[40,640]{1,0:T(8,128)S(1)}, u32[]{:S(2)}, u32[]{:S(2)}) collective-permute-start(f32[40,640]{1,0:T(8,128)S(1)} %get-tuple-element.35.to_far), channel_id=1, source_target_pairs={{0,24},{8,16},{16,8},{24,0},{1,25},{9,17},{17,9},{25,1},{2,26},{10... | collective-permute-start | bytes 307208 | tf_op jit(solution)/shard_map/ppermute | solution.py:435
  11.9 3.4 %collective-permute-start.6 = (f32[72,640]{1,0:T(8,128)S(1)}, f32[72,640]{1,0:T(8,128)S(1)}, u32[]{:S(2)}, u32[]{:S(2)}) collective-permute-start(f32[72,640]{1,0:T(8,128)S(1)} %get-tuple-element.34.to_near), channel_id=1, source_target_pairs={{0,8},{8,0},{16,24},{24,16},{1,9},{9,1},{17,25},{25,17},{2,10},{10... | collective-permute-start | bytes 552968 | tf_op jit(solution)/shard_map/ppermute | solution.py:435
  13.8 1.5 %copy-start.1 = (f32[528]{0:T(1024)S(1)}, f32[528]{0:T(1024)}, u32[]{:S(2)}) copy-start(f32[528]{0:T(1024)} %param.10) | copy-start | bytes 6340
  13.8 1.5 %collective-permute-start.5 = (f32[144,128]{1,0:T(8,128)S(1)}, f32[144,128]{1,0:T(8,128)S(1)}, u32[]{:S(2)}, u32[]{:S(2)}) collective-permute-start(f32[144,128]{1,0:T(8,128)S(1)} %pass.1), channel_id=1, source_target_pairs={{0,8},{8,0},{16,24},{24,16},{1,9},{9,1},{17,25},{25,17},{2,10},{10... | collective-permute-start | bytes 221192 | tf_op jit(solution)/shard_map/ppermute | solution.py:435
  14.0 1.3 %copy-start = (s32[4,32]{1,0:T(4,128)S(1)}, s32[4,32]{1,0:T(4,128)}, u32[]{:S(2)}) copy-start(s32[4,32]{1,0:T(4,128)} %slots.1) | copy-start | bytes 1540
  14.0 3.7 %collective-permute-start.8 = (f32[4,528]{1,0:T(4,128)S(1)}, f32[4,528]{1,0:T(4,128)S(1)}, u32[]{:S(2)}, u32[]{:S(2)}) collective-permute-start(f32[4,528]{1,0:T(4,128)S(1)} %get-tuple-element.36), channel_id=1, source_target_pairs={{0,16},{8,24},{16,0},{24,8},{1,17},{9,25},{17,1},{25,9},{2,18},{10... | collective-permute-start | bytes 25352 | tf_op jit(solution)/shard_map/ppermute | solution.py:435

commit v3 on v2

--- a/solution.py
+++ b/solution.py
@@ -70,28 +70,44 @@
     return lax.rem(lax.axis_index(axis), 2) == 0
 
 
+def x_starts(count, size_y):
+    near = jnp.where(even("gx"), count - size_y, 0)
+    return near, count - size_y - near
+
+
 def x_rows(count, size_y):
-    near = jnp.where(even("gx"), count - size_y, 0)
-    far = count - size_y - near
-    return tuple(pl.ds(pl.multiple_of(start, size_y), size_y) for start in (near, far))
-
-
-COEF_ROWS = 32
-
-
-def write_coefs(message, start, coefs):
-    rows, lanes = coefs.shape
-    for i, first in enumerate(range(0, rows, COEF_ROWS)):
-        part = coefs[first : min(first + COEF_ROWS, rows)]
-        message[start : start + part.shape[0], i * lanes : (i + 1) * lanes] = part
-
-
-def read_coefs(message, start, rows, lanes):
-    parts = []
-    for i, first in enumerate(range(0, rows, COEF_ROWS)):
-        count = min(COEF_ROWS, rows - first)
-        parts.append(message[start : start + count, i * lanes : (i + 1) * lanes])
-    return jnp.concatenate(parts, axis=0)
+    starts = x_starts(count, size_y)
+    return tuple(pl.ds(pl.multiple_of(start, size_y), size_y) for start in starts)
+
+
+def add_packed(work, start, message, rows):
+    def write(first, count, lanes, value):
+        work[pl.ds(pl.multiple_of(start + first, 8), count), lanes] += value
+
+    unpack(message, rows, work.shape[1], write)
+
+
+def packed_rows(rows, width):
+    return rows * (width // 128) + 8
+
+
+def pack(value, message):
+    rows, width = value.shape
+    full, left = width // 128, width % 128
+    for i in range(full):
+        message[i * rows : (i + 1) * rows, :] = value[:, i * 128 : (i + 1) * 128]
+    for i in range(rows // 8):
+        lanes = slice(i * left, (i + 1) * left)
+        message[full * rows : full * rows + 8, lanes] = value[i * 8 : (i + 1) * 8, full * 128 :]
+
+
+def unpack(message, rows, width, write):
+    full, left = width // 128, width % 128
+    for i in range(full):
+        write(0, rows, slice(i * 128, (i + 1) * 128), message[i * rows : (i + 1) * rows, :])
+    for i in range(rows // 8):
+        value = message[full * rows : full * rows + 8, i * left : (i + 1) * left]
+        write(i * 8, 8, slice(full * 128, width), value)
 
 
 def edge_rows(ref, y, size_x, size_y):
@@ -146,8 +162,8 @@
     copies[3].wait()
     total[...] = product(matrix, split(here[...].reshape(size_x * size_y, width)))
     near, far = x_rows(size_x * size_y, size_y)
-    x_near[:, :width] = total[near]
-    x_far[:, :width] = total[far]
+    pack(total[near], x_near)
+    pack(total[far], x_far)
     for first, message in ((0, low), (size_y - 4, high)):
         for i in range(4):
             rows = slice(i * size_x, (i + 1) * size_x)
@@ -155,6 +171,8 @@
             message[rows, width : width + 2] = edge_rows(columns, first + i, size_x, size_y)[:, :2]
     for copy in copies[4:]:
         copy.wait()
+    if x_far.shape[0] > x_near.shape[0]:
+        x_far[x_near.shape[0] :, :] = coefs[...]
 
 
 def node_column(values, start, count):
@@ -184,7 +202,7 @@
     else:
         own, partner = node_column(second[:, 3], 4, 8), node_column(second[:1, 3], 3, 8)
     along = inverse * (own * columns[rows, 0:1] + partner * columns[rows, 2:3])
-    lane = lax.broadcasted_iota(jnp.int32, (8, 128), 1) - width % 128
+    lane = lax.broadcasted_iota(jnp.int32, (8, 128), 1)
     place = lax.broadcasted_iota(jnp.int32, (8, 128), 0)
     tile = jnp.where(lane == line, along, 0.0)
     for i in range(4):
@@ -244,13 +262,16 @@
     line_ends,
     inner,
     work,
+    at_near,
+    at_far,
 ):
-    size_y, width = from_far.shape[0], total.shape[1]
+    size_y, width = total.shape[0] // size_x, total.shape[1]
+    depth = size_y + 8
     second = second_table()
-    near, far = x_rows(size_x * size_y, size_y)
+    near, far = x_starts(size_x * size_y, size_y)
     work[...] = total[...]
-    work[near] += from_near[:, :width]
-    work[far] += from_far[:, :width]
+    add_packed(work, near, from_near, size_y)
+    add_packed(work, far, from_far, size_y)
     sides = ((low, 0, 3, 0), (high, size_y - 1, 0, size_y - 8))
     beyond = []
     for message, y, line, _ in sides:
@@ -271,29 +292,37 @@
         for x in range(size_x):
             out[x * size_y + y : x * size_y + y + 1, :] += rows[x : x + 1]
 
-    x_near[:size_y, :width] = out[near]
-    x_far[:size_y, :width] = out[far]
+    near, far = x_rows(size_x * size_y, size_y)
+    at_near[:size_y, :] = out[near]
+    at_far[:size_y, :] = out[far]
+    last = depth * (width // 128)
+    lanes = depth // 8 * (width % 128)
     high_weights = side_weights(columns, high, size_x, size_y, width, 0)
-    for side, (message, y, line, start) in enumerate(sides):
+    for side, (message, _, line, _) in enumerate(sides):
         weights = high_weights if side else [low_weights[i : i + 8] for i in (0, 8, 16)]
-        behind = slice(width % 128, 128)
-        x_near[start : start + 8, width:] = weights[0][:, behind]
-        x_far[start : start + 8, width:] = weights[1][:, behind]
         inner[side * size_x : (side + 1) * size_x, :] = weights[2][:size_x]
+        place = slice(lanes + 8 * side, lanes + 8 * side + 5)
+        x_near[last : last + 8, place] = weights[0][:, :5]
+        x_far[last : last + 8, place] = weights[1][:, :5]
         for i in range(4):
-            rows = [
+            first, final = (
                 message[i * size_x + x : i * size_x + x + 1, :width] for x in (0, size_x - 1)
-            ]
-            at_near = jnp.where(even("gx"), rows[1], rows[0])
-            at_far = jnp.where(even("gx"), rows[0], rows[1])
+            )
+            row_near = jnp.where(even("gx"), final, first)
+            row_far = jnp.where(even("gx"), first, final)
             place = size_y + 4 * side + i
-            x_near[place : place + 1, :width] = at_near
-            x_far[place : place + 1, :width] = at_far
+            at_near[place : place + 1, :] = row_near
+            at_far[place : place + 1, :] = row_far
             if i == line:
-                line_ends[2 * side : 2 * side + 1, :] = at_far
-                line_ends[2 * side + 1 : 2 * side + 2, :] = at_near
-    if x_near.shape[0] > size_y + 8:
-        write_coefs(x_near, size_y + 8, coefs)
+                line_ends[2 * side : 2 * side + 1, :] = row_far
+                line_ends[2 * side + 1 : 2 * side + 2, :] = row_near
+    pack(at_near[...], x_near)
+    pack(at_far[...], x_far)
+    if x_near.shape[0] > x_far.shape[0]:
+        count = coefs.shape[0]
+        start = last + 8
+        x_near[start : start + count, :] = coefs[...]
+        x_near[start + count :, :] = from_far[packed_rows(size_y, width) :, :]
 
 
 def third_kernel(
@@ -314,33 +343,44 @@
     work,
     turned,
     values,
+    *unpacked,
 ):
     columns, width = total.shape
     size_x, size_y, _ = state.shape
     variables = width // levels
-    near = jnp.where(even("gx"), columns - size_y, 0)
+    rows = size_y + 8
+    last, lanes = rows * (width // 128), rows // 8 * (width % 128)
+    messages = (to_near, to_far, from_near, from_far)
+    for message, target in zip(messages, unpacked):
+
+        def write(first, count, lanes, value, target=target):
+            target[first : first + count, lanes] = value
+
+        unpack(message, rows, width, write)
+    to_near, to_far, from_near, from_far = unpacked
+    near, far = x_starts(columns, size_y)
     sides = ((0, 0, 3, 0), (1, size_y - 1, 0, size_y - 8))
     partners = (
         (near, to_near, from_near, from_far, ends_near, 0),
-        (columns - size_y - near, to_far, from_far, from_near, ends_far, 1),
+        (far, to_far, from_far, from_near, ends_far, 1),
     )
     work[...] = total[...]
     for start, _, theirs, _, _, _ in partners:
         work[pl.ds(pl.multiple_of(start, size_y), size_y), :] += theirs[:size_y, :width]
     for side, y, line, first in sides:
         place = size_y + 4 * side
-        tile = slice(first, first + 8)
-        for start, mine, theirs, others, ends, which in partners:
+        weights = [
+            message[last : last + 8, lanes + 8 * side : lanes + 8 * side + 5] for message in messages
+        ]
+        for which, (start, mine, theirs, others, ends, _) in enumerate(partners):
+            own, beyond = weights[which], weights[2 + which]
             terms = [
-                (weights, i, rows, place + i)
+                (weight[:, i : i + 1], values, place + i)
                 for i in range(4)
-                for weights, rows in ((mine, theirs), (theirs, mine))
+                for weight, values in ((own, theirs), (beyond, mine))
             ]
-            terms += [(mine, 4, others, place + line), (theirs, 4, ends, 2 * side + which)]
-            added = sum(
-                weights[tile, width + i : width + i + 1] * rows[row : row + 1, :width]
-                for weights, i, rows, row in terms
-            )
+            terms += [(own[:, 4:5], others, place + line), (beyond[:, 4:5], ends, 2 * side + which)]
+            added = sum(weight * values[row : row + 1, :width] for weight, values, row in terms)
             work[pl.ds(pl.multiple_of(start + first, 8), 8), :] += added
         for x in range(1, size_x - 1):
             row, weight = x * size_y + y, side * size_x + x
@@ -390,21 +430,18 @@
     return picked
 
 
-def pass_kernel(arrived, passed):
-    passed[...] = arrived[...]
-
-
 def factor_kernel(levels, slots, *refs):
     factors = refs[-1]
-    if len(refs) == 5:
-        own, from_far, relayed, from_near = refs[:4]
+    if len(refs) == 4:
+        own, from_far, from_near = refs[:3]
         here = lax.axis_index("gx")
-        near = read_coefs(from_near, slots.shape[1] + 8, *own.shape)
+        count = own.shape[0]
+        far, near = from_far.shape[0] - count, from_near.shape[0] - 2 * count
         pieces = [
             (here, own[...]),
-            (here ^ 3, from_far[...]),
-            (here ^ 2, relayed[...]),
-            (here ^ 1, near),
+            (here ^ 3, from_far[far:, :]),
+            (here ^ 1, from_near[near : near + count, :]),
+            (here ^ 2, from_near[near + count :, :]),
         ]
     else:
         pieces = [(peer, refs[0][peer]) for peer in range(refs[0].shape[0])]
@@ -478,14 +515,16 @@
     riding = lax.axis_size("gx") == 4
     whole = array(columns, width)
     edge = array(4 * size_x, padded)
+    extra = 3 * levels if riding else 0
+    first_rows, last_rows = packed_rows(size_y, width), packed_rows(size_y + 8, width)
     here, total, x_near, x_far, y_low, y_high, operator, masses, coefs = call(
         start_kernel,
         "start",
         [
             array(size_x, size_y, width),
             whole,
-            array(size_y, padded),
-            array(size_y, padded),
+            array(first_rows, 128),
+            array(first_rows + extra, 128),
             edge,
             edge,
             array(columns, columns),
@@ -515,8 +554,6 @@
     low = shifted(y_high, "gy", 1)
     from_far, from_near = exchanged(x_near, x_far, "gx")
     y_low, _ = lax.optimization_barrier((y_low, from_near))
-    sent, _ = lax.optimization_barrier((coefs, from_near))
-    coefs_far = swapped(sent, "gx", lambda i: i ^ 3) if riding else None
     high = shifted(y_low, "gy", -1)
     (low_weights,) = call(
         functools.partial(weights_kernel, size_x, size_y, width),
@@ -532,12 +569,12 @@
         "second",
         [
             whole,
-            array(size_y + 8 + (COEF_ROWS if riding else 0), padded),
-            array(size_y + 8, padded),
+            array(last_rows + 2 * extra, 128),
+            array(last_rows, 128),
             array(4, width),
             array(2 * size_x, 128),
         ],
-        [scratch(columns, width)],
+        [scratch(columns, width), scratch(size_y + 8, width), scratch(size_y + 8, width)],
         total,
         masses,
         operator,
@@ -555,16 +592,7 @@
     if peers != 4:
         ends_far = swapped(line_ends, "gx", lambda i: (i - (2 if i % 2 else -2)) % peers)
     if riding:
-        (passed,) = call(
-            pass_kernel,
-            "pass",
-            [array(3 * levels, span)],
-            [],
-            coefs_far,
-            cost=LONG,
-        )
-        relayed = swapped(passed, "gx", lambda i: i ^ 1)
-        pieces = [coefs, coefs_far, relayed, last_x[1]]
+        pieces = [coefs, from_far, last_x[1]]
     else:
         pieces = [lax.all_gather(coefs, "gx")]
     (factors,) = call(
@@ -579,7 +607,8 @@
         functools.partial(third_kernel, levels),
         "third",
         [array(size_x, size_y, width)],
-        [scratch(columns, width), scratch(width, columns), scratch(levels, 16, columns)],
+        [scratch(columns, width), scratch(width, columns), scratch(levels, 16, columns)]
+        + [scratch(size_y + 8, width)] * 4,
         here,
         hyper,
         total,

time: 19.4 us -> 18.5 us (0.954)
  starting transfers between devices: 11.1 us -> 9.85 us
    ppermute x7 -> x5, starting transfers between devices: 5.19 us -> 3.95 us  [swapped(): lax.ppermute(value, axis, [(i, partner(i)) for i in range(lax.axis_size(a...]
    ppermute x2, waiting for transfers between devices: 0.75 us -> 1.39 us  [shifted(): lax.ppermute(value, axis, [(i, (i + step) % size) for i in range(size)])]
    ppermute x7 -> x5, waiting for transfers between devices: 2.53 us -> 2.08 us  [swapped(): lax.ppermute(value, axis, [(i, partner(i)) for i in range(lax.axis_size(a...]
    pallas_call x6 -> x5, Pallas kernels: 4.79 us -> 4.96 us  [call(): pl.pallas_call(kernel, out_shape=outs, in_specs=[spec] * len(operands), o...]
  transfers between devices with their start and end apart: 9 -> 7, of which waited for: 4 -> 3; matrix products, arithmetic and copies ran while one was open for 0% -> 0% of each run, Pallas kernels for 8% -> 6%
where the time goes in v3:
time: 18.5 us; the launch traced here: 18.3 us
  starting transfers between devices  9.85 us (53%)
  Pallas kernels  4.96 us (27%)
  waiting for transfers between devices  3.46 us (19%)
    ppermute x2, starting transfers between devices, shifted(): lax.ppermute(value, axis, [(i, (i + step) % size) for i in range(size)])  5.91 us
    pallas_call x5, Pallas kernels, call(): pl.pallas_call(kernel, out_shape=outs, in_specs=[spec] * len(operands), o...  4.96 us
    ppermute x5, starting transfers between devices, swapped(): lax.ppermute(value, axis, [(i, partner(i)) for i in range(lax.axis_size(a...  3.95 us
    ppermute x5, waiting for transfers between devices, swapped(): lax.ppermute(value, axis, [(i, partner(i)) for i in range(lax.axis_size(a...  2.08 us
    ppermute x2, waiting for transfers between devices, shifted(): lax.ppermute(value, axis, [(i, (i + step) % size) for i in range(size)])  1.39 us
  transfers between devices with their start and end apart: 7, of which 3 were waited for; matrix products, arithmetic and copies ran while one was open for 0% of the time, Pallas kernels for 6%

profile of v3, /device:TPU:0, one launch (start us, length us, event | category | flops | bytes accessed | tf_op | source)
XLA Modules:
  0.0 18.3 jit_solution(11496981254638056284)
XLA Ops:
  0.0 1.7 %start.1 = (f32[4,32,528]{2,1,0:T(8,128)S(1)}, f32[128,528]{1,0:T(8,128)S(1)}, f32[136,128]{1,0:T(8,128)S(1)}, f32[280,128]{1,0:T(8,128)S(1)}, f32[16,640]{1,0:T...) custom-call(f32[4,32,528]{2,1,0:T(8,128)} %state.1, ...), custom_call_target="tpu_custom_call" | custom-call | tf_op jit(solution)/shard_map/start/pallas_call | solution.py:504
  1.7 0.5 %collective-permute-start.2 = (f32[136,128]{1,0:T(8,128)S(1)}, f32[136,128]{1,0:T(8,128)S(1)}, u32[]{:S(2)}, u32[]{:S(2)}) collective-permute-start(f32[136,128]{1,0:T(8,128)S(1)} %get-tuple-element.27), channel_id=1, source_target_pairs={{0,8},{8,0},{16,24},{24,16},{1,9},{9,1},{17,25},{25,17},{2,10},{10... | collective-permute-start | bytes 208904 | tf_op jit(solution)/shard_map/ppermute | solution.py:472
  2.2 2.6 %collective-permute-start = (f32[16,640]{1,0:T(8,128)S(1)}, f32[16,640]{1,0:T(8,128)S(1)}, u32[]{:S(2)}, u32[]{:S(2)}) collective-permute-start(f32[16,640]{1,0:T(8,128)S(1)} %get-tuple-element.25), channel_id=1, source_target_pairs={{0,1},{1,2},{2,3},{3,4},{4,5},{5,6},{6,7},{7,0},{8,9},{9,10},{10,1... | collective-permute-start | bytes 122888 | tf_op jit(solution)/shard_map/ppermute | solution.py:484
  4.8 1.3 %collective-permute-start.1 = (f32[280,128]{1,0:T(8,128)S(1)}, f32[280,128]{1,0:T(8,128)S(1)}, u32[]{:S(2)}, u32[]{:S(2)}) collective-permute-start(f32[280,128]{1,0:T(8,128)S(1)} %get-tuple-element.26), channel_id=1, source_target_pairs={{0,24},{8,16},{16,8},{24,0},{1,25},{9,17},{17,9},{25,1},{2,26},{10... | collective-permute-start | bytes 430088 | tf_op jit(solution)/shard_map/ppermute | solution.py:472
  6.0 0.0 collective-permute-done.2.from_near
  6.0 3.3 %collective-permute-start.3 = (f32[16,640]{1,0:T(8,128)S(1)}, f32[16,640]{1,0:T(8,128)S(1)}, u32[]{:S(2)}, u32[]{:S(2)}) collective-permute-start(f32[16,640]{1,0:T(8,128)S(1)} %get-tuple-element.29), channel_id=1, source_target_pairs={{0,7},{1,0},{2,1},{3,2},{4,3},{5,4},{6,5},{7,6},{8,15},{9,8},{10,9... | collective-permute-start | bytes 122888 | tf_op jit(solution)/shard_map/ppermute | solution.py:484
  9.4 0.7 %collective-permute-done.message.low = f32[16,640]{1,0:T(8,128)S(1)} collective-permute-done((f32[16,640]{1,0:T(8,128)S(1)}, f32[16,640]{1,0:T(8,128)S(1)}, u32[]{:S(2)}, u32[]{:S(2)}) %collective-permute-start) | collective-permute-done | bytes 40992 | tf_op jit(solution)/shard_map/ppermute | solution.py:484
  10.1 0.3 %weights.1.low_weights = f32[24,128]{1,0:T(8,128)S(1)} custom-call(f32[128,128]{1,0:T(8,128)S(1)} %get-tuple-element.22.columns.masses, f32[16,640]{1,0:T(8,128)S(1)} %collective-permute-done.message.low), custom_call_target="tpu_custom_call" | custom-call | flops 99999997952 | bytes 30000000 | tf_op jit(solution)/shard_map/weights/pallas_call | solution.py:504
  10.4 0.7 %collective-permute-done.3.high = f32[16,640]{1,0:T(8,128)S(1)} collective-permute-done((f32[16,640]{1,0:T(8,128)S(1)}, f32[16,640]{1,0:T(8,128)S(1)}, u32[]{:S(2)}, u32[]{:S(2)}) %collective-permute-start.3) | collective-permute-done | bytes 40992 | tf_op jit(solution)/shard_map/ppermute | solution.py:484
  11.0 0.0 collective-permute-done.1.from_far.refs_1_
  11.0 0.5 %second.1 = (f32[128,528]{1,0:T(8,128)S(1)}, f32[456,128]{1,0:T(8,128)S(1)}, f32[168,128]{1,0:T(8,128)S(1)}, f32[4,528]{1,0:T(4,128)S(1)}, f32[8,128]{1,0:T(8,128)S(1)}) custom-call(f32[128,528]{1,0:T(8,128)S(1)} %get-tuple-element.21.total, f32[128,128]{1,0:T(8,128)S(1)} %get-tuple-element.22.columns.masses, f32[128,128]{1,0:T(8,128)S(1)} %get-tuple-element.23.operator, ...), custom_call_target="tpu_custom_call" | custom-call | tf_op jit(solution)/shard_map/second/pallas_call | solution.py:504
  11.6 0.0 copy-start.1
  11.6 0.0 collective-permute-start.4
  11.6 1.3 %collective-permute-start.5 = (f32[168,128]{1,0:T(8,128)S(1)}, f32[168,128]{1,0:T(8,128)S(1)}, u32[]{:S(2)}, u32[]{:S(2)}) collective-permute-start(f32[168,128]{1,0:T(8,128)S(1)} %get-tuple-element.33.to_far), channel_id=1, source_target_pairs={{0,24},{8,16},{16,8},{24,0},{1,25},{9,17},{17,9},{25,1},{2,26},{10... | collective-permute-start | bytes 258056 | tf_op jit(solution)/shard_map/ppermute | solution.py:472
  12.9 0.0 copy-start
  12.9 0.9 %collective-permute-start.6 = (f32[4,528]{1,0:T(4,128)S(1)}, f32[4,528]{1,0:T(4,128)S(1)}, u32[]{:S(2)}, u32[]{:S(2)}) collective-permute-start(f32[4,528]{1,0:T(4,128)S(1)} %get-tuple-element.34), channel_id=1, source_target_pairs={{0,16},{8,24},{16,0},{24,8},{1,17},{9,25},{17,1},{25,9},{2,18},{10... | collective-permute-start | bytes 25352 | tf_op jit(solution)/shard_map/ppermute | solution.py:472
  13.8 0.0 copy-done.1
  13.8 0.0 collective-permute-done.4.refs_2_.from_near
  13.8 0.0 copy-done
  13.8 0.9 %factors.1 = f32[288,128]{1,0:T(8,128)S(1)} custom-call(s32[4,32]{1,0:T(4,128)S(1)} %copy-done, f32[144,128]{1,0:T(8,128)S(1)} %get-tuple-element.24.coefs.refs_0_, f32[280,128]{1,0:T(8,128)S(1)} %collective-permute-done.1.from_far.refs_1_, f32[456,128]{1,0:T(8,128)S(1)} %collective-permute-done.4.refs_2_.from_near), custom_call_target="tpu_custom_call" | custom-call | tf_op jit(solution)/shard_map/factors/pallas_call | solution.py:504
  14.7 2.1 %collective-permute-done.6.ends_near.ends_far = f32[4,528]{1,0:T(4,128)S(1)} collective-permute-done((f32[4,528]{1,0:T(4,128)S(1)}, f32[4,528]{1,0:T(4,128)S(1)}, u32[]{:S(2)}, u32[]{:S(2)}) %collective-permute-start.6) | collective-permute-done | bytes 8480 | tf_op jit(solution)/shard_map/ppermute | solution.py:472
  16.7 0.0 collective-permute-done.5.from_far
  16.7 1.6 %third.1 = f32[4,32,528]{2,1,0:T(8,128)} custom-call(f32[4,32,528]{2,1,0:T(8,128)S(1)} %get-tuple-element.20.state, f32[1,528]{1,0:T(1,128)S(1)} %reshape.3.hyper, f32[128,528]{1,0:T(8,128)S(1)} %get-tuple-element.30.total, f32[128,128]{1,0:T(8,128)S(1)} %get-tuple-element.22.columns.masses, f32[8,128]{1,0:T(8,128)S(1)} %get-tuple-element.31.inner, ...), custom_call_target="tpu_custom_call" | custom-call | tf_op jit(solution)/shard_map/third/pallas_call | solution.py:504
  (1 shorter events, 0.0 us)
Async XLA Ops:
  1.7 4.4 %collective-permute-start.2 = (f32[136,128]{1,0:T(8,128)S(1)}, f32[136,128]{1,0:T(8,128)S(1)}, u32[]{:S(2)}, u32[]{:S(2)}) collective-permute-start(f32[136,128]{1,0:T(8,128)S(1)} %get-tuple-element.27), channel_id=1, source_target_pairs={{0,8},{8,0},{16,24},{24,16},{1,9},{9,1},{17,25},{25,17},{2,10},{10... | collective-permute-start | bytes 208904 | tf_op jit(solution)/shard_map/ppermute | solution.py:472
  2.2 7.9 %collective-permute-start = (f32[16,640]{1,0:T(8,128)S(1)}, f32[16,640]{1,0:T(8,128)S(1)}, u32[]{:S(2)}, u32[]{:S(2)}) collective-permute-start(f32[16,640]{1,0:T(8,128)S(1)} %get-tuple-element.25), channel_id=1, source_target_pairs={{0,1},{1,2},{2,3},{3,4},{4,5},{5,6},{6,7},{7,0},{8,9},{9,10},{10,1... | collective-permute-start | bytes 122888 | tf_op jit(solution)/shard_map/ppermute | solution.py:484
  4.8 6.3 %collective-permute-start.1 = (f32[280,128]{1,0:T(8,128)S(1)}, f32[280,128]{1,0:T(8,128)S(1)}, u32[]{:S(2)}, u32[]{:S(2)}) collective-permute-start(f32[280,128]{1,0:T(8,128)S(1)} %get-tuple-element.26), channel_id=1, source_target_pairs={{0,24},{8,16},{16,8},{24,0},{1,25},{9,17},{17,9},{25,1},{2,26},{10... | collective-permute-start | bytes 430088 | tf_op jit(solution)/shard_map/ppermute | solution.py:472
  6.0 5.0 %collective-permute-start.3 = (f32[16,640]{1,0:T(8,128)S(1)}, f32[16,640]{1,0:T(8,128)S(1)}, u32[]{:S(2)}, u32[]{:S(2)}) collective-permute-start(f32[16,640]{1,0:T(8,128)S(1)} %get-tuple-element.29), channel_id=1, source_target_pairs={{0,7},{1,0},{2,1},{3,2},{4,3},{5,4},{6,5},{7,6},{8,15},{9,8},{10,9... | collective-permute-start | bytes 122888 | tf_op jit(solution)/shard_map/ppermute | solution.py:484
  11.6 2.2 %copy-start.1 = (f32[528]{0:T(1024)S(1)}, f32[528]{0:T(1024)}, u32[]{:S(2)}) copy-start(f32[528]{0:T(1024)} %param.10) | copy-start | bytes 6340
  11.6 2.2 %collective-permute-start.4 = (f32[456,128]{1,0:T(8,128)S(1)}, f32[456,128]{1,0:T(8,128)S(1)}, u32[]{:S(2)}, u32[]{:S(2)}) collective-permute-start(f32[456,128]{1,0:T(8,128)S(1)} %get-tuple-element.32.to_near), channel_id=1, source_target_pairs={{0,8},{8,0},{16,24},{24,16},{1,9},{9,1},{17,25},{25,17},{2,10},{10... | collective-permute-start | bytes 700424 | tf_op jit(solution)/shard_map/ppermute | solution.py:472
  11.6 5.1 %collective-permute-start.5 = (f32[168,128]{1,0:T(8,128)S(1)}, f32[168,128]{1,0:T(8,128)S(1)}, u32[]{:S(2)}, u32[]{:S(2)}) collective-permute-start(f32[168,128]{1,0:T(8,128)S(1)} %get-tuple-element.33.to_far), channel_id=1, source_target_pairs={{0,24},{8,16},{16,8},{24,0},{1,25},{9,17},{17,9},{25,1},{2,26},{10... | collective-permute-start | bytes 258056 | tf_op jit(solution)/shard_map/ppermute | solution.py:472
  12.9 0.9 %copy-start = (s32[4,32]{1,0:T(4,128)S(1)}, s32[4,32]{1,0:T(4,128)}, u32[]{:S(2)}) copy-start(s32[4,32]{1,0:T(4,128)} %slots.1) | copy-start | bytes 1540
  12.9 3.9 %collective-permute-start.6 = (f32[4,528]{1,0:T(4,128)S(1)}, f32[4,528]{1,0:T(4,128)S(1)}, u32[]{:S(2)}, u32[]{:S(2)}) collective-permute-start(f32[4,528]{1,0:T(4,128)S(1)} %get-tuple-element.34), channel_id=1, source_target_pairs={{0,16},{8,24},{16,0},{24,8},{1,17},{9,25},{17,1},{25,9},{2,18},{10... | collective-permute-start | bytes 25352 | tf_op jit(solution)/shard_map/ppermute | solution.py:472

commit v4 on v3

--- a/solution.py
+++ b/solution.py
@@ -27,40 +27,55 @@
     return deriv @ deriv
 
 
-def laplacian_tables(size_x, size_y):
-    second = second_table()
-    lap = np.kron(np.kron(np.eye(size_x // 4), second), np.eye(size_y))
-    lap = lap + np.kron(np.eye(size_x), np.kron(np.eye(size_y // 4), second))
-    partner = np.zeros_like(lap)
-    for x in range(size_x):
-        for y in range(size_y):
-            other = y - 1 if y % 4 == 0 else y + 1 if y % 4 == 3 else -1
-            if 0 <= other < size_y:
-                partner[x * size_y + y] = lap[x * size_y + other]
-    return np.stack([lap, partner]).astype(np.float32)
-
-
 def split(value):
     high = value.astype(jnp.bfloat16)
     return high, (value - high.astype(jnp.float32)).astype(jnp.bfloat16)
 
 
 def product(left, right):
-    left_high, left_low = left
-    right_high, right_low = right
-    dot = functools.partial(jnp.dot, preferred_element_type=jnp.float32)
-    return dot(left_high, right_high) + (dot(left_high, right_low) + dot(left_low, right_high))
-
-
-def to_column(plane, partner=False):
+    left = jnp.concatenate([left[0], left[1], left[0]], axis=1)
+    right = jnp.concatenate([right[0], right[0], right[1]], axis=0)
+    return jnp.dot(left, right, preferred_element_type=jnp.float32)
+
+
+def lookup(row, lane):
+    second = second_table()
+    row, lane = lax.rem(row, 4), lax.rem(lane, 4)
+    result = jnp.zeros(row.shape, jnp.float32)
+    for j in range(4):
+        column = jnp.full(row.shape, float(second[3, j]), jnp.float32)
+        for i in range(3):
+            column = jnp.where(row == i, float(second[i, j]), column)
+        result = jnp.where(lane == j, column, result)
+    return result
+
+
+def laplacian(size_x, size_y):
+    count = size_x * size_y
+    row, lane = (lax.broadcasted_iota(jnp.int32, (count, count), i) for i in range(2))
+    row_x, lane_x = lax.div(row, size_y), lax.div(lane, size_y)
+    row_y, lane_y = lax.rem(row, size_y), lax.rem(lane, size_y)
+    same_x = (row_y == lane_y) & (lax.div(row_x, 4) == lax.div(lane_x, 4))
+    same_y = (row_x == lane_x) & (lax.div(row_y, 4) == lax.div(lane_y, 4))
+    along_x = jnp.where(same_x, lookup(row_x, lane_x), 0.0)
+    return along_x + jnp.where(same_y, lookup(row_y, lane_y), 0.0)
+
+
+def of_partner(values, size_y):
+    count = values.shape[0]
+    row_y = lax.rem(lax.broadcasted_iota(jnp.int32, values.shape, 0), size_y)
+    phase = lax.rem(row_y, 4)
+    before = jnp.where((phase == 0) & (row_y > 0), pltpu.roll(values, 1, 0), 0.0)
+    after = (phase == 3) & (row_y < size_y - 1)
+    return jnp.where(after, pltpu.roll(values, count - 1, 0), before)
+
+
+def to_column(plane):
     size_x, size_y = plane.shape
     row = lax.broadcasted_iota(jnp.int32, (size_y, size_y), 0)
     lane = lax.broadcasted_iota(jnp.int32, (size_y, size_y), 1)
-    if partner:
-        row = jnp.where(row % 4 == 0, row - 1, jnp.where(row % 4 == 3, row + 1, -1))
-    pick = row == lane
     parts = [
-        jnp.sum(jnp.where(pick, plane[x : x + 1, :], 0.0), axis=1, keepdims=True)
+        jnp.sum(jnp.where(row == lane, plane[x : x + 1, :], 0.0), axis=1, keepdims=True)
         for x in range(size_x)
     ]
     return jnp.concatenate(parts, axis=0)
@@ -123,7 +138,6 @@
     diff,
     fall,
     cloud,
-    tables,
     here,
     total,
     x_near,
@@ -135,12 +149,12 @@
     coefs,
     mass_here,
     inverse_here,
-    tables_here,
     sems,
 ):
     size_x, size_y, width = state.shape
     levels = diff.shape[1]
-    pairs = [(mass, mass_here), (tables, tables_here), (inverse, inverse_here), (state, here)]
+    pairs = [(mass, mass_here), (inverse, inverse_here)]
+    pairs += [(state.at[x], here.at[x]) for x in range(size_x)]
     for i, source in enumerate((diff, fall, cloud)):
         pairs.append((source.at[0], coefs.at[i * levels : (i + 1) * levels]))
     copies = [
@@ -149,19 +163,22 @@
     ]
     for copy in copies:
         copy.start()
-    for copy in copies[:3]:
+    count = size_x * size_y
+    matrix = laplacian(size_x, size_y)
+    for copy in copies[:2]:
         copy.wait()
-    own = to_column(mass_here[...])
+    own = jnp.broadcast_to(to_column(mass_here[...]), (count, count))
+    matrix = own * matrix
+    matrix = matrix + of_partner(matrix, size_y)
+    operator[...] = matrix
+    partner = of_partner(own, size_y)
+    inverses = to_column(inverse_here[...])
     lane = lax.broadcasted_iota(jnp.int32, columns.shape, 1)
-    partner = to_column(mass_here[...], True)
-    inverses = to_column(inverse_here[...])
     columns[...] = jnp.where(lane == 0, own, jnp.where(lane == 1, inverses, partner))
-    matrix = own * tables_here[0] + partner * tables_here[1]
-    operator[...] = matrix
-    matrix = split(matrix)
-    copies[3].wait()
-    total[...] = product(matrix, split(here[...].reshape(size_x * size_y, width)))
-    near, far = x_rows(size_x * size_y, size_y)
+    for copy in copies[2 : 2 + size_x]:
+        copy.wait()
+    total[...] = product(split(matrix), split(here[...].reshape(count, width)))
+    near, far = x_rows(count, size_y)
     pack(total[near], x_near)
     pack(total[far], x_far)
     for first, message in ((0, low), (size_y - 4, high)):
@@ -169,7 +186,7 @@
             rows = slice(i * size_x, (i + 1) * size_x)
             message[rows, :width] = edge_rows(total, first + i, size_x, size_y)
             message[rows, width : width + 2] = edge_rows(columns, first + i, size_x, size_y)[:, :2]
-    for copy in copies[4:]:
+    for copy in copies[2 + size_x :]:
         copy.wait()
     if x_far.shape[0] > x_near.shape[0]:
         x_far[x_near.shape[0] :, :] = coefs[...]
@@ -343,6 +360,8 @@
     work,
     turned,
     values,
+    staged,
+    sems,
     *unpacked,
 ):
     columns, width = total.shape
@@ -390,28 +409,54 @@
             )
     twice = masses[:, 1:2] * work[...]
     turned[...] = (state[...].reshape(columns, width) - hyper[...] * twice).T
-    scale, down, up, keep, flow, cloud = (
+    scale, carry, gain, keep, flow, cloud = (
         factors.at[i * levels : (i + 1) * levels] for i in range(6)
     )
-    value = jnp.zeros((variables, columns), jnp.float32)
-    for k in range(levels):
-        rows = turned[pl.ds(k, variables, stride=levels), :]
-        value = rows * scale[k : k + 1, :] + down[k : k + 1, :] * value
-        values[k, :variables, :] = value
-    solved = jnp.zeros((variables, columns), jnp.float32)
-    for k in reversed(range(levels)):
-        solved = values[k, :variables, :] + up[k : k + 1, :] * solved
-        turned[pl.ds(k, variables, stride=levels), :] = solved
+
+    def level(k):
+        return pl.ds(k, variables, stride=levels)
+
+    half = levels // 2
+    known = [jnp.zeros((variables, columns), jnp.float32)] * 2
+    for i in range(half):
+        for side, k in enumerate((i, levels - 1 - i)):
+            scaled = turned[level(k), :] * scale[k : k + 1, :]
+            known[side] = scaled + carry[k : k + 1, :] * known[side]
+            values[k, :variables, :] = known[side]
+    meet = factors[6 * levels + half : 6 * levels + half + 1, :]
+    first = (known[0] + gain[half - 1 : half, :] * known[1]) * meet
+    solved = [first, known[1] + gain[half : half + 1, :] * first]
+    for i in reversed(range(half)):
+        for side, k in enumerate((i, levels - 1 - i)):
+            if i < half - 1:
+                solved[side] = values[k, :variables, :] + gain[k : k + 1, :] * solved[side]
+            turned[level(k), :] = solved[side]
+
+    def leave(i):
+        lanes = slice(i * 128, min((i + 1) * 128, width))
+        staged[:, :, lanes] = turned[lanes, :].T.reshape(size_x, size_y, -1)
+        copy = pltpu.make_async_copy(staged.at[:, :, lanes], out.at[:, :, lanes], sems.at[i])
+        copy.start()
+        return copy
+
+    tiles = -(-width // 128)
+    settled_tiles = -(-3 * levels // 128)
+    copies = [leave(i) for i in range(settled_tiles, tiles)]
     heat, vapour, liquid = (turned.at[i * levels : (i + 1) * levels] for i in range(3))
     condensed = cloud[...] * 0.5 * jnp.maximum(vapour[...] - 0.3 * heat[...], 0.0)
     vapour[...] = vapour[...] - condensed
     heat[...] = heat[...] + 2.0 * condensed
     liquid[...] = (liquid[...] + condensed) * keep[...]
-    settled = jnp.zeros((1, columns), jnp.float32)
-    for k in range(levels):
-        settled = liquid[k : k + 1, :] + flow[k : k + 1, :] * settled
-        liquid[k : k + 1, :] = settled
-    out[...] = turned[...].T.reshape(out.shape)
+    settled = [jnp.zeros((1, columns), jnp.float32)] * 2
+    for i in range(half):
+        for side, k in enumerate((i, half + i)):
+            settled[side] = liquid[k : k + 1, :] + flow[k : k + 1, :] * settled[side]
+            liquid[k : k + 1, :] = settled[side]
+    through = factors[6 * levels : 6 * levels + half, :]
+    liquid[half:, :] = liquid[half:, :] + through * settled[0]
+    copies += [leave(i) for i in range(settled_tiles)]
+    for copy in copies:
+        copy.wait()
 
 
 def pick(slots, pieces):
@@ -448,24 +493,34 @@
     columns = factors.shape[1]
     picked = pick(slots, pieces)
     mixing, falling, covered = (picked[i * levels : (i + 1) * levels] for i in range(3))
-    scale, down, up, keep, flow, cover = (
+    scale, carry, gain, keep, flow, cover = (
         factors.at[i * levels : (i + 1) * levels] for i in range(6)
     )
-    gain = jnp.zeros((1, columns), jnp.float32)
-    for k in range(levels):
-        above = mixing[k : k + 1] if k else jnp.zeros_like(gain)
-        below = mixing[k + 1 : k + 2] if k + 1 < levels else jnp.zeros_like(gain)
-        centre = 1.0 + above + (below if k + 1 < levels else mixing[:1])
-        inverse = 1.0 / (centre - above * gain)
-        gain = below * inverse
-        scale[k : k + 1, :] = inverse
-        down[k : k + 1, :] = above * inverse
-        up[k : k + 1, :] = gain
+    zero = jnp.zeros((1, columns), jnp.float32)
     kept = 1.0 / (1.0 + falling)
     keep[...] = kept
-    flow[:1, :] = jnp.zeros((1, columns), jnp.float32)
+    flow[:1, :] = zero
     flow[1:, :] = falling[:-1] * kept[1:]
     cover[...] = covered
+    half = levels // 2
+    gains = [zero, zero]
+    through = jnp.ones((1, columns), jnp.float32)
+    for i in range(half):
+        for side, k in enumerate((i, levels - 1 - i)):
+            above = mixing[k : k + 1] if k else zero
+            below = mixing[k + 1 : k + 2] if k + 1 < levels else zero
+            centre = 1.0 + above + (below if k + 1 < levels else mixing[:1])
+            behind, ahead = (above, below) if side == 0 else (below, above)
+            inverse = 1.0 / (centre - behind * gains[side])
+            gains[side] = ahead * inverse
+            scale[k : k + 1, :] = inverse
+            carry[k : k + 1, :] = behind * inverse
+            gain[k : k + 1, :] = gains[side]
+        k = half + i
+        through = through * falling[k - 1 : k] * kept[k : k + 1]
+        factors[6 * levels + i : 6 * levels + i + 1, :] = through
+    last = 6 * levels + half
+    factors[last : last + 1, :] = 1.0 / (1.0 - gains[0] * gains[1])
 
 
 def swapped(value, axis, partner):
@@ -492,7 +547,6 @@
     columns = size_x * size_y
     hyper = hyper_coef.reshape(1, width)
     padded = -(-(width + 5) // 128) * 128
-    tables = jnp.asarray(laplacian_tables(size_x, size_y))
 
     def array(*shape):
         return jax.ShapeDtypeStruct(shape, jnp.float32)
@@ -500,12 +554,12 @@
     def scratch(*shape):
         return pltpu.VMEM(shape, jnp.float32)
 
-    def call(kernel, name, outs, scratches, *operands, spec=VMEM, cost=None):
+    def call(kernel, name, outs, scratches, *operands, spec=VMEM, out=VMEM, cost=None):
         return pl.pallas_call(
             kernel,
             out_shape=outs,
             in_specs=[spec] * len(operands),
-            out_specs=[VMEM] * len(outs),
+            out_specs=[out] * len(outs),
             scratch_shapes=scratches,
             compiler_params=PARAMS,
             cost_estimate=cost,
@@ -534,8 +588,7 @@
         [
             scratch(size_x, size_y),
             scratch(size_x, size_y),
-            scratch(*tables.shape),
-            pltpu.SemaphoreType.DMA((7,)),
+            pltpu.SemaphoreType.DMA((size_x + 5,)),
         ],
         *(
             pltpu.with_memory_space_constraint(value, pltpu.HBM)
@@ -546,7 +599,6 @@
                 vert_diff,
                 fall_rate,
                 cloud_frac,
-                tables,
             )
         ),
         spec=pl.BlockSpec(memory_space=pltpu.HBM),
@@ -598,7 +650,7 @@
     (factors,) = call(
         functools.partial(factor_kernel, levels),
         "factors",
-        [array(6 * levels, columns)],
+        [array(6 * levels + levels // 2 + 8, columns)],
         [],
         span_slot,
         *pieces,
@@ -607,7 +659,13 @@
         functools.partial(third_kernel, levels),
         "third",
         [array(size_x, size_y, width)],
-        [scratch(columns, width), scratch(width, columns), scratch(levels, 16, columns)]
+        [
+            scratch(columns, width),
+            scratch(width, columns),
+            scratch(levels, 16, columns),
+            scratch(size_x, size_y, width),
+            pltpu.SemaphoreType.DMA((-(-width // 128),)),
+        ]
         + [scratch(size_y + 8, width)] * 4,
         here,
         hyper,
@@ -620,6 +678,7 @@
         *last_x,
         ends_near,
         ends_far,
+        out=pl.BlockSpec(memory_space=pltpu.HBM),
     )
     return result
 

time: 18.5 us -> 18.3 us (0.989)
  Pallas kernels: 4.96 us -> 4.51 us
  waiting for transfers between devices: 3.46 us -> 3.68 us
    pallas_call x5, Pallas kernels: 4.96 us -> 4.51 us  [call(): pl.pallas_call(kernel, out_shape=outs, in_specs=[spec] * len(operands), o...]
    ppermute x5, waiting for transfers between devices: 2.08 us -> 2.29 us  [swapped(): lax.ppermute(value, axis, [(i, partner(i)) for i in range(lax.axis_size(a...]
  transfers between devices with their start and end apart: 7 -> 7, of which waited for: 3 -> 3; matrix products, arithmetic and copies ran while one was open for 0% -> 0% of each run, Pallas kernels for 6% -> 5%
where the time goes in v4:
time: 18.3 us; the launch traced here: 18.1 us
  starting transfers between devices  9.86 us (54%)
  Pallas kernels  4.51 us (25%)
  waiting for transfers between devices  3.68 us (20%)
    ppermute x2, starting transfers between devices, shifted(): lax.ppermute(value, axis, [(i, (i + step) % size) for i in range(size)])  5.9 us
    pallas_call x5, Pallas kernels, call(): pl.pallas_call(kernel, out_shape=outs, in_specs=[spec] * len(operands), o...  4.51 us
    ppermute x5, starting transfers between devices, swapped(): lax.ppermute(value, axis, [(i, partner(i)) for i in range(lax.axis_size(a...  3.95 us
    ppermute x5, waiting for transfers between devices, swapped(): lax.ppermute(value, axis, [(i, partner(i)) for i in range(lax.axis_size(a...  2.29 us
    ppermute x2, waiting for transfers between devices, shifted(): lax.ppermute(value, axis, [(i, (i + step) % size) for i in range(size)])  1.39 us
  transfers between devices with their start and end apart: 7, of which 3 were waited for; matrix products, arithmetic and copies ran while one was open for 0% of the time, Pallas kernels for 5%

profile of v4, /device:TPU:0, one launch (start us, length us, event | category | flops | bytes accessed | tf_op | source)
XLA Modules:
  0.0 18.1 jit_solution(10626016615505347211)
XLA Ops:
  0.0 1.5 %start.1 = (f32[4,32,528]{2,1,0:T(8,128)S(1)}, f32[128,528]{1,0:T(8,128)S(1)}, f32[136,128]{1,0:T(8,128)S(1)}, f32[280,128]{1,0:T(8,128)S(1)}, f32[16,640]{1,0:T...) custom-call(f32[4,32,528]{2,1,0:T(8,128)} %state.1, ...), custom_call_target="tpu_custom_call" | custom-call | tf_op jit(solution)/shard_map/start/pallas_call | solution.py:558
  1.5 0.5 %collective-permute-start.2 = (f32[136,128]{1,0:T(8,128)S(1)}, f32[136,128]{1,0:T(8,128)S(1)}, u32[]{:S(2)}, u32[]{:S(2)}) collective-permute-start(f32[136,128]{1,0:T(8,128)S(1)} %get-tuple-element.27), channel_id=1, source_target_pairs={{0,8},{8,0},{16,24},{24,16},{1,9},{9,1},{17,25},{25,17},{2,10},{10... | collective-permute-start | bytes 208904 | tf_op jit(solution)/shard_map/ppermute | solution.py:527
  2.0 2.6 %collective-permute-start = (f32[16,640]{1,0:T(8,128)S(1)}, f32[16,640]{1,0:T(8,128)S(1)}, u32[]{:S(2)}, u32[]{:S(2)}) collective-permute-start(f32[16,640]{1,0:T(8,128)S(1)} %get-tuple-element.25), channel_id=1, source_target_pairs={{0,1},{1,2},{2,3},{3,4},{4,5},{5,6},{6,7},{7,0},{8,9},{9,10},{10,1... | collective-permute-start | bytes 122888 | tf_op jit(solution)/shard_map/ppermute | solution.py:539
  4.6 1.3 %collective-permute-start.1 = (f32[280,128]{1,0:T(8,128)S(1)}, f32[280,128]{1,0:T(8,128)S(1)}, u32[]{:S(2)}, u32[]{:S(2)}) collective-permute-start(f32[280,128]{1,0:T(8,128)S(1)} %get-tuple-element.26), channel_id=1, source_target_pairs={{0,24},{8,16},{16,8},{24,0},{1,25},{9,17},{17,9},{25,1},{2,26},{10... | collective-permute-start | bytes 430088 | tf_op jit(solution)/shard_map/ppermute | solution.py:527
  5.9 0.0 collective-permute-done.2.from_near
  5.9 3.3 %collective-permute-start.3 = (f32[16,640]{1,0:T(8,128)S(1)}, f32[16,640]{1,0:T(8,128)S(1)}, u32[]{:S(2)}, u32[]{:S(2)}) collective-permute-start(f32[16,640]{1,0:T(8,128)S(1)} %get-tuple-element.29), channel_id=1, source_target_pairs={{0,7},{1,0},{2,1},{3,2},{4,3},{5,4},{6,5},{7,6},{8,15},{9,8},{10,9... | collective-permute-start | bytes 122888 | tf_op jit(solution)/shard_map/ppermute | solution.py:539
  9.2 0.7 %collective-permute-done.message.low = f32[16,640]{1,0:T(8,128)S(1)} collective-permute-done((f32[16,640]{1,0:T(8,128)S(1)}, f32[16,640]{1,0:T(8,128)S(1)}, u32[]{:S(2)}, u32[]{:S(2)}) %collective-permute-start) | collective-permute-done | bytes 40992 | tf_op jit(solution)/shard_map/ppermute | solution.py:539
  9.9 0.3 %weights.1.low_weights = f32[24,128]{1,0:T(8,128)S(1)} custom-call(f32[128,128]{1,0:T(8,128)S(1)} %get-tuple-element.22.columns.masses, f32[16,640]{1,0:T(8,128)S(1)} %collective-permute-done.message.low), custom_call_target="tpu_custom_call" | custom-call | flops 99999997952 | bytes 30000000 | tf_op jit(solution)/shard_map/weights/pallas_call | solution.py:558
  10.2 0.7 %collective-permute-done.3.high = f32[16,640]{1,0:T(8,128)S(1)} collective-permute-done((f32[16,640]{1,0:T(8,128)S(1)}, f32[16,640]{1,0:T(8,128)S(1)}, u32[]{:S(2)}, u32[]{:S(2)}) %collective-permute-start.3) | collective-permute-done | bytes 40992 | tf_op jit(solution)/shard_map/ppermute | solution.py:539
  10.9 0.0 collective-permute-done.1.from_far.refs_1_
  10.9 0.5 %second.1 = (f32[128,528]{1,0:T(8,128)S(1)}, f32[456,128]{1,0:T(8,128)S(1)}, f32[168,128]{1,0:T(8,128)S(1)}, f32[4,528]{1,0:T(4,128)S(1)}, f32[8,128]{1,0:T(8,128)S(1)}) custom-call(f32[128,528]{1,0:T(8,128)S(1)} %get-tuple-element.21.total, f32[128,128]{1,0:T(8,128)S(1)} %get-tuple-element.22.columns.masses, f32[128,128]{1,0:T(8,128)S(1)} %get-tuple-element.23.operator, ...), custom_call_target="tpu_custom_call" | custom-call | tf_op jit(solution)/shard_map/second/pallas_call | solution.py:558
  11.4 0.0 copy-start.1
  11.4 0.0 collective-permute-start.4
  11.4 1.3 %collective-permute-start.5 = (f32[168,128]{1,0:T(8,128)S(1)}, f32[168,128]{1,0:T(8,128)S(1)}, u32[]{:S(2)}, u32[]{:S(2)}) collective-permute-start(f32[168,128]{1,0:T(8,128)S(1)} %get-tuple-element.33.to_far), channel_id=1, source_target_pairs={{0,24},{8,16},{16,8},{24,0},{1,25},{9,17},{17,9},{25,1},{2,26},{10... | collective-permute-start | bytes 258056 | tf_op jit(solution)/shard_map/ppermute | solution.py:527
  12.7 0.0 copy-start
  12.7 0.9 %collective-permute-start.6 = (f32[4,528]{1,0:T(4,128)S(1)}, f32[4,528]{1,0:T(4,128)S(1)}, u32[]{:S(2)}, u32[]{:S(2)}) collective-permute-start(f32[4,528]{1,0:T(4,128)S(1)} %get-tuple-element.34), channel_id=1, source_target_pairs={{0,16},{8,24},{16,0},{24,8},{1,17},{9,25},{17,1},{25,9},{2,18},{10... | collective-permute-start | bytes 25352 | tf_op jit(solution)/shard_map/ppermute | solution.py:527
  13.6 0.0 copy-done.1
  13.6 0.0 collective-permute-done.4.refs_2_.from_near
  13.6 0.0 copy-done
  13.6 0.7 %factors.1 = f32[320,128]{1,0:T(8,128)S(1)} custom-call(s32[4,32]{1,0:T(4,128)S(1)} %copy-done, f32[144,128]{1,0:T(8,128)S(1)} %get-tuple-element.24.coefs.refs_0_, f32[280,128]{1,0:T(8,128)S(1)} %collective-permute-done.1.from_far.refs_1_, f32[456,128]{1,0:T(8,128)S(1)} %collective-permute-done.4.refs_2_.from_near), custom_call_target="tpu_custom_call" | custom-call | tf_op jit(solution)/shard_map/factors/pallas_call | solution.py:558
  14.3 2.3 %collective-permute-done.6.ends_near.ends_far = f32[4,528]{1,0:T(4,128)S(1)} collective-permute-done((f32[4,528]{1,0:T(4,128)S(1)}, f32[4,528]{1,0:T(4,128)S(1)}, u32[]{:S(2)}, u32[]{:S(2)}) %collective-permute-start.6) | collective-permute-done | bytes 8480 | tf_op jit(solution)/shard_map/ppermute | solution.py:527
  16.5 0.0 collective-permute-done.5.from_far
  16.5 1.6 %third.1 = f32[4,32,528]{2,1,0:T(8,128)} custom-call(f32[4,32,528]{2,1,0:T(8,128)S(1)} %get-tuple-element.20.state, f32[1,528]{1,0:T(1,128)S(1)} %reshape.3.hyper, f32[128,528]{1,0:T(8,128)S(1)} %get-tuple-element.30.total, f32[128,128]{1,0:T(8,128)S(1)} %get-tuple-element.22.columns.masses, f32[8,128]{1,0:T(8,128)S(1)} %get-tuple-element.31.inner, ...), custom_call_target="tpu_custom_call" | custom-call | tf_op jit(solution)/shard_map/third/pallas_call | solution.py:558
  (1 shorter events, 0.0 us)
Async XLA Ops:
  1.5 4.4 %collective-permute-start.2 = (f32[136,128]{1,0:T(8,128)S(1)}, f32[136,128]{1,0:T(8,128)S(1)}, u32[]{:S(2)}, u32[]{:S(2)}) collective-permute-start(f32[136,128]{1,0:T(8,128)S(1)} %get-tuple-element.27), channel_id=1, source_target_pairs={{0,8},{8,0},{16,24},{24,16},{1,9},{9,1},{17,25},{25,17},{2,10},{10... | collective-permute-start | bytes 208904 | tf_op jit(solution)/shard_map/ppermute | solution.py:527
  2.0 7.9 %collective-permute-start = (f32[16,640]{1,0:T(8,128)S(1)}, f32[16,640]{1,0:T(8,128)S(1)}, u32[]{:S(2)}, u32[]{:S(2)}) collective-permute-start(f32[16,640]{1,0:T(8,128)S(1)} %get-tuple-element.25), channel_id=1, source_target_pairs={{0,1},{1,2},{2,3},{3,4},{4,5},{5,6},{6,7},{7,0},{8,9},{9,10},{10,1... | collective-permute-start | bytes 122888 | tf_op jit(solution)/shard_map/ppermute | solution.py:539
  4.6 6.3 %collective-permute-start.1 = (f32[280,128]{1,0:T(8,128)S(1)}, f32[280,128]{1,0:T(8,128)S(1)}, u32[]{:S(2)}, u32[]{:S(2)}) collective-permute-start(f32[280,128]{1,0:T(8,128)S(1)} %get-tuple-element.26), channel_id=1, source_target_pairs={{0,24},{8,16},{16,8},{24,0},{1,25},{9,17},{17,9},{25,1},{2,26},{10... | collective-permute-start | bytes 430088 | tf_op jit(solution)/shard_map/ppermute | solution.py:527
  5.9 5.0 %collective-permute-start.3 = (f32[16,640]{1,0:T(8,128)S(1)}, f32[16,640]{1,0:T(8,128)S(1)}, u32[]{:S(2)}, u32[]{:S(2)}) collective-permute-start(f32[16,640]{1,0:T(8,128)S(1)} %get-tuple-element.29), channel_id=1, source_target_pairs={{0,7},{1,0},{2,1},{3,2},{4,3},{5,4},{6,5},{7,6},{8,15},{9,8},{10,9... | collective-permute-start | bytes 122888 | tf_op jit(solution)/shard_map/ppermute | solution.py:539
  11.4 2.2 %copy-start.1 = (f32[528]{0:T(1024)S(1)}, f32[528]{0:T(1024)}, u32[]{:S(2)}) copy-start(f32[528]{0:T(1024)} %param.9) | copy-start | bytes 6340
  11.4 2.2 %collective-permute-start.4 = (f32[456,128]{1,0:T(8,128)S(1)}, f32[456,128]{1,0:T(8,128)S(1)}, u32[]{:S(2)}, u32[]{:S(2)}) collective-permute-start(f32[456,128]{1,0:T(8,128)S(1)} %get-tuple-element.32.to_near), channel_id=1, source_target_pairs={{0,8},{8,0},{16,24},{24,16},{1,9},{9,1},{17,25},{25,17},{2,10},{10... | collective-permute-start | bytes 700424 | tf_op jit(solution)/shard_map/ppermute | solution.py:527
  11.4 5.1 %collective-permute-start.5 = (f32[168,128]{1,0:T(8,128)S(1)}, f32[168,128]{1,0:T(8,128)S(1)}, u32[]{:S(2)}, u32[]{:S(2)}) collective-permute-start(f32[168,128]{1,0:T(8,128)S(1)} %get-tuple-element.33.to_far), channel_id=1, source_target_pairs={{0,24},{8,16},{16,8},{24,0},{1,25},{9,17},{17,9},{25,1},{2,26},{10... | collective-permute-start | bytes 258056 | tf_op jit(solution)/shard_map/ppermute | solution.py:527
  12.7 0.9 %copy-start = (s32[4,32]{1,0:T(4,128)S(1)}, s32[4,32]{1,0:T(4,128)}, u32[]{:S(2)}) copy-start(s32[4,32]{1,0:T(4,128)} %slots.1) | copy-start | bytes 1540
  12.7 3.9 %collective-permute-start.6 = (f32[4,528]{1,0:T(4,128)S(1)}, f32[4,528]{1,0:T(4,128)S(1)}, u32[]{:S(2)}, u32[]{:S(2)}) collective-permute-start(f32[4,528]{1,0:T(4,128)S(1)} %get-tuple-element.34), channel_id=1, source_target_pairs={{0,16},{8,24},{16,0},{24,8},{1,17},{9,25},{17,1},{25,9},{2,18},{10... | collective-permute-start | bytes 25352 | tf_op jit(solution)/shard_map/ppermute | solution.py:527

commit v5 on v4

--- a/solution.py
+++ b/solution.py
@@ -95,33 +95,37 @@
     return tuple(pl.ds(pl.multiple_of(start, size_y), size_y) for start in starts)
 
 
-def add_packed(work, start, message, rows):
+def add_packed(work, start, message, rows, left_message=None):
     def write(first, count, lanes, value):
         work[pl.ds(pl.multiple_of(start + first, 8), count), lanes] += value
 
-    unpack(message, rows, work.shape[1], write)
+    unpack(message, rows, work.shape[1], write, left_message)
 
 
 def packed_rows(rows, width):
     return rows * (width // 128) + 8
 
 
-def pack(value, message):
+def pack(value, message, left_message=None):
     rows, width = value.shape
     full, left = width // 128, width % 128
     for i in range(full):
         message[i * rows : (i + 1) * rows, :] = value[:, i * 128 : (i + 1) * 128]
+    if left_message is None:
+        left_message = message.at[full * rows : full * rows + 8]
     for i in range(rows // 8):
         lanes = slice(i * left, (i + 1) * left)
-        message[full * rows : full * rows + 8, lanes] = value[i * 8 : (i + 1) * 8, full * 128 :]
-
-
-def unpack(message, rows, width, write):
+        left_message[:, lanes] = value[i * 8 : (i + 1) * 8, full * 128 :]
+
+
+def unpack(message, rows, width, write, left_message=None):
     full, left = width // 128, width % 128
     for i in range(full):
         write(0, rows, slice(i * 128, (i + 1) * 128), message[i * rows : (i + 1) * rows, :])
+    if left_message is None:
+        left_message = message.at[full * rows : full * rows + 8]
     for i in range(rows // 8):
-        value = message[full * rows : full * rows + 8, i * left : (i + 1) * left]
+        value = left_message[:, i * left : (i + 1) * left]
         write(i * 8, 8, slice(full * 128, width), value)
 
 
@@ -141,6 +145,7 @@
     here,
     total,
     x_near,
+    x_left,
     x_far,
     low,
     high,
@@ -179,7 +184,7 @@
         copy.wait()
     total[...] = product(split(matrix), split(here[...].reshape(count, width)))
     near, far = x_rows(count, size_y)
-    pack(total[near], x_near)
+    pack(total[near], x_near, x_left)
     pack(total[far], x_far)
     for first, message in ((0, low), (size_y - 4, high)):
         for i in range(4):
@@ -188,8 +193,9 @@
             message[rows, width : width + 2] = edge_rows(columns, first + i, size_x, size_y)[:, :2]
     for copy in copies[2 + size_x :]:
         copy.wait()
-    if x_far.shape[0] > x_near.shape[0]:
-        x_far[x_near.shape[0] :, :] = coefs[...]
+    used = x_near.shape[0] + 8
+    if x_far.shape[0] > used:
+        x_far[used:, :] = coefs[...]
 
 
 def node_column(values, start, count):
@@ -272,6 +278,7 @@
     low,
     from_far,
     from_near,
+    left_near,
     high,
     out,
     x_near,
@@ -287,7 +294,7 @@
     second = second_table()
     near, far = x_starts(size_x * size_y, size_y)
     work[...] = total[...]
-    add_packed(work, near, from_near, size_y)
+    add_packed(work, near, from_near, size_y, left_near)
     add_packed(work, far, from_far, size_y)
     sides = ((low, 0, 3, 0), (high, size_y - 1, 0, size_y - 8))
     beyond = []
@@ -362,7 +369,7 @@
     values,
     staged,
     sems,
-    *unpacked,
+    *beyond_rows,
 ):
     columns, width = total.shape
     size_x, size_y, _ = state.shape
@@ -370,28 +377,34 @@
     rows = size_y + 8
     last, lanes = rows * (width // 128), rows // 8 * (width % 128)
     messages = (to_near, to_far, from_near, from_far)
-    for message, target in zip(messages, unpacked):
-
-        def write(first, count, lanes, value, target=target):
-            target[first : first + count, lanes] = value
-
-        unpack(message, rows, width, write)
-    to_near, to_far, from_near, from_far = unpacked
+    for message, target in zip(messages, beyond_rows):
+        for i in range(width // 128):
+            target[:, i * 128 : (i + 1) * 128] = message[i * rows + size_y : (i + 1) * rows, :]
+        left = width % 128
+        lanes_before = size_y // 8 * left
+        target[:, width - left :] = message[last : last + 8, lanes_before : lanes_before + left]
+    at_near, at_far, over_near, over_far = beyond_rows
     near, far = x_starts(columns, size_y)
     sides = ((0, 0, 3, 0), (1, size_y - 1, 0, size_y - 8))
     partners = (
-        (near, to_near, from_near, from_far, ends_near, 0),
-        (far, to_far, from_far, from_near, ends_far, 1),
+        (near, at_near, over_near, over_far, ends_near),
+        (far, at_far, over_far, over_near, ends_far),
     )
     work[...] = total[...]
-    for start, _, theirs, _, _, _ in partners:
-        work[pl.ds(pl.multiple_of(start, size_y), size_y), :] += theirs[:size_y, :width]
+    for start, message in ((near, from_near), (far, from_far)):
+        for i in range(width // 128):
+            place = pl.ds(pl.multiple_of(start, size_y), size_y)
+            work[place, i * 128 : (i + 1) * 128] += message[i * rows : i * rows + size_y, :]
+        for i in range(size_y // 8):
+            place = pl.ds(pl.multiple_of(start + i * 8, 8), 8)
+            left = width % 128
+            work[place, width - left :] += message[last : last + 8, i * left : (i + 1) * left]
     for side, y, line, first in sides:
-        place = size_y + 4 * side
+        place = 4 * side
         weights = [
             message[last : last + 8, lanes + 8 * side : lanes + 8 * side + 5] for message in messages
         ]
-        for which, (start, mine, theirs, others, ends, _) in enumerate(partners):
+        for which, (start, mine, theirs, others, ends) in enumerate(partners):
             own, beyond = weights[which], weights[2 + which]
             terms = [
                 (weight[:, i : i + 1], values, place + i)
@@ -404,8 +417,8 @@
         for x in range(1, size_x - 1):
             row, weight = x * size_y + y, side * size_x + x
             work[row : row + 1, :] += (
-                inner[weight : weight + 1, 0:1] * from_near[place + line : place + line + 1, :width]
-                + inner[weight : weight + 1, 1:2] * from_far[place + line : place + line + 1, :width]
+                inner[weight : weight + 1, 0:1] * over_near[place + line : place + line + 1, :]
+                + inner[weight : weight + 1, 1:2] * over_far[place + line : place + line + 1, :]
             )
     twice = masses[:, 1:2] * work[...]
     turned[...] = (state[...].reshape(columns, width) - hyper[...] * twice).T
@@ -571,13 +584,14 @@
     edge = array(4 * size_x, padded)
     extra = 3 * levels if riding else 0
     first_rows, last_rows = packed_rows(size_y, width), packed_rows(size_y + 8, width)
-    here, total, x_near, x_far, y_low, y_high, operator, masses, coefs = call(
+    here, total, x_near, x_left, x_far, y_low, y_high, operator, masses, coefs = call(
         start_kernel,
         "start",
         [
             array(size_x, size_y, width),
             whole,
-            array(first_rows, 128),
+            array(first_rows - 8, 128),
+            array(8, 128),
             array(first_rows + extra, 128),
             edge,
             edge,
@@ -604,8 +618,9 @@
         spec=pl.BlockSpec(memory_space=pltpu.HBM),
     )
     low = shifted(y_high, "gy", 1)
+    left_near = swapped(x_left, "gx", lambda i: i ^ 1)
     from_far, from_near = exchanged(x_near, x_far, "gx")
-    y_low, _ = lax.optimization_barrier((y_low, from_near))
+    y_low, _ = lax.optimization_barrier((y_low, left_near))
     high = shifted(y_low, "gy", -1)
     (low_weights,) = call(
         functools.partial(weights_kernel, size_x, size_y, width),
@@ -635,6 +650,7 @@
         low,
         from_far,
         from_near,
+        left_near,
         high,
     )
     last_x = exchanged(x_near, x_far, "gx")
@@ -666,7 +682,7 @@
             scratch(size_x, size_y, width),
             pltpu.SemaphoreType.DMA((-(-width // 128),)),
         ]
-        + [scratch(size_y + 8, width)] * 4,
+        + [scratch(8, width)] * 4,
         here,
         hyper,
         total,

time: 18.3 us -> 18.5 us (1.011)
    ppermute x2, starting transfers between devices: 5.9 us -> 6.22 us  [shifted(): lax.ppermute(value, axis, [(i, (i + step) % size) for i in range(size)])]
    ppermute x5 -> x6, starting transfers between devices: 3.95 us -> 3.78 us  [swapped(): lax.ppermute(value, axis, [(i, partner(i)) for i in range(lax.axis_size(a...]
    ppermute x5 -> x6, waiting for transfers between devices: 2.29 us -> 2.34 us  [swapped(): lax.ppermute(value, axis, [(i, partner(i)) for i in range(lax.axis_size(a...]
  transfers between devices with their start and end apart: 7 -> 8, of which waited for: 3 -> 3; matrix products, arithmetic and copies ran while one was open for 0% -> 0% of each run, Pallas kernels for 5% -> 5%
where the time goes in v5:
time: 18.5 us; the launch traced here: 18.3 us
  starting transfers between devices  10 us (54%)
  Pallas kernels  4.52 us (24%)
  waiting for transfers between devices  3.73 us (20%)
    ppermute x2, starting transfers between devices, shifted(): lax.ppermute(value, axis, [(i, (i + step) % size) for i in range(size)])  6.22 us
    pallas_call x5, Pallas kernels, call(): pl.pallas_call(kernel, out_shape=outs, in_specs=[spec] * len(operands), o...  4.52 us
    ppermute x6, starting transfers between devices, swapped(): lax.ppermute(value, axis, [(i, partner(i)) for i in range(lax.axis_size(a...  3.78 us
    ppermute x6, waiting for transfers between devices, swapped(): lax.ppermute(value, axis, [(i, partner(i)) for i in range(lax.axis_size(a...  2.34 us
    ppermute x2, waiting for transfers between devices, shifted(): lax.ppermute(value, axis, [(i, (i + step) % size) for i in range(size)])  1.39 us
  transfers between devices with their start and end apart: 8, of which 3 were waited for; matrix products, arithmetic and copies ran while one was open for 0% of the time, Pallas kernels for 5%

profile of v5, /device:TPU:0, one launch (start us, length us, event | category | flops | bytes accessed | tf_op | source)
XLA Modules:
  0.0 18.3 jit_solution(1785420371015146984)
XLA Ops:
  0.0 1.5 %start.1 = (f32[4,32,528]{2,1,0:T(8,128)S(1)}, f32[128,528]{1,0:T(8,128)S(1)}, f32[128,128]{1,0:T(8,128)S(1)}, f32[8,128]{1,0:T(8,128)S(1)}, f32[280,128]{1,0:T(...) custom-call(f32[4,32,528]{2,1,0:T(8,128)} %state.1, ...), custom_call_target="tpu_custom_call" | custom-call | tf_op jit(solution)/shard_map/start/pallas_call | solution.py:571
  1.5 3.0 %collective-permute-start = (f32[16,640]{1,0:T(8,128)S(1)}, f32[16,640]{1,0:T(8,128)S(1)}, u32[]{:S(2)}, u32[]{:S(2)}) collective-permute-start(f32[16,640]{1,0:T(8,128)S(1)} %get-tuple-element.26), channel_id=1, source_target_pairs={{0,1},{1,2},{2,3},{3,4},{4,5},{5,6},{6,7},{7,0},{8,9},{9,10},{10,1... | collective-permute-start | bytes 122888 | tf_op jit(solution)/shard_map/ppermute | solution.py:552
  4.5 0.0 collective-permute-start.3
  4.5 0.5 %collective-permute-start.2 = (f32[128,128]{1,0:T(8,128)S(1)}, f32[128,128]{1,0:T(8,128)S(1)}, u32[]{:S(2)}, u32[]{:S(2)}) collective-permute-start(f32[128,128]{1,0:T(8,128)S(1)} %get-tuple-element.28), channel_id=1, source_target_pairs={{0,8},{8,0},{16,24},{24,16},{1,9},{9,1},{17,25},{25,17},{2,10},{10... | collective-permute-start | bytes 196616 | tf_op jit(solution)/shard_map/ppermute | solution.py:540
  5.0 1.1 %collective-permute-start.1 = (f32[280,128]{1,0:T(8,128)S(1)}, f32[280,128]{1,0:T(8,128)S(1)}, u32[]{:S(2)}, u32[]{:S(2)}) collective-permute-start(f32[280,128]{1,0:T(8,128)S(1)} %get-tuple-element.27), channel_id=1, source_target_pairs={{0,24},{8,16},{16,8},{24,0},{1,25},{9,17},{17,9},{25,1},{2,26},{10... | collective-permute-start | bytes 430088 | tf_op jit(solution)/shard_map/ppermute | solution.py:540
  6.1 0.0 collective-permute-done.3.left_near
  6.1 3.2 %collective-permute-start.4 = (f32[16,640]{1,0:T(8,128)S(1)}, f32[16,640]{1,0:T(8,128)S(1)}, u32[]{:S(2)}, u32[]{:S(2)}) collective-permute-start(f32[16,640]{1,0:T(8,128)S(1)} %get-tuple-element.31), channel_id=1, source_target_pairs={{0,7},{1,0},{2,1},{3,2},{4,3},{5,4},{6,5},{7,6},{8,15},{9,8},{10,9... | collective-permute-start | bytes 122888 | tf_op jit(solution)/shard_map/ppermute | solution.py:552
  9.3 0.2 %collective-permute-done.message.low = f32[16,640]{1,0:T(8,128)S(1)} collective-permute-done((f32[16,640]{1,0:T(8,128)S(1)}, f32[16,640]{1,0:T(8,128)S(1)}, u32[]{:S(2)}, u32[]{:S(2)}) %collective-permute-start) | collective-permute-done | bytes 40992 | tf_op jit(solution)/shard_map/ppermute | solution.py:552
  9.6 0.3 %weights.1.low_weights = f32[24,128]{1,0:T(8,128)S(1)} custom-call(f32[128,128]{1,0:T(8,128)S(1)} %get-tuple-element.23.columns.masses, f32[16,640]{1,0:T(8,128)S(1)} %collective-permute-done.message.low), custom_call_target="tpu_custom_call" | custom-call | flops 99999997952 | bytes 30000000 | tf_op jit(solution)/shard_map/weights/pallas_call | solution.py:571
  9.9 1.2 %collective-permute-done.4.high = f32[16,640]{1,0:T(8,128)S(1)} collective-permute-done((f32[16,640]{1,0:T(8,128)S(1)}, f32[16,640]{1,0:T(8,128)S(1)}, u32[]{:S(2)}, u32[]{:S(2)}) %collective-permute-start.4) | collective-permute-done | bytes 40992 | tf_op jit(solution)/shard_map/ppermute | solution.py:552
  11.0 0.0 collective-permute-done.2.from_near
  11.0 0.0 collective-permute-done.1.from_far.refs_1_
  11.0 0.5 %second.1 = (f32[128,528]{1,0:T(8,128)S(1)}, f32[456,128]{1,0:T(8,128)S(1)}, f32[168,128]{1,0:T(8,128)S(1)}, f32[4,528]{1,0:T(4,128)S(1)}, f32[8,128]{1,0:T(8,128)S(1)}) custom-call(f32[128,528]{1,0:T(8,128)S(1)} %get-tuple-element.22.total, f32[128,128]{1,0:T(8,128)S(1)} %get-tuple-element.23.columns.masses, f32[128,128]{1,0:T(8,128)S(1)} %get-tuple-element.24.operator, ...), custom_call_target="tpu_custom_call" | custom-call | tf_op jit(solution)/shard_map/second/pallas_call | solution.py:571
  11.5 0.0 copy-start.1
  11.5 0.0 collective-permute-start.5
  11.6 1.5 %collective-permute-start.6 = (f32[168,128]{1,0:T(8,128)S(1)}, f32[168,128]{1,0:T(8,128)S(1)}, u32[]{:S(2)}, u32[]{:S(2)}) collective-permute-start(f32[168,128]{1,0:T(8,128)S(1)} %get-tuple-element.35.to_far), channel_id=1, source_target_pairs={{0,24},{8,16},{16,8},{24,0},{1,25},{9,17},{17,9},{25,1},{2,26},{10... | collective-permute-start | bytes 258056 | tf_op jit(solution)/shard_map/ppermute | solution.py:540
  13.1 0.0 copy-start
  13.1 0.6 %collective-permute-start.7 = (f32[4,528]{1,0:T(4,128)S(1)}, f32[4,528]{1,0:T(4,128)S(1)}, u32[]{:S(2)}, u32[]{:S(2)}) collective-permute-start(f32[4,528]{1,0:T(4,128)S(1)} %get-tuple-element.36), channel_id=1, source_target_pairs={{0,16},{8,24},{16,0},{24,8},{1,17},{9,25},{17,1},{25,9},{2,18},{10... | collective-permute-start | bytes 25352 | tf_op jit(solution)/shard_map/ppermute | solution.py:540
  13.7 0.0 copy-done.1
  13.7 0.0 collective-permute-done.5.refs_2_.from_near
  13.7 0.0 copy-done
  13.8 0.7 %factors.1 = f32[320,128]{1,0:T(8,128)S(1)} custom-call(s32[4,32]{1,0:T(4,128)S(1)} %copy-done, f32[144,128]{1,0:T(8,128)S(1)} %get-tuple-element.25.coefs.refs_0_, f32[280,128]{1,0:T(8,128)S(1)} %collective-permute-done.1.from_far.refs_1_, f32[456,128]{1,0:T(8,128)S(1)} %collective-permute-done.5.refs_2_.from_near), custom_call_target="tpu_custom_call" | custom-call | tf_op jit(solution)/shard_map/factors/pallas_call | solution.py:571
  14.4 2.3 %collective-permute-done.7.ends_near.ends_far = f32[4,528]{1,0:T(4,128)S(1)} collective-permute-done((f32[4,528]{1,0:T(4,128)S(1)}, f32[4,528]{1,0:T(4,128)S(1)}, u32[]{:S(2)}, u32[]{:S(2)}) %collective-permute-start.7) | collective-permute-done | bytes 8480 | tf_op jit(solution)/shard_map/ppermute | solution.py:540
  16.8 0.0 collective-permute-done.6.from_far
  16.8 1.6 %third.1 = f32[4,32,528]{2,1,0:T(8,128)} custom-call(f32[4,32,528]{2,1,0:T(8,128)S(1)} %get-tuple-element.21.state, f32[1,528]{1,0:T(1,128)S(1)} %reshape.3.hyper, f32[128,528]{1,0:T(8,128)S(1)} %get-tuple-element.32.total, f32[128,128]{1,0:T(8,128)S(1)} %get-tuple-element.23.columns.masses, f32[8,128]{1,0:T(8,128)S(1)} %get-tuple-element.33.inner, ...), custom_call_target="tpu_custom_call" | custom-call | tf_op jit(solution)/shard_map/third/pallas_call | solution.py:571
  (1 shorter events, 0.0 us)
Async XLA Ops:
  1.5 8.1 %collective-permute-start = (f32[16,640]{1,0:T(8,128)S(1)}, f32[16,640]{1,0:T(8,128)S(1)}, u32[]{:S(2)}, u32[]{:S(2)}) collective-permute-start(f32[16,640]{1,0:T(8,128)S(1)} %get-tuple-element.26), channel_id=1, source_target_pairs={{0,1},{1,2},{2,3},{3,4},{4,5},{5,6},{6,7},{7,0},{8,9},{9,10},{10,1... | collective-permute-start | bytes 122888 | tf_op jit(solution)/shard_map/ppermute | solution.py:552
  4.5 1.6 %collective-permute-start.3 = (f32[8,128]{1,0:T(8,128)S(1)}, f32[8,128]{1,0:T(8,128)S(1)}, u32[]{:S(2)}, u32[]{:S(2)}) collective-permute-start(f32[8,128]{1,0:T(8,128)S(1)} %get-tuple-element.29), channel_id=1, source_target_pairs={{0,8},{8,0},{16,24},{24,16},{1,9},{9,1},{17,25},{25,17},{2,10},{10... | collective-permute-start | bytes 12296 | tf_op jit(solution)/shard_map/ppermute | solution.py:540
  4.5 6.5 %collective-permute-start.2 = (f32[128,128]{1,0:T(8,128)S(1)}, f32[128,128]{1,0:T(8,128)S(1)}, u32[]{:S(2)}, u32[]{:S(2)}) collective-permute-start(f32[128,128]{1,0:T(8,128)S(1)} %get-tuple-element.28), channel_id=1, source_target_pairs={{0,8},{8,0},{16,24},{24,16},{1,9},{9,1},{17,25},{25,17},{2,10},{10... | collective-permute-start | bytes 196616 | tf_op jit(solution)/shard_map/ppermute | solution.py:540
  5.0 6.0 %collective-permute-start.1 = (f32[280,128]{1,0:T(8,128)S(1)}, f32[280,128]{1,0:T(8,128)S(1)}, u32[]{:S(2)}, u32[]{:S(2)}) collective-permute-start(f32[280,128]{1,0:T(8,128)S(1)} %get-tuple-element.27), channel_id=1, source_target_pairs={{0,24},{8,16},{16,8},{24,0},{1,25},{9,17},{17,9},{25,1},{2,26},{10... | collective-permute-start | bytes 430088 | tf_op jit(solution)/shard_map/ppermute | solution.py:540
  6.1 4.9 %collective-permute-start.4 = (f32[16,640]{1,0:T(8,128)S(1)}, f32[16,640]{1,0:T(8,128)S(1)}, u32[]{:S(2)}, u32[]{:S(2)}) collective-permute-start(f32[16,640]{1,0:T(8,128)S(1)} %get-tuple-element.31), channel_id=1, source_target_pairs={{0,7},{1,0},{2,1},{3,2},{4,3},{5,4},{6,5},{7,6},{8,15},{9,8},{10,9... | collective-permute-start | bytes 122888 | tf_op jit(solution)/shard_map/ppermute | solution.py:552
  11.5 2.2 %copy-start.1 = (f32[528]{0:T(1024)S(1)}, f32[528]{0:T(1024)}, u32[]{:S(2)}) copy-start(f32[528]{0:T(1024)} %param.9) | copy-start | bytes 6340
  11.5 2.2 %collective-permute-start.5 = (f32[456,128]{1,0:T(8,128)S(1)}, f32[456,128]{1,0:T(8,128)S(1)}, u32[]{:S(2)}, u32[]{:S(2)}) collective-permute-start(f32[456,128]{1,0:T(8,128)S(1)} %get-tuple-element.34.to_near), channel_id=1, source_target_pairs={{0,8},{8,0},{16,24},{24,16},{1,9},{9,1},{17,25},{25,17},{2,10},{10... | collective-permute-start | bytes 700424 | tf_op jit(solution)/shard_map/ppermute | solution.py:540
  11.6 5.2 %collective-permute-start.6 = (f32[168,128]{1,0:T(8,128)S(1)}, f32[168,128]{1,0:T(8,128)S(1)}, u32[]{:S(2)}, u32[]{:S(2)}) collective-permute-start(f32[168,128]{1,0:T(8,128)S(1)} %get-tuple-element.35.to_far), channel_id=1, source_target_pairs={{0,24},{8,16},{16,8},{24,0},{1,25},{9,17},{17,9},{25,1},{2,26},{10... | collective-permute-start | bytes 258056 | tf_op jit(solution)/shard_map/ppermute | solution.py:540
  13.1 0.7 %copy-start = (s32[4,32]{1,0:T(4,128)S(1)}, s32[4,32]{1,0:T(4,128)}, u32[]{:S(2)}) copy-start(s32[4,32]{1,0:T(4,128)} %slots.1) | copy-start | bytes 1540
  13.1 3.7 %collective-permute-start.7 = (f32[4,528]{1,0:T(4,128)S(1)}, f32[4,528]{1,0:T(4,128)S(1)}, u32[]{:S(2)}, u32[]{:S(2)}) collective-permute-start(f32[4,528]{1,0:T(4,128)S(1)} %get-tuple-element.36), channel_id=1, source_target_pairs={{0,16},{8,24},{16,0},{24,8},{1,17},{9,25},{17,1},{25,9},{2,18},{10... | collective-permute-start | bytes 25352 | tf_op jit(solution)/shard_map/ppermute | solution.py:540

commit v6 on v5

--- a/solution.py
+++ b/solution.py
@@ -421,13 +421,16 @@
                 + inner[weight : weight + 1, 1:2] * over_far[place + line : place + line + 1, :]
             )
     twice = masses[:, 1:2] * work[...]
-    turned[...] = (state[...].reshape(columns, width) - hyper[...] * twice).T
+    dynamic = (state[...].reshape(columns, width) - hyper[...] * twice).T
+    pitch = levels + 1
+    for i in range(variables):
+        turned[i * pitch : i * pitch + levels, :] = dynamic[i * levels : (i + 1) * levels]
     scale, carry, gain, keep, flow, cloud = (
         factors.at[i * levels : (i + 1) * levels] for i in range(6)
     )
 
     def level(k):
-        return pl.ds(k, variables, stride=levels)
+        return pl.ds(k, variables, stride=pitch)
 
     half = levels // 2
     known = [jnp.zeros((variables, columns), jnp.float32)] * 2
@@ -447,7 +450,13 @@
 
     def leave(i):
         lanes = slice(i * 128, min((i + 1) * 128, width))
-        staged[:, :, lanes] = turned[lanes, :].T.reshape(size_x, size_y, -1)
+        parts = []
+        for j in range(variables):
+            first, last = max(lanes.start, j * levels), min(lanes.stop, (j + 1) * levels)
+            if first < last:
+                parts.append(turned[first + j : last + j, :])
+        rows = jnp.concatenate(parts, axis=0)
+        staged[:, :, lanes] = rows.T.reshape(size_x, size_y, -1)
         copy = pltpu.make_async_copy(staged.at[:, :, lanes], out.at[:, :, lanes], sems.at[i])
         copy.start()
         return copy
@@ -455,7 +464,7 @@
     tiles = -(-width // 128)
     settled_tiles = -(-3 * levels // 128)
     copies = [leave(i) for i in range(settled_tiles, tiles)]
-    heat, vapour, liquid = (turned.at[i * levels : (i + 1) * levels] for i in range(3))
+    heat, vapour, liquid = (turned.at[i * pitch : i * pitch + levels] for i in range(3))
     condensed = cloud[...] * 0.5 * jnp.maximum(vapour[...] - 0.3 * heat[...], 0.0)
     vapour[...] = vapour[...] - condensed
     heat[...] = heat[...] + 2.0 * condensed
@@ -677,7 +686,7 @@
         [array(size_x, size_y, width)],
         [
             scratch(columns, width),
-            scratch(width, columns),
+            scratch(width // levels * (levels + 1), columns),
             scratch(levels, 16, columns),
             scratch(size_x, size_y, width),
             pltpu.SemaphoreType.DMA((-(-width // 128),)),

time: 18.5 us -> 18.4 us (level)
  no operation moved by 1% of the time
where the time goes in v6:
time: 18.4 us; the launch traced here: 18.3 us
  starting transfers between devices  10 us (54%)
  Pallas kernels  4.44 us (24%)
  waiting for transfers between devices  3.73 us (20%)
    ppermute x2, starting transfers between devices, shifted(): lax.ppermute(value, axis, [(i, (i + step) % size) for i in range(size)])  6.22 us
    pallas_call x5, Pallas kernels, call(): pl.pallas_call(kernel, out_shape=outs, in_specs=[spec] * len(operands), o...  4.44 us
    ppermute x6, starting transfers between devices, swapped(): lax.ppermute(value, axis, [(i, partner(i)) for i in range(lax.axis_size(a...  3.78 us
    ppermute x6, waiting for transfers between devices, swapped(): lax.ppermute(value, axis, [(i, partner(i)) for i in range(lax.axis_size(a...  2.34 us
    ppermute x2, waiting for transfers between devices, shifted(): lax.ppermute(value, axis, [(i, (i + step) % size) for i in range(size)])  1.39 us
  transfers between devices with their start and end apart: 8, of which 3 were waited for; matrix products, arithmetic and copies ran while one was open for 0% of the time, Pallas kernels for 5%

profile of v6, /device:TPU:0, one launch (start us, length us, event | category | flops | bytes accessed | tf_op | source)
XLA Modules:
  0.0 18.3 jit_solution(16662185918581079615)
XLA Ops:
  0.0 1.5 %start.1 = (f32[4,32,528]{2,1,0:T(8,128)S(1)}, f32[128,528]{1,0:T(8,128)S(1)}, f32[128,128]{1,0:T(8,128)S(1)}, f32[8,128]{1,0:T(8,128)S(1)}, f32[280,128]{1,0:T(...) custom-call(f32[4,32,528]{2,1,0:T(8,128)} %state.1, ...), custom_call_target="tpu_custom_call" | custom-call | tf_op jit(solution)/shard_map/start/pallas_call | solution.py:580
  1.5 3.0 %collective-permute-start = (f32[16,640]{1,0:T(8,128)S(1)}, f32[16,640]{1,0:T(8,128)S(1)}, u32[]{:S(2)}, u32[]{:S(2)}) collective-permute-start(f32[16,640]{1,0:T(8,128)S(1)} %get-tuple-element.26), channel_id=1, source_target_pairs={{0,1},{1,2},{2,3},{3,4},{4,5},{5,6},{6,7},{7,0},{8,9},{9,10},{10,1... | collective-permute-start | bytes 122888 | tf_op jit(solution)/shard_map/ppermute | solution.py:561
  4.5 0.0 collective-permute-start.3
  4.5 0.5 %collective-permute-start.2 = (f32[128,128]{1,0:T(8,128)S(1)}, f32[128,128]{1,0:T(8,128)S(1)}, u32[]{:S(2)}, u32[]{:S(2)}) collective-permute-start(f32[128,128]{1,0:T(8,128)S(1)} %get-tuple-element.28), channel_id=1, source_target_pairs={{0,8},{8,0},{16,24},{24,16},{1,9},{9,1},{17,25},{25,17},{2,10},{10... | collective-permute-start | bytes 196616 | tf_op jit(solution)/shard_map/ppermute | solution.py:549
  5.0 1.1 %collective-permute-start.1 = (f32[280,128]{1,0:T(8,128)S(1)}, f32[280,128]{1,0:T(8,128)S(1)}, u32[]{:S(2)}, u32[]{:S(2)}) collective-permute-start(f32[280,128]{1,0:T(8,128)S(1)} %get-tuple-element.27), channel_id=1, source_target_pairs={{0,24},{8,16},{16,8},{24,0},{1,25},{9,17},{17,9},{25,1},{2,26},{10... | collective-permute-start | bytes 430088 | tf_op jit(solution)/shard_map/ppermute | solution.py:549
  6.1 0.0 collective-permute-done.3.left_near
  6.1 3.2 %collective-permute-start.4 = (f32[16,640]{1,0:T(8,128)S(1)}, f32[16,640]{1,0:T(8,128)S(1)}, u32[]{:S(2)}, u32[]{:S(2)}) collective-permute-start(f32[16,640]{1,0:T(8,128)S(1)} %get-tuple-element.31), channel_id=1, source_target_pairs={{0,7},{1,0},{2,1},{3,2},{4,3},{5,4},{6,5},{7,6},{8,15},{9,8},{10,9... | collective-permute-start | bytes 122888 | tf_op jit(solution)/shard_map/ppermute | solution.py:561
  9.3 0.2 %collective-permute-done.message.low = f32[16,640]{1,0:T(8,128)S(1)} collective-permute-done((f32[16,640]{1,0:T(8,128)S(1)}, f32[16,640]{1,0:T(8,128)S(1)}, u32[]{:S(2)}, u32[]{:S(2)}) %collective-permute-start) | collective-permute-done | bytes 40992 | tf_op jit(solution)/shard_map/ppermute | solution.py:561
  9.6 0.3 %weights.1.low_weights = f32[24,128]{1,0:T(8,128)S(1)} custom-call(f32[128,128]{1,0:T(8,128)S(1)} %get-tuple-element.23.columns.masses, f32[16,640]{1,0:T(8,128)S(1)} %collective-permute-done.message.low), custom_call_target="tpu_custom_call" | custom-call | flops 99999997952 | bytes 30000000 | tf_op jit(solution)/shard_map/weights/pallas_call | solution.py:580
  9.9 1.2 %collective-permute-done.4.high = f32[16,640]{1,0:T(8,128)S(1)} collective-permute-done((f32[16,640]{1,0:T(8,128)S(1)}, f32[16,640]{1,0:T(8,128)S(1)}, u32[]{:S(2)}, u32[]{:S(2)}) %collective-permute-start.4) | collective-permute-done | bytes 40992 | tf_op jit(solution)/shard_map/ppermute | solution.py:561
  11.0 0.0 collective-permute-done.2.from_near
  11.0 0.0 collective-permute-done.1.from_far.refs_1_
  11.0 0.5 %second.1 = (f32[128,528]{1,0:T(8,128)S(1)}, f32[456,128]{1,0:T(8,128)S(1)}, f32[168,128]{1,0:T(8,128)S(1)}, f32[4,528]{1,0:T(4,128)S(1)}, f32[8,128]{1,0:T(8,128)S(1)}) custom-call(f32[128,528]{1,0:T(8,128)S(1)} %get-tuple-element.22.total, f32[128,128]{1,0:T(8,128)S(1)} %get-tuple-element.23.columns.masses, f32[128,128]{1,0:T(8,128)S(1)} %get-tuple-element.24.operator, ...), custom_call_target="tpu_custom_call" | custom-call | tf_op jit(solution)/shard_map/second/pallas_call | solution.py:580
  11.5 0.0 copy-start.1
  11.5 0.0 collective-permute-start.5
  11.6 1.5 %collective-permute-start.6 = (f32[168,128]{1,0:T(8,128)S(1)}, f32[168,128]{1,0:T(8,128)S(1)}, u32[]{:S(2)}, u32[]{:S(2)}) collective-permute-start(f32[168,128]{1,0:T(8,128)S(1)} %get-tuple-element.35.to_far), channel_id=1, source_target_pairs={{0,24},{8,16},{16,8},{24,0},{1,25},{9,17},{17,9},{25,1},{2,26},{10... | collective-permute-start | bytes 258056 | tf_op jit(solution)/shard_map/ppermute | solution.py:549
  13.1 0.0 copy-start
  13.1 0.6 %collective-permute-start.7 = (f32[4,528]{1,0:T(4,128)S(1)}, f32[4,528]{1,0:T(4,128)S(1)}, u32[]{:S(2)}, u32[]{:S(2)}) collective-permute-start(f32[4,528]{1,0:T(4,128)S(1)} %get-tuple-element.36), channel_id=1, source_target_pairs={{0,16},{8,24},{16,0},{24,8},{1,17},{9,25},{17,1},{25,9},{2,18},{10... | collective-permute-start | bytes 25352 | tf_op jit(solution)/shard_map/ppermute | solution.py:549
  13.7 0.0 copy-done.1
  13.7 0.0 collective-permute-done.5.refs_2_.from_near
  13.7 0.0 copy-done
  13.8 0.7 %factors.1 = f32[320,128]{1,0:T(8,128)S(1)} custom-call(s32[4,32]{1,0:T(4,128)S(1)} %copy-done, f32[144,128]{1,0:T(8,128)S(1)} %get-tuple-element.25.coefs.refs_0_, f32[280,128]{1,0:T(8,128)S(1)} %collective-permute-done.1.from_far.refs_1_, f32[456,128]{1,0:T(8,128)S(1)} %collective-permute-done.5.refs_2_.from_near), custom_call_target="tpu_custom_call" | custom-call | tf_op jit(solution)/shard_map/factors/pallas_call | solution.py:580
  14.4 2.3 %collective-permute-done.7.ends_near.ends_far = f32[4,528]{1,0:T(4,128)S(1)} collective-permute-done((f32[4,528]{1,0:T(4,128)S(1)}, f32[4,528]{1,0:T(4,128)S(1)}, u32[]{:S(2)}, u32[]{:S(2)}) %collective-permute-start.7) | collective-permute-done | bytes 8480 | tf_op jit(solution)/shard_map/ppermute | solution.py:549
  16.8 0.0 collective-permute-done.6.from_far
  16.8 1.5 %third.1 = f32[4,32,528]{2,1,0:T(8,128)} custom-call(f32[4,32,528]{2,1,0:T(8,128)S(1)} %get-tuple-element.21.state, f32[1,528]{1,0:T(1,128)S(1)} %reshape.3.hyper, f32[128,528]{1,0:T(8,128)S(1)} %get-tuple-element.32.total, f32[128,128]{1,0:T(8,128)S(1)} %get-tuple-element.23.columns.masses, f32[8,128]{1,0:T(8,128)S(1)} %get-tuple-element.33.inner, ...), custom_call_target="tpu_custom_call" | custom-call | tf_op jit(solution)/shard_map/third/pallas_call | solution.py:580
  (1 shorter events, 0.0 us)
Async XLA Ops:
  1.5 8.1 %collective-permute-start = (f32[16,640]{1,0:T(8,128)S(1)}, f32[16,640]{1,0:T(8,128)S(1)}, u32[]{:S(2)}, u32[]{:S(2)}) collective-permute-start(f32[16,640]{1,0:T(8,128)S(1)} %get-tuple-element.26), channel_id=1, source_target_pairs={{0,1},{1,2},{2,3},{3,4},{4,5},{5,6},{6,7},{7,0},{8,9},{9,10},{10,1... | collective-permute-start | bytes 122888 | tf_op jit(solution)/shard_map/ppermute | solution.py:561
  4.5 1.6 %collective-permute-start.3 = (f32[8,128]{1,0:T(8,128)S(1)}, f32[8,128]{1,0:T(8,128)S(1)}, u32[]{:S(2)}, u32[]{:S(2)}) collective-permute-start(f32[8,128]{1,0:T(8,128)S(1)} %get-tuple-element.29), channel_id=1, source_target_pairs={{0,8},{8,0},{16,24},{24,16},{1,9},{9,1},{17,25},{25,17},{2,10},{10... | collective-permute-start | bytes 12296 | tf_op jit(solution)/shard_map/ppermute | solution.py:549
  4.5 6.5 %collective-permute-start.2 = (f32[128,128]{1,0:T(8,128)S(1)}, f32[128,128]{1,0:T(8,128)S(1)}, u32[]{:S(2)}, u32[]{:S(2)}) collective-permute-start(f32[128,128]{1,0:T(8,128)S(1)} %get-tuple-element.28), channel_id=1, source_target_pairs={{0,8},{8,0},{16,24},{24,16},{1,9},{9,1},{17,25},{25,17},{2,10},{10... | collective-permute-start | bytes 196616 | tf_op jit(solution)/shard_map/ppermute | solution.py:549
  5.0 6.0 %collective-permute-start.1 = (f32[280,128]{1,0:T(8,128)S(1)}, f32[280,128]{1,0:T(8,128)S(1)}, u32[]{:S(2)}, u32[]{:S(2)}) collective-permute-start(f32[280,128]{1,0:T(8,128)S(1)} %get-tuple-element.27), channel_id=1, source_target_pairs={{0,24},{8,16},{16,8},{24,0},{1,25},{9,17},{17,9},{25,1},{2,26},{10... | collective-permute-start | bytes 430088 | tf_op jit(solution)/shard_map/ppermute | solution.py:549
  6.1 4.9 %collective-permute-start.4 = (f32[16,640]{1,0:T(8,128)S(1)}, f32[16,640]{1,0:T(8,128)S(1)}, u32[]{:S(2)}, u32[]{:S(2)}) collective-permute-start(f32[16,640]{1,0:T(8,128)S(1)} %get-tuple-element.31), channel_id=1, source_target_pairs={{0,7},{1,0},{2,1},{3,2},{4,3},{5,4},{6,5},{7,6},{8,15},{9,8},{10,9... | collective-permute-start | bytes 122888 | tf_op jit(solution)/shard_map/ppermute | solution.py:561
  11.5 2.2 %copy-start.1 = (f32[528]{0:T(1024)S(1)}, f32[528]{0:T(1024)}, u32[]{:S(2)}) copy-start(f32[528]{0:T(1024)} %param.9) | copy-start | bytes 6340
  11.5 2.2 %collective-permute-start.5 = (f32[456,128]{1,0:T(8,128)S(1)}, f32[456,128]{1,0:T(8,128)S(1)}, u32[]{:S(2)}, u32[]{:S(2)}) collective-permute-start(f32[456,128]{1,0:T(8,128)S(1)} %get-tuple-element.34.to_near), channel_id=1, source_target_pairs={{0,8},{8,0},{16,24},{24,16},{1,9},{9,1},{17,25},{25,17},{2,10},{10... | collective-permute-start | bytes 700424 | tf_op jit(solution)/shard_map/ppermute | solution.py:549
  11.6 5.2 %collective-permute-start.6 = (f32[168,128]{1,0:T(8,128)S(1)}, f32[168,128]{1,0:T(8,128)S(1)}, u32[]{:S(2)}, u32[]{:S(2)}) collective-permute-start(f32[168,128]{1,0:T(8,128)S(1)} %get-tuple-element.35.to_far), channel_id=1, source_target_pairs={{0,24},{8,16},{16,8},{24,0},{1,25},{9,17},{17,9},{25,1},{2,26},{10... | collective-permute-start | bytes 258056 | tf_op jit(solution)/shard_map/ppermute | solution.py:549
  13.1 0.7 %copy-start = (s32[4,32]{1,0:T(4,128)S(1)}, s32[4,32]{1,0:T(4,128)}, u32[]{:S(2)}) copy-start(s32[4,32]{1,0:T(4,128)} %slots.1) | copy-start | bytes 1540
  13.1 3.7 %collective-permute-start.7 = (f32[4,528]{1,0:T(4,128)S(1)}, f32[4,528]{1,0:T(4,128)S(1)}, u32[]{:S(2)}, u32[]{:S(2)}) collective-permute-start(f32[4,528]{1,0:T(4,128)S(1)} %get-tuple-element.36), channel_id=1, source_target_pairs={{0,16},{8,24},{16,0},{24,8},{1,17},{9,25},{17,1},{25,9},{2,18},{10... | collective-permute-start | bytes 25352 | tf_op jit(solution)/shard_map/ppermute | solution.py:549

commit v7 on v5

--- a/solution.py
+++ b/solution.py
@@ -351,9 +351,8 @@
 
 def third_kernel(
     levels,
-    state,
     hyper,
-    total,
+    base,
     masses,
     inner,
     factors,
@@ -366,13 +365,15 @@
     out,
     work,
     turned,
+    turned_rest,
     values,
+    values_rest,
     staged,
     sems,
     *beyond_rows,
 ):
-    columns, width = total.shape
-    size_x, size_y, _ = state.shape
+    columns, width = base.shape
+    size_x, size_y, _ = out.shape
     variables = width // levels
     rows = size_y + 8
     last, lanes = rows * (width // 128), rows // 8 * (width % 128)
@@ -390,15 +391,17 @@
         (near, at_near, over_near, over_far, ends_near),
         (far, at_far, over_far, over_near, ends_far),
     )
-    work[...] = total[...]
+    for x in range(1, size_x - 1):
+        for first in (0, size_y - 8):
+            work[x * size_y + first : x * size_y + first + 8, :] = jnp.zeros((8, width), jnp.float32)
     for start, message in ((near, from_near), (far, from_far)):
         for i in range(width // 128):
             place = pl.ds(pl.multiple_of(start, size_y), size_y)
-            work[place, i * 128 : (i + 1) * 128] += message[i * rows : i * rows + size_y, :]
+            work[place, i * 128 : (i + 1) * 128] = message[i * rows : i * rows + size_y, :]
         for i in range(size_y // 8):
             place = pl.ds(pl.multiple_of(start + i * 8, 8), 8)
             left = width % 128
-            work[place, width - left :] += message[last : last + 8, i * left : (i + 1) * left]
+            work[place, width - left :] = message[last : last + 8, i * left : (i + 1) * left]
     for side, y, line, first in sides:
         place = 4 * side
         weights = [
@@ -420,42 +423,77 @@
                 inner[weight : weight + 1, 0:1] * over_near[place + line : place + line + 1, :]
                 + inner[weight : weight + 1, 1:2] * over_far[place + line : place + line + 1, :]
             )
-    twice = masses[:, 1:2] * work[...]
-    turned[...] = (state[...].reshape(columns, width) - hyper[...] * twice).T
+    for start in (near, far):
+        place = pl.ds(pl.multiple_of(start, size_y), size_y)
+        work[place, :] = base[place, :] - hyper[...] * (masses[place, 1:2] * work[place, :])
+    for x in range(1, size_x - 1):
+        for first in (0, size_y - 8):
+            rows = slice(x * size_y + first, x * size_y + first + 8)
+            work[rows, :] = base[rows, :] - hyper[...] * (masses[rows, 1:2] * work[rows, :])
+        rows = slice(x * size_y + 8, (x + 1) * size_y - 8)
+        work[rows, :] = base[rows, :]
+    pitch, half = levels + 1, levels // 2
     scale, carry, gain, keep, flow, cloud = (
         factors.at[i * levels : (i + 1) * levels] for i in range(6)
     )
-
-    def level(k):
-        return pl.ds(k, variables, stride=levels)
-
-    half = levels // 2
-    known = [jnp.zeros((variables, columns), jnp.float32)] * 2
-    for i in range(half):
-        for side, k in enumerate((i, levels - 1 - i)):
-            scaled = turned[level(k), :] * scale[k : k + 1, :]
-            known[side] = scaled + carry[k : k + 1, :] * known[side]
-            values[k, :variables, :] = known[side]
-    meet = factors[6 * levels + half : 6 * levels + half + 1, :]
-    first = (known[0] + gain[half - 1 : half, :] * known[1]) * meet
-    solved = [first, known[1] + gain[half : half + 1, :] * first]
-    for i in reversed(range(half)):
-        for side, k in enumerate((i, levels - 1 - i)):
-            if i < half - 1:
-                solved[side] = values[k, :variables, :] + gain[k : k + 1, :] * solved[side]
-            turned[level(k), :] = solved[side]
+    groups = [(first, min(8, variables - first)) for first in range(0, variables, 8)]
+    buffers = list(zip(groups, (turned, turned_rest), (values, values_rest)))
+
+    def turn(group, turned):
+        first, count = group
+        start, stop = first * levels, (first + count) * levels
+        tile = start // 128 * 128
+        rows = work[:, tile:stop].T
+        for i in range(count):
+            row = start - tile + i * levels
+            turned[i * pitch : i * pitch + levels, :] = rows[row : row + levels]
+
+    def forward(group, turned, values):
+        count = group[1]
+        known = [jnp.zeros((count, columns), jnp.float32)] * 2
+        for i in range(half):
+            for side, k in enumerate((i, levels - 1 - i)):
+                scaled = turned[pl.ds(k, count, stride=pitch), :] * scale[k : k + 1, :]
+                known[side] = scaled + carry[k : k + 1, :] * known[side]
+                values[k, :count, :] = known[side]
+        return known
+
+    def back(group, turned, values, known):
+        count = group[1]
+        meet = factors[6 * levels + half : 6 * levels + half + 1, :]
+        first = (known[0] + gain[half - 1 : half, :] * known[1]) * meet
+        solved = [first, known[1] + gain[half : half + 1, :] * first]
+        for i in reversed(range(half)):
+            for side, k in enumerate((i, levels - 1 - i)):
+                if i < half - 1:
+                    solved[side] = values[k, :count, :] + gain[k : k + 1, :] * solved[side]
+                turned[pl.ds(k, count, stride=pitch), :] = solved[side]
 
     def leave(i):
         lanes = slice(i * 128, min((i + 1) * 128, width))
-        staged[:, :, lanes] = turned[lanes, :].T.reshape(size_x, size_y, -1)
+        parts = []
+        for (start, count), source, _ in buffers:
+            for j in range(start, start + count):
+                first, last = max(lanes.start, j * levels), min(lanes.stop, (j + 1) * levels)
+                if first < last:
+                    offset = (j - start) * pitch - j * levels
+                    parts.append(source[first + offset : last + offset, :])
+        rows = jnp.concatenate(parts, axis=0)
+        staged[:, :, lanes] = rows.T.reshape(size_x, size_y, -1)
         copy = pltpu.make_async_copy(staged.at[:, :, lanes], out.at[:, :, lanes], sems.at[i])
         copy.start()
         return copy
 
+    (main, main_turned, main_values), (rest, rest_turned, rest_values) = buffers
+    turn(main, main_turned)
+    main_known = forward(main, main_turned, main_values)
+    turn(rest, rest_turned)
+    rest_known = forward(rest, rest_turned, rest_values)
+    back(main, main_turned, main_values, main_known)
     tiles = -(-width // 128)
-    settled_tiles = -(-3 * levels // 128)
-    copies = [leave(i) for i in range(settled_tiles, tiles)]
-    heat, vapour, liquid = (turned.at[i * levels : (i + 1) * levels] for i in range(3))
+    settled_tiles, main_tiles = -(-3 * levels // 128), main[1] * levels // 128
+    copies = [leave(i) for i in range(settled_tiles, main_tiles)]
+    heat, vapour, liquid = (turned.at[i * pitch : i * pitch + levels] for i in range(3))
     condensed = cloud[...] * 0.5 * jnp.maximum(vapour[...] - 0.3 * heat[...], 0.0)
     vapour[...] = vapour[...] - condensed
     heat[...] = heat[...] + 2.0 * condensed
@@ -467,9 +505,17 @@
             liquid[k : k + 1, :] = settled[side]
     through = factors[6 * levels : 6 * levels + half, :]
     liquid[half:, :] = liquid[half:, :] + through * settled[0]
+    back(rest, rest_turned, rest_values, rest_known)
     copies += [leave(i) for i in range(settled_tiles)]
+    copies += [leave(i) for i in range(main_tiles, tiles)]
     for copy in copies:
         copy.wait()
+
+
+def base_kernel(state, hyper, total, masses, base):
+    columns, width = total.shape
+    twice = masses[:, 1:2] * total[...]
+    base[...] = state[...].reshape(columns, width) - hyper[...] * twice
 
 
 def pick(slots, pieces):
@@ -671,21 +717,23 @@
         span_slot,
         *pieces,
     )
+    (base,) = call(base_kernel, "base", [whole], [], here, hyper, total, masses)
     (result,) = call(
         functools.partial(third_kernel, levels),
         "third",
         [array(size_x, size_y, width)],
         [
             scratch(columns, width),
-            scratch(width, columns),
-            scratch(levels, 16, columns),
+            scratch(8 * (levels + 1), columns),
+            scratch((width // levels - 8) * (levels + 1), columns),
+            scratch(levels, 8, columns),
+            scratch(levels, 8, columns),
             scratch(size_x, size_y, width),
             pltpu.SemaphoreType.DMA((-(-width // 128),)),
         ]
         + [scratch(8, width)] * 4,
-        here,
         hyper,
-        total,
+        base,
         masses,
         inner,
         factors,

time: 18.5 us -> 18.3 us (0.989)
  waiting for transfers between devices: 3.73 us -> 3.02 us
  local copies, waits for them, and re-layouts: 0.05 us -> 0.56 us
    ppermute x6, waiting for transfers between devices: 2.34 us -> 1.63 us  [swapped(): lax.ppermute(value, axis, [(i, partner(i)) for i in range(lax.axis_size(a...]
    unnamed x4, local copies, waits for them, and re-layouts: 0.04 us -> 0.56 us
    pallas_call x5 -> x6, Pallas kernels: 4.52 us -> 4.46 us  [call(): pl.pallas_call(kernel, out_shape=outs, in_specs=[spec] * len(operands), o...]
  transfers between devices with their start and end apart: 8 -> 8, of which waited for: 3 -> 3; matrix products, arithmetic and copies ran while one was open for 0% -> 0% of each run, Pallas kernels for 5% -> 6%
where the time goes in v7:
time: 18.3 us; the launch traced here: 18.1 us
  starting transfers between devices  10 us (55%)
  Pallas kernels  4.46 us (24%)
  waiting for transfers between devices  3.02 us (17%)
  local copies, waits for them, and re-layouts  0.56 us (3%)
    ppermute x2, starting transfers between devices, shifted(): lax.ppermute(value, axis, [(i, (i + step) % size) for i in range(size)])  6.22 us
    pallas_call x6, Pallas kernels, call(): pl.pallas_call(kernel, out_shape=outs, in_specs=[spec] * len(operands), o...  4.46 us
    ppermute x6, starting transfers between devices, swapped(): lax.ppermute(value, axis, [(i, partner(i)) for i in range(lax.axis_size(a...  3.79 us
    ppermute x6, waiting for transfers between devices, swapped(): lax.ppermute(value, axis, [(i, partner(i)) for i in range(lax.axis_size(a...  1.63 us
    ppermute x2, waiting for transfers between devices, shifted(): lax.ppermute(value, axis, [(i, (i + step) % size) for i in range(size)])  1.39 us
    unnamed x4, local copies, waits for them, and re-layouts  0.56 us
  transfers between devices with their start and end apart: 8, of which 3 were waited for; matrix products, arithmetic and copies ran while one was open for 0% of the time, Pallas kernels for 6%

profile of v7, /device:TPU:0, one launch (start us, length us, event | category | flops | bytes accessed | tf_op | source)
XLA Modules:
  0.0 18.1 jit_solution(2980772890114815839)
XLA Ops:
  0.0 1.5 %start.1 = (f32[4,32,528]{2,1,0:T(8,128)S(1)}, f32[128,528]{1,0:T(8,128)S(1)}, f32[128,128]{1,0:T(8,128)S(1)}, f32[8,128]{1,0:T(8,128)S(1)}, f32[280,128]{1,0:T(...) custom-call(f32[4,32,528]{2,1,0:T(8,128)} %state.1, ...), custom_call_target="tpu_custom_call" | custom-call | tf_op jit(solution)/shard_map/start/pallas_call | solution.py:617
  1.5 3.0 %collective-permute-start = (f32[16,640]{1,0:T(8,128)S(1)}, f32[16,640]{1,0:T(8,128)S(1)}, u32[]{:S(2)}, u32[]{:S(2)}) collective-permute-start(f32[16,640]{1,0:T(8,128)S(1)} %get-tuple-element.26), channel_id=1, source_target_pairs={{0,1},{1,2},{2,3},{3,4},{4,5},{5,6},{6,7},{7,0},{8,9},{9,10},{10,1... | collective-permute-start | bytes 122888 | tf_op jit(solution)/shard_map/ppermute | solution.py:598
  4.5 0.0 collective-permute-start.3
  4.5 1.6 %collective-permute-start.1 = (f32[280,128]{1,0:T(8,128)S(1)}, f32[280,128]{1,0:T(8,128)S(1)}, u32[]{:S(2)}, u32[]{:S(2)}) collective-permute-start(f32[280,128]{1,0:T(8,128)S(1)} %get-tuple-element.27), channel_id=1, source_target_pairs={{0,24},{8,16},{16,8},{24,0},{1,25},{9,17},{17,9},{25,1},{2,26},{10... | collective-permute-start | bytes 430088 | tf_op jit(solution)/shard_map/ppermute | solution.py:586
  6.1 0.0 collective-permute-start.2
  6.1 0.0 collective-permute-done.3.left_near
  6.1 3.2 %collective-permute-start.4 = (f32[16,640]{1,0:T(8,128)S(1)}, f32[16,640]{1,0:T(8,128)S(1)}, u32[]{:S(2)}, u32[]{:S(2)}) collective-permute-start(f32[16,640]{1,0:T(8,128)S(1)} %get-tuple-element.31), channel_id=1, source_target_pairs={{0,7},{1,0},{2,1},{3,2},{4,3},{5,4},{6,5},{7,6},{8,15},{9,8},{10,9... | collective-permute-start | bytes 122888 | tf_op jit(solution)/shard_map/ppermute | solution.py:598
  9.3 0.2 %collective-permute-done.message.low = f32[16,640]{1,0:T(8,128)S(1)} collective-permute-done((f32[16,640]{1,0:T(8,128)S(1)}, f32[16,640]{1,0:T(8,128)S(1)}, u32[]{:S(2)}, u32[]{:S(2)}) %collective-permute-start) | collective-permute-done | bytes 40992 | tf_op jit(solution)/shard_map/ppermute | solution.py:598
  9.6 0.3 %weights.1.low_weights = f32[24,128]{1,0:T(8,128)S(1)} custom-call(f32[128,128]{1,0:T(8,128)S(1)} %get-tuple-element.23.columns.masses, f32[16,640]{1,0:T(8,128)S(1)} %collective-permute-done.message.low), custom_call_target="tpu_custom_call" | custom-call | flops 99999997952 | bytes 30000000 | tf_op jit(solution)/shard_map/weights/pallas_call | solution.py:617
  9.9 1.2 %collective-permute-done.4.high = f32[16,640]{1,0:T(8,128)S(1)} collective-permute-done((f32[16,640]{1,0:T(8,128)S(1)}, f32[16,640]{1,0:T(8,128)S(1)}, u32[]{:S(2)}, u32[]{:S(2)}) %collective-permute-start.4) | collective-permute-done | bytes 40992 | tf_op jit(solution)/shard_map/ppermute | solution.py:598
  11.0 0.0 collective-permute-done.2.from_near
  11.0 0.0 collective-permute-done.1.from_far.refs_1_
  11.0 0.5 %second.1 = (f32[128,528]{1,0:T(8,128)S(1)}, f32[456,128]{1,0:T(8,128)S(1)}, f32[168,128]{1,0:T(8,128)S(1)}, f32[4,528]{1,0:T(4,128)S(1)}, f32[8,128]{1,0:T(8,128)S(1)}) custom-call(f32[128,528]{1,0:T(8,128)S(1)} %get-tuple-element.22.total, f32[128,128]{1,0:T(8,128)S(1)} %get-tuple-element.23.columns.masses, f32[128,128]{1,0:T(8,128)S(1)} %get-tuple-element.24.operator, ...), custom_call_target="tpu_custom_call" | custom-call | tf_op jit(solution)/shard_map/second/pallas_call | solution.py:617
  11.5 0.0 copy-start.1
  11.5 0.0 collective-permute-start.5
  11.6 1.2 %collective-permute-start.6 = (f32[168,128]{1,0:T(8,128)S(1)}, f32[168,128]{1,0:T(8,128)S(1)}, u32[]{:S(2)}, u32[]{:S(2)}) collective-permute-start(f32[168,128]{1,0:T(8,128)S(1)} %get-tuple-element.35.to_far), channel_id=1, source_target_pairs={{0,24},{8,16},{16,8},{24,0},{1,25},{9,17},{17,9},{25,1},{2,26},{10... | collective-permute-start | bytes 258056 | tf_op jit(solution)/shard_map/ppermute | solution.py:586
  12.7 1.0 %collective-permute-start.7 = (f32[4,528]{1,0:T(4,128)S(1)}, f32[4,528]{1,0:T(4,128)S(1)}, u32[]{:S(2)}, u32[]{:S(2)}) collective-permute-start(f32[4,528]{1,0:T(4,128)S(1)} %get-tuple-element.36), channel_id=1, source_target_pairs={{0,16},{8,24},{16,0},{24,8},{1,17},{9,25},{17,1},{25,9},{2,18},{10... | collective-permute-start | bytes 25352 | tf_op jit(solution)/shard_map/ppermute | solution.py:586
  13.7 0.0 copy-done.1
  13.7 0.0 copy-start
  13.7 0.1 base.1
  13.9 0.0 collective-permute-done.5.refs_2_.from_near
  13.9 0.6 %copy-done = s32[4,32]{1,0:T(4,128)S(1)} copy-done((s32[4,32]{1,0:T(4,128)S(1)}, s32[4,32]{1,0:T(4,128)}, u32[]{:S(2)}) %copy-start) | copy-done | bytes 536
  14.4 0.7 %factors.1 = f32[320,128]{1,0:T(8,128)S(1)} custom-call(s32[4,32]{1,0:T(4,128)S(1)} %copy-done, f32[144,128]{1,0:T(8,128)S(1)} %get-tuple-element.25.coefs.refs_0_, f32[280,128]{1,0:T(8,128)S(1)} %collective-permute-done.1.from_far.refs_1_, f32[456,128]{1,0:T(8,128)S(1)} %collective-permute-done.5.refs_2_.from_near), custom_call_target="tpu_custom_call" | custom-call | tf_op jit(solution)/shard_map/factors/pallas_call | solution.py:617
  15.1 1.6 %collective-permute-done.7.ends_near.ends_far = f32[4,528]{1,0:T(4,128)S(1)} collective-permute-done((f32[4,528]{1,0:T(4,128)S(1)}, f32[4,528]{1,0:T(4,128)S(1)}, u32[]{:S(2)}, u32[]{:S(2)}) %collective-permute-start.7) | collective-permute-done | bytes 8480 | tf_op jit(solution)/shard_map/ppermute | solution.py:586
  16.7 0.0 collective-permute-done.6.from_far
  16.7 1.4 %third.1 = f32[4,32,528]{2,1,0:T(8,128)} custom-call(f32[1,528]{1,0:T(1,128)S(1)} %reshape.3.hyper, f32[128,528]{1,0:T(8,128)S(1)} %base.1, f32[128,128]{1,0:T(8,128)S(1)} %get-tuple-element.23.columns.masses, f32[8,128]{1,0:T(8,128)S(1)} %get-tuple-element.33.inner, f32[320,128]{1,0:T(8,128)S(1)} %factors.1, f32[456,128]{1,0:T(8,128)S(1)} %get-tuple-element.34.to_near, ...), custom_call_target="tpu_custom_call" | custom-call | tf_op jit(solution)/shard_map/third/pallas_call | solution.py:617
  (1 shorter events, 0.0 us)
Async XLA Ops:
  1.5 8.1 %collective-permute-start = (f32[16,640]{1,0:T(8,128)S(1)}, f32[16,640]{1,0:T(8,128)S(1)}, u32[]{:S(2)}, u32[]{:S(2)}) collective-permute-start(f32[16,640]{1,0:T(8,128)S(1)} %get-tuple-element.26), channel_id=1, source_target_pairs={{0,1},{1,2},{2,3},{3,4},{4,5},{5,6},{6,7},{7,0},{8,9},{9,10},{10,1... | collective-permute-start | bytes 122888 | tf_op jit(solution)/shard_map/ppermute | solution.py:598
  4.5 1.6 %collective-permute-start.3 = (f32[8,128]{1,0:T(8,128)S(1)}, f32[8,128]{1,0:T(8,128)S(1)}, u32[]{:S(2)}, u32[]{:S(2)}) collective-permute-start(f32[8,128]{1,0:T(8,128)S(1)} %get-tuple-element.29), channel_id=1, source_target_pairs={{0,8},{8,0},{16,24},{24,16},{1,9},{9,1},{17,25},{25,17},{2,10},{10... | collective-permute-start | bytes 12296 | tf_op jit(solution)/shard_map/ppermute | solution.py:586
  4.5 6.5 %collective-permute-start.1 = (f32[280,128]{1,0:T(8,128)S(1)}, f32[280,128]{1,0:T(8,128)S(1)}, u32[]{:S(2)}, u32[]{:S(2)}) collective-permute-start(f32[280,128]{1,0:T(8,128)S(1)} %get-tuple-element.27), channel_id=1, source_target_pairs={{0,24},{8,16},{16,8},{24,0},{1,25},{9,17},{17,9},{25,1},{2,26},{10... | collective-permute-start | bytes 430088 | tf_op jit(solution)/shard_map/ppermute | solution.py:586
  6.1 4.9 %collective-permute-start.2 = (f32[128,128]{1,0:T(8,128)S(1)}, f32[128,128]{1,0:T(8,128)S(1)}, u32[]{:S(2)}, u32[]{:S(2)}) collective-permute-start(f32[128,128]{1,0:T(8,128)S(1)} %get-tuple-element.28), channel_id=1, source_target_pairs={{0,8},{8,0},{16,24},{24,16},{1,9},{9,1},{17,25},{25,17},{2,10},{10... | collective-permute-start | bytes 196616 | tf_op jit(solution)/shard_map/ppermute | solution.py:586
  6.1 4.9 %collective-permute-start.4 = (f32[16,640]{1,0:T(8,128)S(1)}, f32[16,640]{1,0:T(8,128)S(1)}, u32[]{:S(2)}, u32[]{:S(2)}) collective-permute-start(f32[16,640]{1,0:T(8,128)S(1)} %get-tuple-element.31), channel_id=1, source_target_pairs={{0,7},{1,0},{2,1},{3,2},{4,3},{5,4},{6,5},{7,6},{8,15},{9,8},{10,9... | collective-permute-start | bytes 122888 | tf_op jit(solution)/shard_map/ppermute | solution.py:598
  11.5 2.2 %copy-start.1 = (f32[528]{0:T(1024)S(1)}, f32[528]{0:T(1024)}, u32[]{:S(2)}) copy-start(f32[528]{0:T(1024)} %param.9) | copy-start | bytes 6340
  11.5 2.3 %collective-permute-start.5 = (f32[456,128]{1,0:T(8,128)S(1)}, f32[456,128]{1,0:T(8,128)S(1)}, u32[]{:S(2)}, u32[]{:S(2)}) collective-permute-start(f32[456,128]{1,0:T(8,128)S(1)} %get-tuple-element.34.to_near), channel_id=1, source_target_pairs={{0,8},{8,0},{16,24},{24,16},{1,9},{9,1},{17,25},{25,17},{2,10},{10... | collective-permute-start | bytes 700424 | tf_op jit(solution)/shard_map/ppermute | solution.py:586
  11.6 5.1 %collective-permute-start.6 = (f32[168,128]{1,0:T(8,128)S(1)}, f32[168,128]{1,0:T(8,128)S(1)}, u32[]{:S(2)}, u32[]{:S(2)}) collective-permute-start(f32[168,128]{1,0:T(8,128)S(1)} %get-tuple-element.35.to_far), channel_id=1, source_target_pairs={{0,24},{8,16},{16,8},{24,0},{1,25},{9,17},{17,9},{25,1},{2,26},{10... | collective-permute-start | bytes 258056 | tf_op jit(solution)/shard_map/ppermute | solution.py:586
  12.7 4.0 %collective-permute-start.7 = (f32[4,528]{1,0:T(4,128)S(1)}, f32[4,528]{1,0:T(4,128)S(1)}, u32[]{:S(2)}, u32[]{:S(2)}) collective-permute-start(f32[4,528]{1,0:T(4,128)S(1)} %get-tuple-element.36), channel_id=1, source_target_pairs={{0,16},{8,24},{16,0},{24,8},{1,17},{9,25},{17,1},{25,9},{2,18},{10... | collective-permute-start | bytes 25352 | tf_op jit(solution)/shard_map/ppermute | solution.py:586
  13.7 0.7 %copy-start = (s32[4,32]{1,0:T(4,128)S(1)}, s32[4,32]{1,0:T(4,128)}, u32[]{:S(2)}) copy-start(s32[4,32]{1,0:T(4,128)} %slots.1) | copy-start | bytes 1540

commit v8 on v7

--- a/solution.py
+++ b/solution.py
@@ -95,37 +95,33 @@
     return tuple(pl.ds(pl.multiple_of(start, size_y), size_y) for start in starts)
 
 
-def add_packed(work, start, message, rows, left_message=None):
+def add_packed(work, start, message, rows):
     def write(first, count, lanes, value):
         work[pl.ds(pl.multiple_of(start + first, 8), count), lanes] += value
 
-    unpack(message, rows, work.shape[1], write, left_message)
+    unpack(message, rows, work.shape[1], write)
 
 
 def packed_rows(rows, width):
     return rows * (width // 128) + 8
 
 
-def pack(value, message, left_message=None):
+def pack(value, message):
     rows, width = value.shape
     full, left = width // 128, width % 128
     for i in range(full):
         message[i * rows : (i + 1) * rows, :] = value[:, i * 128 : (i + 1) * 128]
-    if left_message is None:
-        left_message = message.at[full * rows : full * rows + 8]
     for i in range(rows // 8):
         lanes = slice(i * left, (i + 1) * left)
-        left_message[:, lanes] = value[i * 8 : (i + 1) * 8, full * 128 :]
-
-
-def unpack(message, rows, width, write, left_message=None):
+        message[full * rows : full * rows + 8, lanes] = value[i * 8 : (i + 1) * 8, full * 128 :]
+
+
+def unpack(message, rows, width, write):
     full, left = width // 128, width % 128
     for i in range(full):
         write(0, rows, slice(i * 128, (i + 1) * 128), message[i * rows : (i + 1) * rows, :])
-    if left_message is None:
-        left_message = message.at[full * rows : full * rows + 8]
     for i in range(rows // 8):
-        value = left_message[:, i * left : (i + 1) * left]
+        value = message[full * rows : full * rows + 8, i * left : (i + 1) * left]
         write(i * 8, 8, slice(full * 128, width), value)
 
 
@@ -145,7 +141,6 @@
     here,
     total,
     x_near,
-    x_left,
     x_far,
     low,
     high,
@@ -184,7 +179,7 @@
         copy.wait()
     total[...] = product(split(matrix), split(here[...].reshape(count, width)))
     near, far = x_rows(count, size_y)
-    pack(total[near], x_near, x_left)
+    pack(total[near], x_near)
     pack(total[far], x_far)
     for first, message in ((0, low), (size_y - 4, high)):
         for i in range(4):
@@ -193,9 +188,8 @@
             message[rows, width : width + 2] = edge_rows(columns, first + i, size_x, size_y)[:, :2]
     for copy in copies[2 + size_x :]:
         copy.wait()
-    used = x_near.shape[0] + 8
-    if x_far.shape[0] > used:
-        x_far[used:, :] = coefs[...]
+    if x_far.shape[0] > x_near.shape[0]:
+        x_far[x_near.shape[0] :, :] = coefs[...]
 
 
 def node_column(values, start, count):
@@ -278,7 +272,6 @@
     low,
     from_far,
     from_near,
-    left_near,
     high,
     out,
     x_near,
@@ -294,7 +287,7 @@
     second = second_table()
     near, far = x_starts(size_x * size_y, size_y)
     work[...] = total[...]
-    add_packed(work, near, from_near, size_y, left_near)
+    add_packed(work, near, from_near, size_y)
     add_packed(work, far, from_far, size_y)
     sides = ((low, 0, 3, 0), (high, size_y - 1, 0, size_y - 8))
     beyond = []
@@ -536,17 +529,13 @@
 
 def factor_kernel(levels, slots, *refs):
     factors = refs[-1]
-    if len(refs) == 4:
-        own, from_far, from_near = refs[:3]
+    if len(refs) == 3:
         here = lax.axis_index("gx")
-        count = own.shape[0]
-        far, near = from_far.shape[0] - count, from_near.shape[0] - 2 * count
-        pieces = [
-            (here, own[...]),
-            (here ^ 3, from_far[far:, :]),
-            (here ^ 1, from_near[near : near + count, :]),
-            (here ^ 2, from_near[near + count :, :]),
-        ]
+        pieces = []
+        for message, owner in zip(refs, (here, here ^ 1)):
+            start = message.shape[0] - 6 * levels
+            pieces.append((owner, message[start : start + 3 * levels, :]))
+            pieces.append((owner ^ 3, message[start + 3 * levels :, :]))
     else:
         pieces = [(peer, refs[0][peer]) for peer in range(refs[0].shape[0])]
     columns = factors.shape[1]
@@ -630,14 +619,13 @@
     edge = array(4 * size_x, padded)
     extra = 3 * levels if riding else 0
     first_rows, last_rows = packed_rows(size_y, width), packed_rows(size_y + 8, width)
-    here, total, x_near, x_left, x_far, y_low, y_high, operator, masses, coefs = call(
+    here, total, x_near, x_far, y_low, y_high, operator, masses, coefs = call(
         start_kernel,
         "start",
         [
             array(size_x, size_y, width),
             whole,
-            array(first_rows - 8, 128),
-            array(8, 128),
+            array(first_rows, 128),
             array(first_rows + extra, 128),
             edge,
             edge,
@@ -664,9 +652,7 @@
         spec=pl.BlockSpec(memory_space=pltpu.HBM),
     )
     low = shifted(y_high, "gy", 1)
-    left_near = swapped(x_left, "gx", lambda i: i ^ 1)
     from_far, from_near = exchanged(x_near, x_far, "gx")
-    y_low, _ = lax.optimization_barrier((y_low, left_near))
     high = shifted(y_low, "gy", -1)
     (low_weights,) = call(
         functools.partial(weights_kernel, size_x, size_y, width),
@@ -696,7 +682,6 @@
         low,
         from_far,
         from_near,
-        left_near,
         high,
     )
     last_x = exchanged(x_near, x_far, "gx")
@@ -706,7 +691,7 @@
     if peers != 4:
         ends_far = swapped(line_ends, "gx", lambda i: (i - (2 if i % 2 else -2)) % peers)
     if riding:
-        pieces = [coefs, from_far, last_x[1]]
+        pieces = [x_near, last_x[1]]
     else:
         pieces = [lax.all_gather(coefs, "gx")]
     (factors,) = call(

time: 18.3 us -> 18.3 us (level)
    ppermute x6 -> x5, starting transfers between devices: 3.79 us -> 3.78 us  [swapped(): lax.ppermute(value, axis, [(i, partner(i)) for i in range(lax.axis_size(a...]
    ppermute x6 -> x5, waiting for transfers between devices: 1.63 us -> 1.63 us  [swapped(): lax.ppermute(value, axis, [(i, partner(i)) for i in range(lax.axis_size(a...]
  transfers between devices with their start and end apart: 8 -> 7, of which waited for: 3 -> 3; matrix products, arithmetic and copies ran while one was open for 0% -> 0% of each run, Pallas kernels for 6% -> 6%
where the time goes in v8:
time: 18.3 us; the launch traced here: 18.1 us
  starting transfers between devices  10 us (55%)
  Pallas kernels  4.46 us (24%)
  waiting for transfers between devices  3.02 us (17%)
  local copies, waits for them, and re-layouts  0.56 us (3%)
    ppermute x2, starting transfers between devices, shifted(): lax.ppermute(value, axis, [(i, (i + step) % size) for i in range(size)])  6.22 us
    pallas_call x6, Pallas kernels, call(): pl.pallas_call(kernel, out_shape=outs, in_specs=[spec] * len(operands), o...  4.46 us
    ppermute x5, starting transfers between devices, swapped(): lax.ppermute(value, axis, [(i, partner(i)) for i in range(lax.axis_size(a...  3.78 us
    ppermute x5, waiting for transfers between devices, swapped(): lax.ppermute(value, axis, [(i, partner(i)) for i in range(lax.axis_size(a...  1.63 us
    ppermute x2, waiting for transfers between devices, shifted(): lax.ppermute(value, axis, [(i, (i + step) % size) for i in range(size)])  1.39 us
    unnamed x4, local copies, waits for them, and re-layouts  0.55 us
  transfers between devices with their start and end apart: 7, of which 3 were waited for; matrix products, arithmetic and copies ran while one was open for 0% of the time, Pallas kernels for 6%

profile of v8, /device:TPU:0, one launch (start us, length us, event | category | flops | bytes accessed | tf_op | source)
XLA Modules:
  0.0 18.1 jit_solution(17539471488650992579)
XLA Ops:
  0.0 1.5 %start.1 = (f32[4,32,528]{2,1,0:T(8,128)S(1)}, f32[128,528]{1,0:T(8,128)S(1)}, f32[136,128]{1,0:T(8,128)S(1)}, f32[280,128]{1,0:T(8,128)S(1)}, f32[16,640]{1,0:T...) custom-call(f32[4,32,528]{2,1,0:T(8,128)} %state.1, ...), custom_call_target="tpu_custom_call" | custom-call | tf_op jit(solution)/shard_map/start/pallas_call | solution.py:606
  1.5 3.0 %collective-permute-start = (f32[16,640]{1,0:T(8,128)S(1)}, f32[16,640]{1,0:T(8,128)S(1)}, u32[]{:S(2)}, u32[]{:S(2)}) collective-permute-start(f32[16,640]{1,0:T(8,128)S(1)} %get-tuple-element.24), channel_id=1, source_target_pairs={{0,1},{1,2},{2,3},{3,4},{4,5},{5,6},{6,7},{7,0},{8,9},{9,10},{10,1... | collective-permute-start | bytes 122888 | tf_op jit(solution)/shard_map/ppermute | solution.py:587
  4.5 0.6 %collective-permute-start.1 = (f32[280,128]{1,0:T(8,128)S(1)}, f32[280,128]{1,0:T(8,128)S(1)}, u32[]{:S(2)}, u32[]{:S(2)}) collective-permute-start(f32[280,128]{1,0:T(8,128)S(1)} %get-tuple-element.25), channel_id=1, source_target_pairs={{0,24},{8,16},{16,8},{24,0},{1,25},{9,17},{17,9},{25,1},{2,26},{10... | collective-permute-start | bytes 430088 | tf_op jit(solution)/shard_map/ppermute | solution.py:575
  5.2 1.0 %collective-permute-start.2 = (f32[136,128]{1,0:T(8,128)S(1)}, f32[136,128]{1,0:T(8,128)S(1)}, u32[]{:S(2)}, u32[]{:S(2)}) collective-permute-start(f32[136,128]{1,0:T(8,128)S(1)} %get-tuple-element.26), channel_id=1, source_target_pairs={{0,8},{8,0},{16,24},{24,16},{1,9},{9,1},{17,25},{25,17},{2,10},{10... | collective-permute-start | bytes 208904 | tf_op jit(solution)/shard_map/ppermute | solution.py:575
  6.1 3.2 %collective-permute-start.3 = (f32[16,640]{1,0:T(8,128)S(1)}, f32[16,640]{1,0:T(8,128)S(1)}, u32[]{:S(2)}, u32[]{:S(2)}) collective-permute-start(f32[16,640]{1,0:T(8,128)S(1)} %get-tuple-element.27), channel_id=1, source_target_pairs={{0,7},{1,0},{2,1},{3,2},{4,3},{5,4},{6,5},{7,6},{8,15},{9,8},{10,9... | collective-permute-start | bytes 122888 | tf_op jit(solution)/shard_map/ppermute | solution.py:587
  9.3 0.3 %collective-permute-done.message.low = f32[16,640]{1,0:T(8,128)S(1)} collective-permute-done((f32[16,640]{1,0:T(8,128)S(1)}, f32[16,640]{1,0:T(8,128)S(1)}, u32[]{:S(2)}, u32[]{:S(2)}) %collective-permute-start) | collective-permute-done | bytes 40992 | tf_op jit(solution)/shard_map/ppermute | solution.py:587
  9.6 0.3 %weights.1.low_weights = f32[24,128]{1,0:T(8,128)S(1)} custom-call(f32[128,128]{1,0:T(8,128)S(1)} %get-tuple-element.21.columns.masses, f32[16,640]{1,0:T(8,128)S(1)} %collective-permute-done.message.low), custom_call_target="tpu_custom_call" | custom-call | flops 99999997952 | bytes 30000000 | tf_op jit(solution)/shard_map/weights/pallas_call | solution.py:606
  9.9 1.1 %collective-permute-done.3.high = f32[16,640]{1,0:T(8,128)S(1)} collective-permute-done((f32[16,640]{1,0:T(8,128)S(1)}, f32[16,640]{1,0:T(8,128)S(1)}, u32[]{:S(2)}, u32[]{:S(2)}) %collective-permute-start.3) | collective-permute-done | bytes 40992 | tf_op jit(solution)/shard_map/ppermute | solution.py:587
  11.0 0.0 collective-permute-done.2.from_near
  11.0 0.0 collective-permute-done.1.from_far
  11.0 0.5 %second.1 = (f32[128,528]{1,0:T(8,128)S(1)}, f32[456,128]{1,0:T(8,128)S(1)}, f32[168,128]{1,0:T(8,128)S(1)}, f32[4,528]{1,0:T(4,128)S(1)}, f32[8,128]{1,0:T(8,128)S(1)}) custom-call(f32[128,528]{1,0:T(8,128)S(1)} %get-tuple-element.20.total, f32[128,128]{1,0:T(8,128)S(1)} %get-tuple-element.21.columns.masses, f32[128,128]{1,0:T(8,128)S(1)} %get-tuple-element.22.operator, ...), custom_call_target="tpu_custom_call" | custom-call | tf_op jit(solution)/shard_map/second/pallas_call | solution.py:606
  11.5 0.0 copy-start.1
  11.5 0.0 collective-permute-start.4
  11.6 0.9 %collective-permute-start.5 = (f32[168,128]{1,0:T(8,128)S(1)}, f32[168,128]{1,0:T(8,128)S(1)}, u32[]{:S(2)}, u32[]{:S(2)}) collective-permute-start(f32[168,128]{1,0:T(8,128)S(1)} %get-tuple-element.31.to_far), channel_id=1, source_target_pairs={{0,24},{8,16},{16,8},{24,0},{1,25},{9,17},{17,9},{25,1},{2,26},{10... | collective-permute-start | bytes 258056 | tf_op jit(solution)/shard_map/ppermute | solution.py:575
  12.5 1.2 %collective-permute-start.6 = (f32[4,528]{1,0:T(4,128)S(1)}, f32[4,528]{1,0:T(4,128)S(1)}, u32[]{:S(2)}, u32[]{:S(2)}) collective-permute-start(f32[4,528]{1,0:T(4,128)S(1)} %get-tuple-element.32), channel_id=1, source_target_pairs={{0,16},{8,24},{16,0},{24,8},{1,17},{9,25},{17,1},{25,9},{2,18},{10... | collective-permute-start | bytes 25352 | tf_op jit(solution)/shard_map/ppermute | solution.py:575
  13.7 0.0 copy-done.1
  13.7 0.0 copy-start
  13.7 0.1 base.1
  13.8 0.0 collective-permute-done.4.refs_1_.from_near
  13.9 0.5 %copy-done = s32[4,32]{1,0:T(4,128)S(1)} copy-done((s32[4,32]{1,0:T(4,128)S(1)}, s32[4,32]{1,0:T(4,128)}, u32[]{:S(2)}) %copy-start) | copy-done | bytes 536
  14.4 0.7 %factors.1 = f32[320,128]{1,0:T(8,128)S(1)} custom-call(s32[4,32]{1,0:T(4,128)S(1)} %copy-done, f32[456,128]{1,0:T(8,128)S(1)} %get-tuple-element.30.refs_0_.to_near, f32[456,128]{1,0:T(8,128)S(1)} %collective-permute-done.4.refs_1_.from_near), custom_call_target="tpu_custom_call" | custom-call | tf_op jit(solution)/shard_map/factors/pallas_call | solution.py:606
  15.1 1.6 %collective-permute-done.6.ends_near.ends_far = f32[4,528]{1,0:T(4,128)S(1)} collective-permute-done((f32[4,528]{1,0:T(4,128)S(1)}, f32[4,528]{1,0:T(4,128)S(1)}, u32[]{:S(2)}, u32[]{:S(2)}) %collective-permute-start.6) | collective-permute-done | bytes 8480 | tf_op jit(solution)/shard_map/ppermute | solution.py:575
  16.7 0.0 collective-permute-done.5.from_far
  16.7 1.4 %third.1 = f32[4,32,528]{2,1,0:T(8,128)} custom-call(f32[1,528]{1,0:T(1,128)S(1)} %reshape.3.hyper, f32[128,528]{1,0:T(8,128)S(1)} %base.1, f32[128,128]{1,0:T(8,128)S(1)} %get-tuple-element.21.columns.masses, f32[8,128]{1,0:T(8,128)S(1)} %get-tuple-element.29.inner, f32[320,128]{1,0:T(8,128)S(1)} %factors.1, ...), custom_call_target="tpu_custom_call" | custom-call | tf_op jit(solution)/shard_map/third/pallas_call | solution.py:606
  (1 shorter events, 0.0 us)
Async XLA Ops:
  1.5 8.1 %collective-permute-start = (f32[16,640]{1,0:T(8,128)S(1)}, f32[16,640]{1,0:T(8,128)S(1)}, u32[]{:S(2)}, u32[]{:S(2)}) collective-permute-start(f32[16,640]{1,0:T(8,128)S(1)} %get-tuple-element.24), channel_id=1, source_target_pairs={{0,1},{1,2},{2,3},{3,4},{4,5},{5,6},{6,7},{7,0},{8,9},{9,10},{10,1... | collective-permute-start | bytes 122888 | tf_op jit(solution)/shard_map/ppermute | solution.py:587
  4.5 6.5 %collective-permute-start.1 = (f32[280,128]{1,0:T(8,128)S(1)}, f32[280,128]{1,0:T(8,128)S(1)}, u32[]{:S(2)}, u32[]{:S(2)}) collective-permute-start(f32[280,128]{1,0:T(8,128)S(1)} %get-tuple-element.25), channel_id=1, source_target_pairs={{0,24},{8,16},{16,8},{24,0},{1,25},{9,17},{17,9},{25,1},{2,26},{10... | collective-permute-start | bytes 430088 | tf_op jit(solution)/shard_map/ppermute | solution.py:575
  5.2 5.8 %collective-permute-start.2 = (f32[136,128]{1,0:T(8,128)S(1)}, f32[136,128]{1,0:T(8,128)S(1)}, u32[]{:S(2)}, u32[]{:S(2)}) collective-permute-start(f32[136,128]{1,0:T(8,128)S(1)} %get-tuple-element.26), channel_id=1, source_target_pairs={{0,8},{8,0},{16,24},{24,16},{1,9},{9,1},{17,25},{25,17},{2,10},{10... | collective-permute-start | bytes 208904 | tf_op jit(solution)/shard_map/ppermute | solution.py:575
  6.1 4.9 %collective-permute-start.3 = (f32[16,640]{1,0:T(8,128)S(1)}, f32[16,640]{1,0:T(8,128)S(1)}, u32[]{:S(2)}, u32[]{:S(2)}) collective-permute-start(f32[16,640]{1,0:T(8,128)S(1)} %get-tuple-element.27), channel_id=1, source_target_pairs={{0,7},{1,0},{2,1},{3,2},{4,3},{5,4},{6,5},{7,6},{8,15},{9,8},{10,9... | collective-permute-start | bytes 122888 | tf_op jit(solution)/shard_map/ppermute | solution.py:587
  11.5 2.2 %copy-start.1 = (f32[528]{0:T(1024)S(1)}, f32[528]{0:T(1024)}, u32[]{:S(2)}) copy-start(f32[528]{0:T(1024)} %param.9) | copy-start | bytes 6340
  11.5 2.3 %collective-permute-start.4 = (f32[456,128]{1,0:T(8,128)S(1)}, f32[456,128]{1,0:T(8,128)S(1)}, u32[]{:S(2)}, u32[]{:S(2)}) collective-permute-start(f32[456,128]{1,0:T(8,128)S(1)} %get-tuple-element.30.refs_0_.to_near), channel_id=1, source_target_pairs={{0,8},{8,0},{16,24},{24,16},{1,9},{9,1},{17,25},{25,17},{2,10},{10... | collective-permute-start | bytes 700424 | tf_op jit(solution)/shard_map/ppermute | solution.py:575
  11.6 5.1 %collective-permute-start.5 = (f32[168,128]{1,0:T(8,128)S(1)}, f32[168,128]{1,0:T(8,128)S(1)}, u32[]{:S(2)}, u32[]{:S(2)}) collective-permute-start(f32[168,128]{1,0:T(8,128)S(1)} %get-tuple-element.31.to_far), channel_id=1, source_target_pairs={{0,24},{8,16},{16,8},{24,0},{1,25},{9,17},{17,9},{25,1},{2,26},{10... | collective-permute-start | bytes 258056 | tf_op jit(solution)/shard_map/ppermute | solution.py:575
  12.5 4.2 %collective-permute-start.6 = (f32[4,528]{1,0:T(4,128)S(1)}, f32[4,528]{1,0:T(4,128)S(1)}, u32[]{:S(2)}, u32[]{:S(2)}) collective-permute-start(f32[4,528]{1,0:T(4,128)S(1)} %get-tuple-element.32), channel_id=1, source_target_pairs={{0,16},{8,24},{16,0},{24,8},{1,17},{9,25},{17,1},{25,9},{2,18},{10... | collective-permute-start | bytes 25352 | tf_op jit(solution)/shard_map/ppermute | solution.py:575
  13.7 0.7 %copy-start = (s32[4,32]{1,0:T(4,128)S(1)}, s32[4,32]{1,0:T(4,128)}, u32[]{:S(2)}) copy-start(s32[4,32]{1,0:T(4,128)} %slots.1) | copy-start | bytes 1540

commit v9 on v8

--- a/solution.py
+++ b/solution.py
@@ -141,6 +141,7 @@
     here,
     total,
     x_near,
+    x_near_rest,
     x_far,
     low,
     high,
@@ -149,6 +150,7 @@
     coefs,
     mass_here,
     inverse_here,
+    near_rows,
     sems,
 ):
     size_x, size_y, width = state.shape
@@ -179,7 +181,10 @@
         copy.wait()
     total[...] = product(split(matrix), split(here[...].reshape(count, width)))
     near, far = x_rows(count, size_y)
-    pack(total[near], x_near)
+    pack(total[near], near_rows)
+    rest = x_near_rest.shape[0]
+    x_near_rest[...] = near_rows[:rest, :]
+    x_near[...] = near_rows[rest:, :]
     pack(total[far], x_far)
     for first, message in ((0, low), (size_y - 4, high)):
         for i in range(4):
@@ -188,8 +193,8 @@
             message[rows, width : width + 2] = edge_rows(columns, first + i, size_x, size_y)[:, :2]
     for copy in copies[2 + size_x :]:
         copy.wait()
-    if x_far.shape[0] > x_near.shape[0]:
-        x_far[x_near.shape[0] :, :] = coefs[...]
+    if x_far.shape[0] > near_rows.shape[0]:
+        x_far[near_rows.shape[0] :, :] = coefs[...]
 
 
 def node_column(values, start, count):
@@ -272,6 +277,7 @@
     low,
     from_far,
     from_near,
+    from_near_rest,
     high,
     out,
     x_near,
@@ -281,13 +287,17 @@
     work,
     at_near,
     at_far,
+    near_rows,
 ):
     size_y, width = total.shape[0] // size_x, total.shape[1]
     depth = size_y + 8
     second = second_table()
     near, far = x_starts(size_x * size_y, size_y)
     work[...] = total[...]
-    add_packed(work, near, from_near, size_y)
+    rest = from_near_rest.shape[0]
+    near_rows[:rest, :] = from_near_rest[...]
+    near_rows[rest:, :] = from_near[...]
+    add_packed(work, near, near_rows, size_y)
     add_packed(work, far, from_far, size_y)
     sides = ((low, 0, 3, 0), (high, size_y - 1, 0, size_y - 8))
     beyond = []
@@ -618,14 +628,16 @@
     whole = array(columns, width)
     edge = array(4 * size_x, padded)
     extra = 3 * levels if riding else 0
+    rest = width // 256 * size_y
     first_rows, last_rows = packed_rows(size_y, width), packed_rows(size_y + 8, width)
-    here, total, x_near, x_far, y_low, y_high, operator, masses, coefs = call(
+    here, total, x_near, x_near_rest, x_far, y_low, y_high, operator, masses, coefs = call(
         start_kernel,
         "start",
         [
             array(size_x, size_y, width),
             whole,
-            array(first_rows, 128),
+            array(first_rows - rest, 128),
+            array(rest, 128),
             array(first_rows + extra, 128),
             edge,
             edge,
@@ -636,6 +648,7 @@
         [
             scratch(size_x, size_y),
             scratch(size_x, size_y),
+            scratch(first_rows, 128),
             pltpu.SemaphoreType.DMA((size_x + 5,)),
         ],
         *(
@@ -653,6 +666,7 @@
     )
     low = shifted(y_high, "gy", 1)
     from_far, from_near = exchanged(x_near, x_far, "gx")
+    from_near_rest = swapped(x_near_rest, "gx", lambda i: i ^ 1)
     high = shifted(y_low, "gy", -1)
     (low_weights,) = call(
         functools.partial(weights_kernel, size_x, size_y, width),
@@ -673,7 +687,12 @@
             array(4, width),
             array(2 * size_x, 128),
         ],
-        [scratch(columns, width), scratch(size_y + 8, width), scratch(size_y + 8, width)],
+        [
+            scratch(columns, width),
+            scratch(size_y + 8, width),
+            scratch(size_y + 8, width),
+            scratch(first_rows, 128),
+        ],
         total,
         masses,
         operator,
@@ -682,6 +701,7 @@
         low,
         from_far,
         from_near,
+        from_near_rest,
         high,
     )
     last_x = exchanged(x_near, x_far, "gx")

time: 18.3 us -> 17.8 us (0.973)
  starting transfers between devices: 10 us -> 9.78 us
  waiting for transfers between devices: 3.02 us -> 2.81 us
    ppermute x2, waiting for transfers between devices: 1.39 us -> 0.63 us  [shifted(): lax.ppermute(value, axis, [(i, (i + step) % size) for i in range(size)])]
    ppermute x5 -> x6, waiting for transfers between devices: 1.63 us -> 2.19 us  [swapped(): lax.ppermute(value, axis, [(i, partner(i)) for i in range(lax.axis_size(a...]
    ppermute x5 -> x6, starting transfers between devices: 3.78 us -> 3.36 us  [swapped(): lax.ppermute(value, axis, [(i, partner(i)) for i in range(lax.axis_size(a...]
    ppermute x2, starting transfers between devices: 6.22 us -> 6.42 us  [shifted(): lax.ppermute(value, axis, [(i, (i + step) % size) for i in range(size)])]
  transfers between devices with their start and end apart: 7 -> 8, of which waited for: 3 -> 5; matrix products, arithmetic and copies ran while one was open for 0% -> 0% of each run, Pallas kernels for 6% -> 6%
where the time goes in v9:
time: 17.8 us; the launch traced here: 17.7 us
  starting transfers between devices  9.78 us (55%)
  Pallas kernels  4.47 us (25%)
  waiting for transfers between devices  2.81 us (16%)
  local copies, waits for them, and re-layouts  0.56 us (3%)
    ppermute x2, starting transfers between devices, shifted(): lax.ppermute(value, axis, [(i, (i + step) % size) for i in range(size)])  6.42 us
    pallas_call x6, Pallas kernels, call(): pl.pallas_call(kernel, out_shape=outs, in_specs=[spec] * len(operands), o...  4.47 us
    ppermute x6, starting transfers between devices, swapped(): lax.ppermute(value, axis, [(i, partner(i)) for i in range(lax.axis_size(a...  3.36 us
    ppermute x6, waiting for transfers between devices, swapped(): lax.ppermute(value, axis, [(i, partner(i)) for i in range(lax.axis_size(a...  2.19 us
    ppermute x2, waiting for transfers between devices, shifted(): lax.ppermute(value, axis, [(i, (i + step) % size) for i in range(size)])  0.63 us
    unnamed x4, local copies, waits for them, and re-layouts  0.55 us
  transfers between devices with their start and end apart: 8, of which 5 were waited for; matrix products, arithmetic and copies ran while one was open for 0% of the time, Pallas kernels for 6%

profile of v9, /device:TPU:0, one launch (start us, length us, event | category | flops | bytes accessed | tf_op | source)
XLA Modules:
  0.0 17.7 jit_solution(16015412498931905351)
XLA Ops:
  0.0 1.5 %start.1 = (f32[4,32,528]{2,1,0:T(8,128)S(1)}, f32[128,528]{1,0:T(8,128)S(1)}, f32[72,128]{1,0:T(8,128)S(1)}, f32[64,128]{1,0:T(8,128)S(1)}, f32[280,128]{1,0:T(...) custom-call(f32[4,32,528]{2,1,0:T(8,128)} %state.1, ...), custom_call_target="tpu_custom_call" | custom-call | tf_op jit(solution)/shard_map/start/pallas_call | solution.py:616
  1.5 3.0 %collective-permute-start = (f32[16,640]{1,0:T(8,128)S(1)}, f32[16,640]{1,0:T(8,128)S(1)}, u32[]{:S(2)}, u32[]{:S(2)}) collective-permute-start(f32[16,640]{1,0:T(8,128)S(1)} %get-tuple-element.25), channel_id=1, source_target_pairs={{0,1},{1,2},{2,3},{3,4},{4,5},{5,6},{6,7},{7,0},{8,9},{9,10},{10,1... | collective-permute-start | bytes 122888 | tf_op jit(solution)/shard_map/ppermute | solution.py:597
  4.5 0.6 %collective-permute-start.1 = (f32[280,128]{1,0:T(8,128)S(1)}, f32[280,128]{1,0:T(8,128)S(1)}, u32[]{:S(2)}, u32[]{:S(2)}) collective-permute-start(f32[280,128]{1,0:T(8,128)S(1)} %get-tuple-element.26), channel_id=1, source_target_pairs={{0,24},{8,16},{16,8},{24,0},{1,25},{9,17},{17,9},{25,1},{2,26},{10... | collective-permute-start | bytes 430088 | tf_op jit(solution)/shard_map/ppermute | solution.py:585
  5.2 3.4 %collective-permute-start.4 = (f32[16,640]{1,0:T(8,128)S(1)}, f32[16,640]{1,0:T(8,128)S(1)}, u32[]{:S(2)}, u32[]{:S(2)}) collective-permute-start(f32[16,640]{1,0:T(8,128)S(1)} %get-tuple-element.29), channel_id=1, source_target_pairs={{0,7},{1,0},{2,1},{3,2},{4,3},{5,4},{6,5},{7,6},{8,15},{9,8},{10,9... | collective-permute-start | bytes 122888 | tf_op jit(solution)/shard_map/ppermute | solution.py:597
  8.6 0.5 %collective-permute-start.2 = (f32[72,128]{1,0:T(8,128)S(1)}, f32[72,128]{1,0:T(8,128)S(1)}, u32[]{:S(2)}, u32[]{:S(2)}) collective-permute-start(f32[72,128]{1,0:T(8,128)S(1)} %get-tuple-element.27), channel_id=1, source_target_pairs={{0,8},{8,0},{16,24},{24,16},{1,9},{9,1},{17,25},{25,17},{2,10},{10... | collective-permute-start | bytes 110600 | tf_op jit(solution)/shard_map/ppermute | solution.py:585
  9.1 0.0 collective-permute-start.3
  9.1 0.6 %collective-permute-done.message.low = f32[16,640]{1,0:T(8,128)S(1)} collective-permute-done((f32[16,640]{1,0:T(8,128)S(1)}, f32[16,640]{1,0:T(8,128)S(1)}, u32[]{:S(2)}, u32[]{:S(2)}) %collective-permute-start) | collective-permute-done | bytes 40992 | tf_op jit(solution)/shard_map/ppermute | solution.py:597
  9.7 0.3 %weights.1.low_weights = f32[24,128]{1,0:T(8,128)S(1)} custom-call(f32[128,128]{1,0:T(8,128)S(1)} %get-tuple-element.22.columns.masses, f32[16,640]{1,0:T(8,128)S(1)} %collective-permute-done.message.low), custom_call_target="tpu_custom_call" | custom-call | flops 99999997952 | bytes 30000000 | tf_op jit(solution)/shard_map/weights/pallas_call | solution.py:616
  9.9 0.3 %collective-permute-done.3.from_near_rest = f32[64,128]{1,0:T(8,128)S(1)} collective-permute-done((f32[64,128]{1,0:T(8,128)S(1)}, f32[64,128]{1,0:T(8,128)S(1)}, u32[]{:S(2)}, u32[]{:S(2)}) %collective-permute-start.3) | collective-permute-done | bytes 32800 | tf_op jit(solution)/shard_map/ppermute | solution.py:585
  10.3 0.0 collective-permute-done.2.from_near
  10.3 0.1 collective-permute-done.4.high
  10.3 0.2 %collective-permute-done.1.from_far = f32[280,128]{1,0:T(8,128)S(1)} collective-permute-done((f32[280,128]{1,0:T(8,128)S(1)}, f32[280,128]{1,0:T(8,128)S(1)}, u32[]{:S(2)}, u32[]{:S(2)}) %collective-permute-start.1) | collective-permute-done | bytes 143392 | tf_op jit(solution)/shard_map/ppermute | solution.py:585
  10.5 0.5 %second.1 = (f32[128,528]{1,0:T(8,128)S(1)}, f32[456,128]{1,0:T(8,128)S(1)}, f32[168,128]{1,0:T(8,128)S(1)}, f32[4,528]{1,0:T(4,128)S(1)}, f32[8,128]{1,0:T(8,128)S(1)}) custom-call(f32[128,528]{1,0:T(8,128)S(1)} %get-tuple-element.21.total, f32[128,128]{1,0:T(8,128)S(1)} %get-tuple-element.22.columns.masses, f32[128,128]{1,0:T(8,128)S(1)} %get-tuple-element.23.operator, ...), custom_call_target="tpu_custom_call" | custom-call | tf_op jit(solution)/shard_map/second/pallas_call | solution.py:616
  11.1 0.0 copy-start.1
  11.1 0.1 collective-permute-start.5
  11.2 1.3 %collective-permute-start.6 = (f32[168,128]{1,0:T(8,128)S(1)}, f32[168,128]{1,0:T(8,128)S(1)}, u32[]{:S(2)}, u32[]{:S(2)}) collective-permute-start(f32[168,128]{1,0:T(8,128)S(1)} %get-tuple-element.33.to_far), channel_id=1, source_target_pairs={{0,24},{8,16},{16,8},{24,0},{1,25},{9,17},{17,9},{25,1},{2,26},{10... | collective-permute-start | bytes 258056 | tf_op jit(solution)/shard_map/ppermute | solution.py:585
  12.5 0.8 %collective-permute-start.7 = (f32[4,528]{1,0:T(4,128)S(1)}, f32[4,528]{1,0:T(4,128)S(1)}, u32[]{:S(2)}, u32[]{:S(2)}) collective-permute-start(f32[4,528]{1,0:T(4,128)S(1)} %get-tuple-element.34), channel_id=1, source_target_pairs={{0,16},{8,24},{16,0},{24,8},{1,17},{9,25},{17,1},{25,9},{2,18},{10... | collective-permute-start | bytes 25352 | tf_op jit(solution)/shard_map/ppermute | solution.py:585
  13.3 0.0 copy-done.1
  13.3 0.0 copy-start
  13.3 0.1 base.1
  13.4 0.0 collective-permute-done.5.refs_1_.from_near
  13.4 0.5 %copy-done = s32[4,32]{1,0:T(4,128)S(1)} copy-done((s32[4,32]{1,0:T(4,128)S(1)}, s32[4,32]{1,0:T(4,128)}, u32[]{:S(2)}) %copy-start) | copy-done | bytes 536
  14.0 0.7 %factors.1 = f32[320,128]{1,0:T(8,128)S(1)} custom-call(s32[4,32]{1,0:T(4,128)S(1)} %copy-done, f32[456,128]{1,0:T(8,128)S(1)} %get-tuple-element.32.refs_0_.to_near, f32[456,128]{1,0:T(8,128)S(1)} %collective-permute-done.5.refs_1_.from_near), custom_call_target="tpu_custom_call" | custom-call | tf_op jit(solution)/shard_map/factors/pallas_call | solution.py:616
  14.6 1.6 %collective-permute-done.7.ends_near.ends_far = f32[4,528]{1,0:T(4,128)S(1)} collective-permute-done((f32[4,528]{1,0:T(4,128)S(1)}, f32[4,528]{1,0:T(4,128)S(1)}, u32[]{:S(2)}, u32[]{:S(2)}) %collective-permute-start.7) | collective-permute-done | bytes 8480 | tf_op jit(solution)/shard_map/ppermute | solution.py:585
  16.3 0.0 collective-permute-done.6.from_far
  16.3 1.4 %third.1 = f32[4,32,528]{2,1,0:T(8,128)} custom-call(f32[1,528]{1,0:T(1,128)S(1)} %reshape.3.hyper, f32[128,528]{1,0:T(8,128)S(1)} %base.1, f32[128,128]{1,0:T(8,128)S(1)} %get-tuple-element.22.columns.masses, f32[8,128]{1,0:T(8,128)S(1)} %get-tuple-element.31.inner, f32[320,128]{1,0:T(8,128)S(1)} %factors.1, ...), custom_call_target="tpu_custom_call" | custom-call | tf_op jit(solution)/shard_map/third/pallas_call | solution.py:616
  (1 shorter events, 0.0 us)
Async XLA Ops:
  1.5 8.1 %collective-permute-start = (f32[16,640]{1,0:T(8,128)S(1)}, f32[16,640]{1,0:T(8,128)S(1)}, u32[]{:S(2)}, u32[]{:S(2)}) collective-permute-start(f32[16,640]{1,0:T(8,128)S(1)} %get-tuple-element.25), channel_id=1, source_target_pairs={{0,1},{1,2},{2,3},{3,4},{4,5},{5,6},{6,7},{7,0},{8,9},{9,10},{10,1... | collective-permute-start | bytes 122888 | tf_op jit(solution)/shard_map/ppermute | solution.py:597
  4.5 6.0 %collective-permute-start.1 = (f32[280,128]{1,0:T(8,128)S(1)}, f32[280,128]{1,0:T(8,128)S(1)}, u32[]{:S(2)}, u32[]{:S(2)}) collective-permute-start(f32[280,128]{1,0:T(8,128)S(1)} %get-tuple-element.26), channel_id=1, source_target_pairs={{0,24},{8,16},{16,8},{24,0},{1,25},{9,17},{17,9},{25,1},{2,26},{10... | collective-permute-start | bytes 430088 | tf_op jit(solution)/shard_map/ppermute | solution.py:585
  5.2 5.2 %collective-permute-start.4 = (f32[16,640]{1,0:T(8,128)S(1)}, f32[16,640]{1,0:T(8,128)S(1)}, u32[]{:S(2)}, u32[]{:S(2)}) collective-permute-start(f32[16,640]{1,0:T(8,128)S(1)} %get-tuple-element.29), channel_id=1, source_target_pairs={{0,7},{1,0},{2,1},{3,2},{4,3},{5,4},{6,5},{7,6},{8,15},{9,8},{10,9... | collective-permute-start | bytes 122888 | tf_op jit(solution)/shard_map/ppermute | solution.py:597
  8.6 1.7 %collective-permute-start.2 = (f32[72,128]{1,0:T(8,128)S(1)}, f32[72,128]{1,0:T(8,128)S(1)}, u32[]{:S(2)}, u32[]{:S(2)}) collective-permute-start(f32[72,128]{1,0:T(8,128)S(1)} %get-tuple-element.27), channel_id=1, source_target_pairs={{0,8},{8,0},{16,24},{24,16},{1,9},{9,1},{17,25},{25,17},{2,10},{10... | collective-permute-start | bytes 110600 | tf_op jit(solution)/shard_map/ppermute | solution.py:585
  9.1 1.2 %collective-permute-start.3 = (f32[64,128]{1,0:T(8,128)S(1)}, f32[64,128]{1,0:T(8,128)S(1)}, u32[]{:S(2)}, u32[]{:S(2)}) collective-permute-start(f32[64,128]{1,0:T(8,128)S(1)} %get-tuple-element.28), channel_id=1, source_target_pairs={{0,8},{8,0},{16,24},{24,16},{1,9},{9,1},{17,25},{25,17},{2,10},{10... | collective-permute-start | bytes 98312 | tf_op jit(solution)/shard_map/ppermute | solution.py:585
  11.1 2.2 %copy-start.1 = (f32[528]{0:T(1024)S(1)}, f32[528]{0:T(1024)}, u32[]{:S(2)}) copy-start(f32[528]{0:T(1024)} %param.9) | copy-start | bytes 6340
  11.1 2.3 %collective-permute-start.5 = (f32[456,128]{1,0:T(8,128)S(1)}, f32[456,128]{1,0:T(8,128)S(1)}, u32[]{:S(2)}, u32[]{:S(2)}) collective-permute-start(f32[456,128]{1,0:T(8,128)S(1)} %get-tuple-element.32.refs_0_.to_near), channel_id=1, source_target_pairs={{0,8},{8,0},{16,24},{24,16},{1,9},{9,1},{17,25},{25,17},{2,10},{10... | collective-permute-start | bytes 700424 | tf_op jit(solution)/shard_map/ppermute | solution.py:585
  11.2 5.1 %collective-permute-start.6 = (f32[168,128]{1,0:T(8,128)S(1)}, f32[168,128]{1,0:T(8,128)S(1)}, u32[]{:S(2)}, u32[]{:S(2)}) collective-permute-start(f32[168,128]{1,0:T(8,128)S(1)} %get-tuple-element.33.to_far), channel_id=1, source_target_pairs={{0,24},{8,16},{16,8},{24,0},{1,25},{9,17},{17,9},{25,1},{2,26},{10... | collective-permute-start | bytes 258056 | tf_op jit(solution)/shard_map/ppermute | solution.py:585
  12.5 3.8 %collective-permute-start.7 = (f32[4,528]{1,0:T(4,128)S(1)}, f32[4,528]{1,0:T(4,128)S(1)}, u32[]{:S(2)}, u32[]{:S(2)}) collective-permute-start(f32[4,528]{1,0:T(4,128)S(1)} %get-tuple-element.34), channel_id=1, source_target_pairs={{0,16},{8,24},{16,0},{24,8},{1,17},{9,25},{17,1},{25,9},{2,18},{10... | collective-permute-start | bytes 25352 | tf_op jit(solution)/shard_map/ppermute | solution.py:585
  13.3 0.7 %copy-start = (s32[4,32]{1,0:T(4,128)S(1)}, s32[4,32]{1,0:T(4,128)}, u32[]{:S(2)}) copy-start(s32[4,32]{1,0:T(4,128)} %slots.1) | copy-start | bytes 1540

commit v10 on v9

--- a/solution.py
+++ b/solution.py
@@ -284,6 +284,8 @@
     x_far,
     line_ends,
     inner,
+    own_coefs,
+    far_coefs,
     work,
     at_near,
     at_far,
@@ -345,11 +347,10 @@
                 line_ends[2 * side + 1 : 2 * side + 2, :] = row_near
     pack(at_near[...], x_near)
     pack(at_far[...], x_far)
-    if x_near.shape[0] > x_far.shape[0]:
-        count = coefs.shape[0]
-        start = last + 8
-        x_near[start : start + count, :] = coefs[...]
-        x_near[start + count :, :] = from_far[packed_rows(size_y, width) :, :]
+    own_coefs[...] = coefs[...]
+    start = packed_rows(size_y, width)
+    if from_far.shape[0] > start:
+        far_coefs[...] = from_far[start:, :]
 
 
 def third_kernel(
@@ -539,13 +540,10 @@
 
 def factor_kernel(levels, slots, *refs):
     factors = refs[-1]
-    if len(refs) == 3:
+    if len(refs) == 5:
         here = lax.axis_index("gx")
-        pieces = []
-        for message, owner in zip(refs, (here, here ^ 1)):
-            start = message.shape[0] - 6 * levels
-            pieces.append((owner, message[start : start + 3 * levels, :]))
-            pieces.append((owner ^ 3, message[start + 3 * levels :, :]))
+        owners = (here, here ^ 3, here ^ 1, here ^ 2)
+        pieces = [(owner, message[...]) for owner, message in zip(owners, refs)]
     else:
         pieces = [(peer, refs[0][peer]) for peer in range(refs[0].shape[0])]
     columns = factors.shape[1]
@@ -677,15 +675,17 @@
         low,
         cost=LONG,
     )
-    total, x_near, x_far, line_ends, inner = call(
+    total, x_near, x_far, line_ends, inner, own_coefs, far_coefs = call(
         functools.partial(second_kernel, size_x),
         "second",
         [
             whole,
-            array(last_rows + 2 * extra, 128),
             array(last_rows, 128),
+            array(last_rows + 8, 128),
             array(4, width),
             array(2 * size_x, 128),
+            array(3 * levels, span),
+            array(3 * levels, span),
         ],
         [
             scratch(columns, width),
@@ -711,7 +711,8 @@
     if peers != 4:
         ends_far = swapped(line_ends, "gx", lambda i: (i - (2 if i % 2 else -2)) % peers)
     if riding:
-        pieces = [x_near, last_x[1]]
+        pieces = [own_coefs, far_coefs]
+        pieces += [swapped(piece, "gx", lambda i: i ^ 1) for piece in pieces]
     else:
         pieces = [lax.all_gather(coefs, "gx")]
     (factors,) = call(

time: 17.8 us -> 18.3 us (1.028)
  starting transfers between devices: 9.78 us -> 10.3 us
    ppermute x6 -> x8, starting transfers between devices: 3.36 us -> 3.84 us  [swapped(): lax.ppermute(value, axis, [(i, partner(i)) for i in range(lax.axis_size(a...]
    ppermute x6 -> x8, waiting for transfers between devices: 2.19 us -> 2.14 us  [swapped(): lax.ppermute(value, axis, [(i, partner(i)) for i in range(lax.axis_size(a...]
  transfers between devices with their start and end apart: 8 -> 10, of which waited for: 5 -> 5; matrix products, arithmetic and copies ran while one was open for 0% -> 0% of each run, Pallas kernels for 6% -> 6%
where the time goes in v10:
time: 18.3 us; the launch traced here: 18.1 us
  starting transfers between devices  10.3 us (56%)
  Pallas kernels  4.47 us (24%)
  waiting for transfers between devices  2.77 us (15%)
  local copies, waits for them, and re-layouts  0.54 us (3%)
    ppermute x2, starting transfers between devices, shifted(): lax.ppermute(value, axis, [(i, (i + step) % size) for i in range(size)])  6.42 us
    pallas_call x6, Pallas kernels, call(): pl.pallas_call(kernel, out_shape=outs, in_specs=[spec] * len(operands), o...  4.47 us
    ppermute x8, starting transfers between devices, swapped(): lax.ppermute(value, axis, [(i, partner(i)) for i in range(lax.axis_size(a...  3.84 us
    ppermute x8, waiting for transfers between devices, swapped(): lax.ppermute(value, axis, [(i, partner(i)) for i in range(lax.axis_size(a...  2.14 us
    ppermute x2, waiting for transfers between devices, shifted(): lax.ppermute(value, axis, [(i, (i + step) % size) for i in range(size)])  0.63 us
    unnamed x4, local copies, waits for them, and re-layouts  0.54 us
  transfers between devices with their start and end apart: 10, of which 5 were waited for; matrix products, arithmetic and copies ran while one was open for 0% of the time, Pallas kernels for 6%

profile of v10, /device:TPU:0, one launch (start us, length us, event | category | flops | bytes accessed | tf_op | source)
XLA Modules:
  0.0 18.1 jit_solution(7596785181823744523)
XLA Ops:
  0.0 1.5 %start.1 = (f32[4,32,528]{2,1,0:T(8,128)S(1)}, f32[128,528]{1,0:T(8,128)S(1)}, f32[72,128]{1,0:T(8,128)S(1)}, f32[64,128]{1,0:T(8,128)S(1)}, f32[280,128]{1,0:T(...) custom-call(f32[4,32,528]{2,1,0:T(8,128)} %state.1, ...), custom_call_target="tpu_custom_call" | custom-call | tf_op jit(solution)/shard_map/start/pallas_call | solution.py:614
  1.5 3.0 %collective-permute-start = (f32[16,640]{1,0:T(8,128)S(1)}, f32[16,640]{1,0:T(8,128)S(1)}, u32[]{:S(2)}, u32[]{:S(2)}) collective-permute-start(f32[16,640]{1,0:T(8,128)S(1)} %get-tuple-element.27), channel_id=1, source_target_pairs={{0,1},{1,2},{2,3},{3,4},{4,5},{5,6},{6,7},{7,0},{8,9},{9,10},{10,1... | collective-permute-start | bytes 122888 | tf_op jit(solution)/shard_map/ppermute | solution.py:595
  4.5 0.6 %collective-permute-start.1 = (f32[280,128]{1,0:T(8,128)S(1)}, f32[280,128]{1,0:T(8,128)S(1)}, u32[]{:S(2)}, u32[]{:S(2)}) collective-permute-start(f32[280,128]{1,0:T(8,128)S(1)} %get-tuple-element.28), channel_id=1, source_target_pairs={{0,24},{8,16},{16,8},{24,0},{1,25},{9,17},{17,9},{25,1},{2,26},{10... | collective-permute-start | bytes 430088 | tf_op jit(solution)/shard_map/ppermute | solution.py:583
  5.2 3.4 %collective-permute-start.4 = (f32[16,640]{1,0:T(8,128)S(1)}, f32[16,640]{1,0:T(8,128)S(1)}, u32[]{:S(2)}, u32[]{:S(2)}) collective-permute-start(f32[16,640]{1,0:T(8,128)S(1)} %get-tuple-element.31), channel_id=1, source_target_pairs={{0,7},{1,0},{2,1},{3,2},{4,3},{5,4},{6,5},{7,6},{8,15},{9,8},{10,9... | collective-permute-start | bytes 122888 | tf_op jit(solution)/shard_map/ppermute | solution.py:595
  8.6 0.5 %collective-permute-start.2 = (f32[72,128]{1,0:T(8,128)S(1)}, f32[72,128]{1,0:T(8,128)S(1)}, u32[]{:S(2)}, u32[]{:S(2)}) collective-permute-start(f32[72,128]{1,0:T(8,128)S(1)} %get-tuple-element.29), channel_id=1, source_target_pairs={{0,8},{8,0},{16,24},{24,16},{1,9},{9,1},{17,25},{25,17},{2,10},{10... | collective-permute-start | bytes 110600 | tf_op jit(solution)/shard_map/ppermute | solution.py:583
  9.1 0.0 collective-permute-start.3
  9.1 0.6 %collective-permute-done.message.low = f32[16,640]{1,0:T(8,128)S(1)} collective-permute-done((f32[16,640]{1,0:T(8,128)S(1)}, f32[16,640]{1,0:T(8,128)S(1)}, u32[]{:S(2)}, u32[]{:S(2)}) %collective-permute-start) | collective-permute-done | bytes 40992 | tf_op jit(solution)/shard_map/ppermute | solution.py:595
  9.7 0.3 %weights.1.low_weights = f32[24,128]{1,0:T(8,128)S(1)} custom-call(f32[128,128]{1,0:T(8,128)S(1)} %get-tuple-element.24.columns.masses, f32[16,640]{1,0:T(8,128)S(1)} %collective-permute-done.message.low), custom_call_target="tpu_custom_call" | custom-call | flops 99999997952 | bytes 30000000 | tf_op jit(solution)/shard_map/weights/pallas_call | solution.py:614
  9.9 0.3 %collective-permute-done.3.from_near_rest = f32[64,128]{1,0:T(8,128)S(1)} collective-permute-done((f32[64,128]{1,0:T(8,128)S(1)}, f32[64,128]{1,0:T(8,128)S(1)}, u32[]{:S(2)}, u32[]{:S(2)}) %collective-permute-start.3) | collective-permute-done | bytes 32800 | tf_op jit(solution)/shard_map/ppermute | solution.py:583
  10.3 0.0 collective-permute-done.2.from_near
  10.3 0.1 collective-permute-done.4.high
  10.3 0.2 %collective-permute-done.1.from_far = f32[280,128]{1,0:T(8,128)S(1)} collective-permute-done((f32[280,128]{1,0:T(8,128)S(1)}, f32[280,128]{1,0:T(8,128)S(1)}, u32[]{:S(2)}, u32[]{:S(2)}) %collective-permute-start.1) | collective-permute-done | bytes 143392 | tf_op jit(solution)/shard_map/ppermute | solution.py:583
  10.5 0.5 %second.1 = (f32[128,528]{1,0:T(8,128)S(1)}, f32[168,128]{1,0:T(8,128)S(1)}, f32[176,128]{1,0:T(8,128)S(1)}, f32[4,528]{1,0:T(4,128)S(1)}, f32[8,128]{1,0:T(8,12...) custom-call(f32[128,528]{1,0:T(8,128)S(1)} %get-tuple-element.23.total, ...), custom_call_target="tpu_custom_call" | custom-call | tf_op jit(solution)/shard_map/second/pallas_call | solution.py:614
  11.1 0.0 copy-start.1
  11.1 0.8 %collective-permute-start.7 = (f32[176,128]{1,0:T(8,128)S(1)}, f32[176,128]{1,0:T(8,128)S(1)}, u32[]{:S(2)}, u32[]{:S(2)}) collective-permute-start(f32[176,128]{1,0:T(8,128)S(1)} %get-tuple-element.37.to_far), channel_id=1, source_target_pairs={{0,24},{8,16},{16,8},{24,0},{1,25},{9,17},{17,9},{25,1},{2,26},{10... | collective-permute-start | bytes 270344 | tf_op jit(solution)/shard_map/ppermute | solution.py:583
  11.8 0.7 %collective-permute-start.8 = (f32[168,128]{1,0:T(8,128)S(1)}, f32[168,128]{1,0:T(8,128)S(1)}, u32[]{:S(2)}, u32[]{:S(2)}) collective-permute-start(f32[168,128]{1,0:T(8,128)S(1)} %get-tuple-element.36.to_near), channel_id=1, source_target_pairs={{0,8},{8,0},{16,24},{24,16},{1,9},{9,1},{17,25},{25,17},{2,10},{10... | collective-permute-start | bytes 258056 | tf_op jit(solution)/shard_map/ppermute | solution.py:583
  12.5 0.0 collective-permute-start.5
  12.5 0.5 %collective-permute-start.6 = (f32[144,128]{1,0:T(8,128)S(1)}, f32[144,128]{1,0:T(8,128)S(1)}, u32[]{:S(2)}, u32[]{:S(2)}) collective-permute-start(f32[144,128]{1,0:T(8,128)S(1)} %get-tuple-element.35.refs_1_), channel_id=1, source_target_pairs={{0,8},{8,0},{16,24},{24,16},{1,9},{9,1},{17,25},{25,17},{2,10},{10... | collective-permute-start | bytes 221192 | tf_op jit(solution)/shard_map/ppermute | solution.py:583
  13.0 0.8 %collective-permute-start.9 = (f32[4,528]{1,0:T(4,128)S(1)}, f32[4,528]{1,0:T(4,128)S(1)}, u32[]{:S(2)}, u32[]{:S(2)}) collective-permute-start(f32[4,528]{1,0:T(4,128)S(1)} %get-tuple-element.38), channel_id=1, source_target_pairs={{0,16},{8,24},{16,0},{24,8},{1,17},{9,25},{17,1},{25,9},{2,18},{10... | collective-permute-start | bytes 25352 | tf_op jit(solution)/shard_map/ppermute | solution.py:583
  13.8 0.0 copy-done.1
  13.8 0.0 copy-start
  13.8 0.1 base.1
  13.9 0.0 collective-permute-done.5.refs_2_
  13.9 0.0 collective-permute-done.6.refs_3_
  13.9 0.5 %copy-done = s32[4,32]{1,0:T(4,128)S(1)} copy-done((s32[4,32]{1,0:T(4,128)S(1)}, s32[4,32]{1,0:T(4,128)}, u32[]{:S(2)}) %copy-start) | copy-done | bytes 536
  14.4 0.7 %factors.1 = f32[320,128]{1,0:T(8,128)S(1)} custom-call(s32[4,32]{1,0:T(4,128)S(1)} %copy-done, f32[144,128]{1,0:T(8,128)S(1)} %get-tuple-element.34.refs_0_, f32[144,128]{1,0:T(8,128)S(1)} %get-tuple-element.35.refs_1_, f32[144,128]{1,0:T(8,128)S(1)} %collective-permute-done.5.refs_2_, f32[144,128]{1,0:T(8,128)S(1)} %collective-permute-done.6.refs_3_), custom_call_target="tpu_custom_call" | custom-call | tf_op jit(solution)/shard_map/factors/pallas_call | solution.py:614
  15.1 1.6 %collective-permute-done.9.ends_near.ends_far = f32[4,528]{1,0:T(4,128)S(1)} collective-permute-done((f32[4,528]{1,0:T(4,128)S(1)}, f32[4,528]{1,0:T(4,128)S(1)}, u32[]{:S(2)}, u32[]{:S(2)}) %collective-permute-start.9) | collective-permute-done | bytes 8480 | tf_op jit(solution)/shard_map/ppermute | solution.py:583
  16.7 0.0 collective-permute-done.8.from_near
  16.7 0.0 collective-permute-done.7.from_far
  16.7 1.4 %third.1 = f32[4,32,528]{2,1,0:T(8,128)} custom-call(f32[1,528]{1,0:T(1,128)S(1)} %reshape.3.hyper, f32[128,528]{1,0:T(8,128)S(1)} %base.1, f32[128,128]{1,0:T(8,128)S(1)} %get-tuple-element.24.columns.masses, f32[8,128]{1,0:T(8,128)S(1)} %get-tuple-element.33.inner, f32[320,128]{1,0:T(8,128)S(1)} %factors.1, f32[168,128]{1,0:T(8,128)S(1)} %get-tuple-element.36.to_near, ...), custom_call_target="tpu_custom_call" | custom-call | tf_op jit(solution)/shard_map/third/pallas_call | solution.py:614
  (1 shorter events, 0.0 us)
Async XLA Ops:
  1.5 8.1 %collective-permute-start = (f32[16,640]{1,0:T(8,128)S(1)}, f32[16,640]{1,0:T(8,128)S(1)}, u32[]{:S(2)}, u32[]{:S(2)}) collective-permute-start(f32[16,640]{1,0:T(8,128)S(1)} %get-tuple-element.27), channel_id=1, source_target_pairs={{0,1},{1,2},{2,3},{3,4},{4,5},{5,6},{6,7},{7,0},{8,9},{9,10},{10,1... | collective-permute-start | bytes 122888 | tf_op jit(solution)/shard_map/ppermute | solution.py:595
  4.5 6.0 %collective-permute-start.1 = (f32[280,128]{1,0:T(8,128)S(1)}, f32[280,128]{1,0:T(8,128)S(1)}, u32[]{:S(2)}, u32[]{:S(2)}) collective-permute-start(f32[280,128]{1,0:T(8,128)S(1)} %get-tuple-element.28), channel_id=1, source_target_pairs={{0,24},{8,16},{16,8},{24,0},{1,25},{9,17},{17,9},{25,1},{2,26},{10... | collective-permute-start | bytes 430088 | tf_op jit(solution)/shard_map/ppermute | solution.py:583
  5.2 5.2 %collective-permute-start.4 = (f32[16,640]{1,0:T(8,128)S(1)}, f32[16,640]{1,0:T(8,128)S(1)}, u32[]{:S(2)}, u32[]{:S(2)}) collective-permute-start(f32[16,640]{1,0:T(8,128)S(1)} %get-tuple-element.31), channel_id=1, source_target_pairs={{0,7},{1,0},{2,1},{3,2},{4,3},{5,4},{6,5},{7,6},{8,15},{9,8},{10,9... | collective-permute-start | bytes 122888 | tf_op jit(solution)/shard_map/ppermute | solution.py:595
  8.6 1.7 %collective-permute-start.2 = (f32[72,128]{1,0:T(8,128)S(1)}, f32[72,128]{1,0:T(8,128)S(1)}, u32[]{:S(2)}, u32[]{:S(2)}) collective-permute-start(f32[72,128]{1,0:T(8,128)S(1)} %get-tuple-element.29), channel_id=1, source_target_pairs={{0,8},{8,0},{16,24},{24,16},{1,9},{9,1},{17,25},{25,17},{2,10},{10... | collective-permute-start | bytes 110600 | tf_op jit(solution)/shard_map/ppermute | solution.py:583
  9.1 1.2 %collective-permute-start.3 = (f32[64,128]{1,0:T(8,128)S(1)}, f32[64,128]{1,0:T(8,128)S(1)}, u32[]{:S(2)}, u32[]{:S(2)}) collective-permute-start(f32[64,128]{1,0:T(8,128)S(1)} %get-tuple-element.30), channel_id=1, source_target_pairs={{0,8},{8,0},{16,24},{24,16},{1,9},{9,1},{17,25},{25,17},{2,10},{10... | collective-permute-start | bytes 98312 | tf_op jit(solution)/shard_map/ppermute | solution.py:583
  11.1 2.7 %copy-start.1 = (f32[528]{0:T(1024)S(1)}, f32[528]{0:T(1024)}, u32[]{:S(2)}) copy-start(f32[528]{0:T(1024)} %param.9) | copy-start | bytes 6340
  11.1 5.6 %collective-permute-start.7 = (f32[176,128]{1,0:T(8,128)S(1)}, f32[176,128]{1,0:T(8,128)S(1)}, u32[]{:S(2)}, u32[]{:S(2)}) collective-permute-start(f32[176,128]{1,0:T(8,128)S(1)} %get-tuple-element.37.to_far), channel_id=1, source_target_pairs={{0,24},{8,16},{16,8},{24,0},{1,25},{9,17},{17,9},{25,1},{2,26},{10... | collective-permute-start | bytes 270344 | tf_op jit(solution)/shard_map/ppermute | solution.py:583
  11.8 4.9 %collective-permute-start.8 = (f32[168,128]{1,0:T(8,128)S(1)}, f32[168,128]{1,0:T(8,128)S(1)}, u32[]{:S(2)}, u32[]{:S(2)}) collective-permute-start(f32[168,128]{1,0:T(8,128)S(1)} %get-tuple-element.36.to_near), channel_id=1, source_target_pairs={{0,8},{8,0},{16,24},{24,16},{1,9},{9,1},{17,25},{25,17},{2,10},{10... | collective-permute-start | bytes 258056 | tf_op jit(solution)/shard_map/ppermute | solution.py:583
  12.5 1.4 %collective-permute-start.5 = (f32[144,128]{1,0:T(8,128)S(1)}, f32[144,128]{1,0:T(8,128)S(1)}, u32[]{:S(2)}, u32[]{:S(2)}) collective-permute-start(f32[144,128]{1,0:T(8,128)S(1)} %get-tuple-element.34.refs_0_), channel_id=1, source_target_pairs={{0,8},{8,0},{16,24},{24,16},{1,9},{9,1},{17,25},{25,17},{2,10},{10... | collective-permute-start | bytes 221192 | tf_op jit(solution)/shard_map/ppermute | solution.py:583
  12.5 1.4 %collective-permute-start.6 = (f32[144,128]{1,0:T(8,128)S(1)}, f32[144,128]{1,0:T(8,128)S(1)}, u32[]{:S(2)}, u32[]{:S(2)}) collective-permute-start(f32[144,128]{1,0:T(8,128)S(1)} %get-tuple-element.35.refs_1_), channel_id=1, source_target_pairs={{0,8},{8,0},{16,24},{24,16},{1,9},{9,1},{17,25},{25,17},{2,10},{10... | collective-permute-start | bytes 221192 | tf_op jit(solution)/shard_map/ppermute | solution.py:583
  13.0 3.7 %collective-permute-start.9 = (f32[4,528]{1,0:T(4,128)S(1)}, f32[4,528]{1,0:T(4,128)S(1)}, u32[]{:S(2)}, u32[]{:S(2)}) collective-permute-start(f32[4,528]{1,0:T(4,128)S(1)} %get-tuple-element.38), channel_id=1, source_target_pairs={{0,16},{8,24},{16,0},{24,8},{1,17},{9,25},{17,1},{25,9},{2,18},{10... | collective-permute-start | bytes 25352 | tf_op jit(solution)/shard_map/ppermute | solution.py:583
  13.8 0.7 %copy-start = (s32[4,32]{1,0:T(4,128)S(1)}, s32[4,32]{1,0:T(4,128)}, u32[]{:S(2)}) copy-start(s32[4,32]{1,0:T(4,128)} %slots.1) | copy-start | bytes 1540

commit v11 on v9

--- a/solution.py
+++ b/solution.py
@@ -159,6 +159,9 @@
     pairs += [(state.at[x], here.at[x]) for x in range(size_x)]
     for i, source in enumerate((diff, fall, cloud)):
         pairs.append((source.at[0], coefs.at[i * levels : (i + 1) * levels]))
+        start = near_rows.shape[0] + i * levels
+        if x_far.shape[0] > start:
+            pairs.append((source.at[0], x_far.at[start : start + levels]))
     copies = [
         pltpu.make_async_copy(source, target, sems.at[i])
         for i, (source, target) in enumerate(pairs)
@@ -193,8 +196,6 @@
             message[rows, width : width + 2] = edge_rows(columns, first + i, size_x, size_y)[:, :2]
     for copy in copies[2 + size_x :]:
         copy.wait()
-    if x_far.shape[0] > near_rows.shape[0]:
-        x_far[near_rows.shape[0] :, :] = coefs[...]
 
 
 def node_column(values, start, count):
@@ -494,8 +495,9 @@
     rest_known = forward(rest, rest_turned, rest_values)
     back(main, main_turned, main_values, main_known)
     tiles = -(-width // 128)
-    settled_tiles, main_tiles = -(-3 * levels // 128), main[1] * levels // 128
-    copies = [leave(i) for i in range(settled_tiles, main_tiles)]
+    settled_tiles = -(-3 * levels // 128)
+    back(rest, rest_turned, rest_values, rest_known)
+    copies = [leave(i) for i in range(settled_tiles, tiles)]
     heat, vapour, liquid = (turned.at[i * pitch : i * pitch + levels] for i in range(3))
     condensed = cloud[...] * 0.5 * jnp.maximum(vapour[...] - 0.3 * heat[...], 0.0)
     vapour[...] = vapour[...] - condensed
@@ -508,9 +510,7 @@
             liquid[k : k + 1, :] = settled[side]
     through = factors[6 * levels : 6 * levels + half, :]
     liquid[half:, :] = liquid[half:, :] + through * settled[0]
-    back(rest, rest_turned, rest_values, rest_known)
     copies += [leave(i) for i in range(settled_tiles)]
-    copies += [leave(i) for i in range(main_tiles, tiles)]
     for copy in copies:
         copy.wait()
 
@@ -649,7 +649,7 @@
             scratch(size_x, size_y),
             scratch(size_x, size_y),
             scratch(first_rows, 128),
-            pltpu.SemaphoreType.DMA((size_x + 5,)),
+            pltpu.SemaphoreType.DMA((size_x + 8,)),
         ],
         *(
             pltpu.with_memory_space_constraint(value, pltpu.HBM)

time: 17.8 us -> 18 us (1.011)
  no operation moved by 1% of the time
where the time goes in v11:
time: 18 us; the launch traced here: 17.8 us
  starting transfers between devices  9.78 us (54%)
  Pallas kernels  4.59 us (26%)
  waiting for transfers between devices  2.81 us (16%)
  local copies, waits for them, and re-layouts  0.56 us (3%)
    ppermute x2, starting transfers between devices, shifted(): lax.ppermute(value, axis, [(i, (i + step) % size) for i in range(size)])  6.42 us
    pallas_call x6, Pallas kernels, call(): pl.pallas_call(kernel, out_shape=outs, in_specs=[spec] * len(operands), o...  4.59 us
    ppermute x6, starting transfers between devices, swapped(): lax.ppermute(value, axis, [(i, partner(i)) for i in range(lax.axis_size(a...  3.36 us
    ppermute x6, waiting for transfers between devices, swapped(): lax.ppermute(value, axis, [(i, partner(i)) for i in range(lax.axis_size(a...  2.19 us
    ppermute x2, waiting for transfers between devices, shifted(): lax.ppermute(value, axis, [(i, (i + step) % size) for i in range(size)])  0.63 us
    unnamed x4, local copies, waits for them, and re-layouts  0.55 us
  transfers between devices with their start and end apart: 8, of which 5 were waited for; matrix products, arithmetic and copies ran while one was open for 0% of the time, Pallas kernels for 6%

profile of v11, /device:TPU:0, one launch (start us, length us, event | category | flops | bytes accessed | tf_op | source)
XLA Modules:
  0.0 17.8 jit_solution(6920104205296713370)
XLA Ops:
  0.0 1.5 %start.1 = (f32[4,32,528]{2,1,0:T(8,128)S(1)}, f32[128,528]{1,0:T(8,128)S(1)}, f32[72,128]{1,0:T(8,128)S(1)}, f32[64,128]{1,0:T(8,128)S(1)}, f32[280,128]{1,0:T(...) custom-call(f32[4,32,528]{2,1,0:T(8,128)} %state.1, ...), custom_call_target="tpu_custom_call" | custom-call | tf_op jit(solution)/shard_map/start/pallas_call | solution.py:616
  1.5 3.0 %collective-permute-start = (f32[16,640]{1,0:T(8,128)S(1)}, f32[16,640]{1,0:T(8,128)S(1)}, u32[]{:S(2)}, u32[]{:S(2)}) collective-permute-start(f32[16,640]{1,0:T(8,128)S(1)} %get-tuple-element.25), channel_id=1, source_target_pairs={{0,1},{1,2},{2,3},{3,4},{4,5},{5,6},{6,7},{7,0},{8,9},{9,10},{10,1... | collective-permute-start | bytes 122888 | tf_op jit(solution)/shard_map/ppermute | solution.py:597
  4.6 0.6 %collective-permute-start.1 = (f32[280,128]{1,0:T(8,128)S(1)}, f32[280,128]{1,0:T(8,128)S(1)}, u32[]{:S(2)}, u32[]{:S(2)}) collective-permute-start(f32[280,128]{1,0:T(8,128)S(1)} %get-tuple-element.26), channel_id=1, source_target_pairs={{0,24},{8,16},{16,8},{24,0},{1,25},{9,17},{17,9},{25,1},{2,26},{10... | collective-permute-start | bytes 430088 | tf_op jit(solution)/shard_map/ppermute | solution.py:585
  5.2 3.4 %collective-permute-start.4 = (f32[16,640]{1,0:T(8,128)S(1)}, f32[16,640]{1,0:T(8,128)S(1)}, u32[]{:S(2)}, u32[]{:S(2)}) collective-permute-start(f32[16,640]{1,0:T(8,128)S(1)} %get-tuple-element.29), channel_id=1, source_target_pairs={{0,7},{1,0},{2,1},{3,2},{4,3},{5,4},{6,5},{7,6},{8,15},{9,8},{10,9... | collective-permute-start | bytes 122888 | tf_op jit(solution)/shard_map/ppermute | solution.py:597
  8.6 0.5 %collective-permute-start.2 = (f32[72,128]{1,0:T(8,128)S(1)}, f32[72,128]{1,0:T(8,128)S(1)}, u32[]{:S(2)}, u32[]{:S(2)}) collective-permute-start(f32[72,128]{1,0:T(8,128)S(1)} %get-tuple-element.27), channel_id=1, source_target_pairs={{0,8},{8,0},{16,24},{24,16},{1,9},{9,1},{17,25},{25,17},{2,10},{10... | collective-permute-start | bytes 110600 | tf_op jit(solution)/shard_map/ppermute | solution.py:585
  9.1 0.0 collective-permute-start.3
  9.1 0.6 %collective-permute-done.message.low = f32[16,640]{1,0:T(8,128)S(1)} collective-permute-done((f32[16,640]{1,0:T(8,128)S(1)}, f32[16,640]{1,0:T(8,128)S(1)}, u32[]{:S(2)}, u32[]{:S(2)}) %collective-permute-start) | collective-permute-done | bytes 40992 | tf_op jit(solution)/shard_map/ppermute | solution.py:597
  9.7 0.3 %weights.1.low_weights = f32[24,128]{1,0:T(8,128)S(1)} custom-call(f32[128,128]{1,0:T(8,128)S(1)} %get-tuple-element.22.columns.masses, f32[16,640]{1,0:T(8,128)S(1)} %collective-permute-done.message.low), custom_call_target="tpu_custom_call" | custom-call | flops 99999997952 | bytes 30000000 | tf_op jit(solution)/shard_map/weights/pallas_call | solution.py:616
  10.0 0.3 %collective-permute-done.3.from_near_rest = f32[64,128]{1,0:T(8,128)S(1)} collective-permute-done((f32[64,128]{1,0:T(8,128)S(1)}, f32[64,128]{1,0:T(8,128)S(1)}, u32[]{:S(2)}, u32[]{:S(2)}) %collective-permute-start.3) | collective-permute-done | bytes 32800 | tf_op jit(solution)/shard_map/ppermute | solution.py:585
  10.3 0.0 collective-permute-done.2.from_near
  10.3 0.1 collective-permute-done.4.high
  10.4 0.2 %collective-permute-done.1.from_far = f32[280,128]{1,0:T(8,128)S(1)} collective-permute-done((f32[280,128]{1,0:T(8,128)S(1)}, f32[280,128]{1,0:T(8,128)S(1)}, u32[]{:S(2)}, u32[]{:S(2)}) %collective-permute-start.1) | collective-permute-done | bytes 143392 | tf_op jit(solution)/shard_map/ppermute | solution.py:585
  10.6 0.5 %second.1 = (f32[128,528]{1,0:T(8,128)S(1)}, f32[456,128]{1,0:T(8,128)S(1)}, f32[168,128]{1,0:T(8,128)S(1)}, f32[4,528]{1,0:T(4,128)S(1)}, f32[8,128]{1,0:T(8,128)S(1)}) custom-call(f32[128,528]{1,0:T(8,128)S(1)} %get-tuple-element.21.total, f32[128,128]{1,0:T(8,128)S(1)} %get-tuple-element.22.columns.masses, f32[128,128]{1,0:T(8,128)S(1)} %get-tuple-element.23.operator, ...), custom_call_target="tpu_custom_call" | custom-call | tf_op jit(solution)/shard_map/second/pallas_call | solution.py:616
  11.1 0.0 copy-start.1
  11.1 0.1 collective-permute-start.5
  11.2 1.3 %collective-permute-start.6 = (f32[168,128]{1,0:T(8,128)S(1)}, f32[168,128]{1,0:T(8,128)S(1)}, u32[]{:S(2)}, u32[]{:S(2)}) collective-permute-start(f32[168,128]{1,0:T(8,128)S(1)} %get-tuple-element.33.to_far), channel_id=1, source_target_pairs={{0,24},{8,16},{16,8},{24,0},{1,25},{9,17},{17,9},{25,1},{2,26},{10... | collective-permute-start | bytes 258056 | tf_op jit(solution)/shard_map/ppermute | solution.py:585
  12.5 0.8 %collective-permute-start.7 = (f32[4,528]{1,0:T(4,128)S(1)}, f32[4,528]{1,0:T(4,128)S(1)}, u32[]{:S(2)}, u32[]{:S(2)}) collective-permute-start(f32[4,528]{1,0:T(4,128)S(1)} %get-tuple-element.34), channel_id=1, source_target_pairs={{0,16},{8,24},{16,0},{24,8},{1,17},{9,25},{17,1},{25,9},{2,18},{10... | collective-permute-start | bytes 25352 | tf_op jit(solution)/shard_map/ppermute | solution.py:585
  13.3 0.0 copy-done.1
  13.3 0.0 copy-start
  13.3 0.1 base.1
  13.4 0.0 collective-permute-done.5.refs_1_.from_near
  13.4 0.5 %copy-done = s32[4,32]{1,0:T(4,128)S(1)} copy-done((s32[4,32]{1,0:T(4,128)S(1)}, s32[4,32]{1,0:T(4,128)}, u32[]{:S(2)}) %copy-start) | copy-done | bytes 536
  14.0 0.7 %factors.1 = f32[320,128]{1,0:T(8,128)S(1)} custom-call(s32[4,32]{1,0:T(4,128)S(1)} %copy-done, f32[456,128]{1,0:T(8,128)S(1)} %get-tuple-element.32.refs_0_.to_near, f32[456,128]{1,0:T(8,128)S(1)} %collective-permute-done.5.refs_1_.from_near), custom_call_target="tpu_custom_call" | custom-call | tf_op jit(solution)/shard_map/factors/pallas_call | solution.py:616
  14.6 1.6 %collective-permute-done.7.ends_near.ends_far = f32[4,528]{1,0:T(4,128)S(1)} collective-permute-done((f32[4,528]{1,0:T(4,128)S(1)}, f32[4,528]{1,0:T(4,128)S(1)}, u32[]{:S(2)}, u32[]{:S(2)}) %collective-permute-start.7) | collective-permute-done | bytes 8480 | tf_op jit(solution)/shard_map/ppermute | solution.py:585
  16.3 0.0 collective-permute-done.6.from_far
  16.3 1.5 %third.1 = f32[4,32,528]{2,1,0:T(8,128)} custom-call(f32[1,528]{1,0:T(1,128)S(1)} %reshape.3.hyper, f32[128,528]{1,0:T(8,128)S(1)} %base.1, f32[128,128]{1,0:T(8,128)S(1)} %get-tuple-element.22.columns.masses, f32[8,128]{1,0:T(8,128)S(1)} %get-tuple-element.31.inner, f32[320,128]{1,0:T(8,128)S(1)} %factors.1, ...), custom_call_target="tpu_custom_call" | custom-call | tf_op jit(solution)/shard_map/third/pallas_call | solution.py:616
  (1 shorter events, 0.0 us)
Async XLA Ops:
  1.5 8.1 %collective-permute-start = (f32[16,640]{1,0:T(8,128)S(1)}, f32[16,640]{1,0:T(8,128)S(1)}, u32[]{:S(2)}, u32[]{:S(2)}) collective-permute-start(f32[16,640]{1,0:T(8,128)S(1)} %get-tuple-element.25), channel_id=1, source_target_pairs={{0,1},{1,2},{2,3},{3,4},{4,5},{5,6},{6,7},{7,0},{8,9},{9,10},{10,1... | collective-permute-start | bytes 122888 | tf_op jit(solution)/shard_map/ppermute | solution.py:597
  4.6 6.0 %collective-permute-start.1 = (f32[280,128]{1,0:T(8,128)S(1)}, f32[280,128]{1,0:T(8,128)S(1)}, u32[]{:S(2)}, u32[]{:S(2)}) collective-permute-start(f32[280,128]{1,0:T(8,128)S(1)} %get-tuple-element.26), channel_id=1, source_target_pairs={{0,24},{8,16},{16,8},{24,0},{1,25},{9,17},{17,9},{25,1},{2,26},{10... | collective-permute-start | bytes 430088 | tf_op jit(solution)/shard_map/ppermute | solution.py:585
  5.2 5.2 %collective-permute-start.4 = (f32[16,640]{1,0:T(8,128)S(1)}, f32[16,640]{1,0:T(8,128)S(1)}, u32[]{:S(2)}, u32[]{:S(2)}) collective-permute-start(f32[16,640]{1,0:T(8,128)S(1)} %get-tuple-element.29), channel_id=1, source_target_pairs={{0,7},{1,0},{2,1},{3,2},{4,3},{5,4},{6,5},{7,6},{8,15},{9,8},{10,9... | collective-permute-start | bytes 122888 | tf_op jit(solution)/shard_map/ppermute | solution.py:597
  8.6 1.7 %collective-permute-start.2 = (f32[72,128]{1,0:T(8,128)S(1)}, f32[72,128]{1,0:T(8,128)S(1)}, u32[]{:S(2)}, u32[]{:S(2)}) collective-permute-start(f32[72,128]{1,0:T(8,128)S(1)} %get-tuple-element.27), channel_id=1, source_target_pairs={{0,8},{8,0},{16,24},{24,16},{1,9},{9,1},{17,25},{25,17},{2,10},{10... | collective-permute-start | bytes 110600 | tf_op jit(solution)/shard_map/ppermute | solution.py:585
  9.1 1.2 %collective-permute-start.3 = (f32[64,128]{1,0:T(8,128)S(1)}, f32[64,128]{1,0:T(8,128)S(1)}, u32[]{:S(2)}, u32[]{:S(2)}) collective-permute-start(f32[64,128]{1,0:T(8,128)S(1)} %get-tuple-element.28), channel_id=1, source_target_pairs={{0,8},{8,0},{16,24},{24,16},{1,9},{9,1},{17,25},{25,17},{2,10},{10... | collective-permute-start | bytes 98312 | tf_op jit(solution)/shard_map/ppermute | solution.py:585
  11.1 2.2 %copy-start.1 = (f32[528]{0:T(1024)S(1)}, f32[528]{0:T(1024)}, u32[]{:S(2)}) copy-start(f32[528]{0:T(1024)} %param.9) | copy-start | bytes 6340
  11.1 2.3 %collective-permute-start.5 = (f32[456,128]{1,0:T(8,128)S(1)}, f32[456,128]{1,0:T(8,128)S(1)}, u32[]{:S(2)}, u32[]{:S(2)}) collective-permute-start(f32[456,128]{1,0:T(8,128)S(1)} %get-tuple-element.32.refs_0_.to_near), channel_id=1, source_target_pairs={{0,8},{8,0},{16,24},{24,16},{1,9},{9,1},{17,25},{25,17},{2,10},{10... | collective-permute-start | bytes 700424 | tf_op jit(solution)/shard_map/ppermute | solution.py:585
  11.2 5.1 %collective-permute-start.6 = (f32[168,128]{1,0:T(8,128)S(1)}, f32[168,128]{1,0:T(8,128)S(1)}, u32[]{:S(2)}, u32[]{:S(2)}) collective-permute-start(f32[168,128]{1,0:T(8,128)S(1)} %get-tuple-element.33.to_far), channel_id=1, source_target_pairs={{0,24},{8,16},{16,8},{24,0},{1,25},{9,17},{17,9},{25,1},{2,26},{10... | collective-permute-start | bytes 258056 | tf_op jit(solution)/shard_map/ppermute | solution.py:585
  12.5 3.8 %collective-permute-start.7 = (f32[4,528]{1,0:T(4,128)S(1)}, f32[4,528]{1,0:T(4,128)S(1)}, u32[]{:S(2)}, u32[]{:S(2)}) collective-permute-start(f32[4,528]{1,0:T(4,128)S(1)} %get-tuple-element.34), channel_id=1, source_target_pairs={{0,16},{8,24},{16,0},{24,8},{1,17},{9,25},{17,1},{25,9},{2,18},{10... | collective-permute-start | bytes 25352 | tf_op jit(solution)/shard_map/ppermute | solution.py:585
  13.3 0.7 %copy-start = (s32[4,32]{1,0:T(4,128)S(1)}, s32[4,32]{1,0:T(4,128)}, u32[]{:S(2)}) copy-start(s32[4,32]{1,0:T(4,128)} %slots.1) | copy-start | bytes 1540

commit v12 on v9

--- a/solution.py
+++ b/solution.py
@@ -156,7 +156,7 @@
     size_x, size_y, width = state.shape
     levels = diff.shape[1]
     pairs = [(mass, mass_here), (inverse, inverse_here)]
-    pairs += [(state.at[x], here.at[x]) for x in range(size_x)]
+    pairs.append((state, here))
     for i, source in enumerate((diff, fall, cloud)):
         pairs.append((source.at[0], coefs.at[i * levels : (i + 1) * levels]))
     copies = [
@@ -177,8 +177,7 @@
     inverses = to_column(inverse_here[...])
     lane = lax.broadcasted_iota(jnp.int32, columns.shape, 1)
     columns[...] = jnp.where(lane == 0, own, jnp.where(lane == 1, inverses, partner))
-    for copy in copies[2 : 2 + size_x]:
-        copy.wait()
+    copies[2].wait()
     total[...] = product(split(matrix), split(here[...].reshape(count, width)))
     near, far = x_rows(count, size_y)
     pack(total[near], near_rows)
@@ -191,7 +190,7 @@
             rows = slice(i * size_x, (i + 1) * size_x)
             message[rows, :width] = edge_rows(total, first + i, size_x, size_y)
             message[rows, width : width + 2] = edge_rows(columns, first + i, size_x, size_y)[:, :2]
-    for copy in copies[2 + size_x :]:
+    for copy in copies[3:]:
         copy.wait()
     if x_far.shape[0] > near_rows.shape[0]:
         x_far[near_rows.shape[0] :, :] = coefs[...]
@@ -472,7 +471,7 @@
                     solved[side] = values[k, :count, :] + gain[k : k + 1, :] * solved[side]
                 turned[pl.ds(k, count, stride=pitch), :] = solved[side]
 
-    def leave(i):
+    def place(i):
         lanes = slice(i * 128, min((i + 1) * 128, width))
         parts = []
         for (start, count), source, _ in buffers:
@@ -483,7 +482,12 @@
                     parts.append(source[first + offset : last + offset, :])
         rows = jnp.concatenate(parts, axis=0)
         staged[:, :, lanes] = rows.T.reshape(size_x, size_y, -1)
-        copy = pltpu.make_async_copy(staged.at[:, :, lanes], out.at[:, :, lanes], sems.at[i])
+
+    def leave(which, first, last):
+        for i in range(first, last):
+            place(i)
+        lanes = slice(first * 128, min(last * 128, width))
+        copy = pltpu.make_async_copy(staged.at[:, :, lanes], out.at[:, :, lanes], sems.at[which])
         copy.start()
         return copy
 
@@ -495,7 +499,7 @@
     back(main, main_turned, main_values, main_known)
     tiles = -(-width // 128)
     settled_tiles, main_tiles = -(-3 * levels // 128), main[1] * levels // 128
-    copies = [leave(i) for i in range(settled_tiles, main_tiles)]
+    copies = [leave(0, settled_tiles, main_tiles)]
     heat, vapour, liquid = (turned.at[i * pitch : i * pitch + levels] for i in range(3))
     condensed = cloud[...] * 0.5 * jnp.maximum(vapour[...] - 0.3 * heat[...], 0.0)
     vapour[...] = vapour[...] - condensed
@@ -509,8 +513,8 @@
     through = factors[6 * levels : 6 * levels + half, :]
     liquid[half:, :] = liquid[half:, :] + through * settled[0]
     back(rest, rest_turned, rest_values, rest_known)
-    copies += [leave(i) for i in range(settled_tiles)]
-    copies += [leave(i) for i in range(main_tiles, tiles)]
+    copies.append(leave(1, 0, settled_tiles))
+    copies.append(leave(2, main_tiles, tiles))
     for copy in copies:
         copy.wait()
 
@@ -649,7 +653,7 @@
             scratch(size_x, size_y),
             scratch(size_x, size_y),
             scratch(first_rows, 128),
-            pltpu.SemaphoreType.DMA((size_x + 5,)),
+            pltpu.SemaphoreType.DMA((6,)),
         ],
         *(
             pltpu.with_memory_space_constraint(value, pltpu.HBM)
@@ -734,7 +738,7 @@
             scratch(levels, 8, columns),
             scratch(levels, 8, columns),
             scratch(size_x, size_y, width),
-            pltpu.SemaphoreType.DMA((-(-width // 128),)),
+            pltpu.SemaphoreType.DMA((3,)),
         ]
         + [scratch(8, width)] * 4,
         hyper,

time: 17.8 us -> 17.8 us (level)
  no operation moved by 1% of the time
where the time goes in v12:
time: 17.8 us; the launch traced here: 17.6 us
  starting transfers between devices  9.78 us (55%)
  Pallas kernels  4.42 us (25%)
  waiting for transfers between devices  2.81 us (16%)
  local copies, waits for them, and re-layouts  0.56 us (3%)
    ppermute x2, starting transfers between devices, shifted(): lax.ppermute(value, axis, [(i, (i + step) % size) for i in range(size)])  6.41 us
    pallas_call x6, Pallas kernels, call(): pl.pallas_call(kernel, out_shape=outs, in_specs=[spec] * len(operands), o...  4.42 us
    ppermute x6, starting transfers between devices, swapped(): lax.ppermute(value, axis, [(i, partner(i)) for i in range(lax.axis_size(a...  3.37 us
    ppermute x6, waiting for transfers between devices, swapped(): lax.ppermute(value, axis, [(i, partner(i)) for i in range(lax.axis_size(a...  2.19 us
    ppermute x2, waiting for transfers between devices, shifted(): lax.ppermute(value, axis, [(i, (i + step) % size) for i in range(size)])  0.63 us
    unnamed x4, local copies, waits for them, and re-layouts  0.55 us
  transfers between devices with their start and end apart: 8, of which 5 were waited for; matrix products, arithmetic and copies ran while one was open for 0% of the time, Pallas kernels for 6%

profile of v12, /device:TPU:0, one launch (start us, length us, event | category | flops | bytes accessed | tf_op | source)
XLA Modules:
  0.0 17.6 jit_solution(7856021304978350890)
XLA Ops:
  0.0 1.4 %start.1 = (f32[4,32,528]{2,1,0:T(8,128)S(1)}, f32[128,528]{1,0:T(8,128)S(1)}, f32[72,128]{1,0:T(8,128)S(1)}, f32[64,128]{1,0:T(8,128)S(1)}, f32[280,128]{1,0:T(...) custom-call(f32[4,32,528]{2,1,0:T(8,128)} %state.1, ...), custom_call_target="tpu_custom_call" | custom-call | tf_op jit(solution)/shard_map/start/pallas_call | solution.py:620
  1.5 3.0 %collective-permute-start = (f32[16,640]{1,0:T(8,128)S(1)}, f32[16,640]{1,0:T(8,128)S(1)}, u32[]{:S(2)}, u32[]{:S(2)}) collective-permute-start(f32[16,640]{1,0:T(8,128)S(1)} %get-tuple-element.25), channel_id=1, source_target_pairs={{0,1},{1,2},{2,3},{3,4},{4,5},{5,6},{6,7},{7,0},{8,9},{9,10},{10,1... | collective-permute-start | bytes 122888 | tf_op jit(solution)/shard_map/ppermute | solution.py:601
  4.5 0.7 %collective-permute-start.1 = (f32[280,128]{1,0:T(8,128)S(1)}, f32[280,128]{1,0:T(8,128)S(1)}, u32[]{:S(2)}, u32[]{:S(2)}) collective-permute-start(f32[280,128]{1,0:T(8,128)S(1)} %get-tuple-element.26), channel_id=1, source_target_pairs={{0,24},{8,16},{16,8},{24,0},{1,25},{9,17},{17,9},{25,1},{2,26},{10... | collective-permute-start | bytes 430088 | tf_op jit(solution)/shard_map/ppermute | solution.py:589
  5.1 3.4 %collective-permute-start.4 = (f32[16,640]{1,0:T(8,128)S(1)}, f32[16,640]{1,0:T(8,128)S(1)}, u32[]{:S(2)}, u32[]{:S(2)}) collective-permute-start(f32[16,640]{1,0:T(8,128)S(1)} %get-tuple-element.29), channel_id=1, source_target_pairs={{0,7},{1,0},{2,1},{3,2},{4,3},{5,4},{6,5},{7,6},{8,15},{9,8},{10,9... | collective-permute-start | bytes 122888 | tf_op jit(solution)/shard_map/ppermute | solution.py:601
  8.5 0.5 %collective-permute-start.2 = (f32[72,128]{1,0:T(8,128)S(1)}, f32[72,128]{1,0:T(8,128)S(1)}, u32[]{:S(2)}, u32[]{:S(2)}) collective-permute-start(f32[72,128]{1,0:T(8,128)S(1)} %get-tuple-element.27), channel_id=1, source_target_pairs={{0,8},{8,0},{16,24},{24,16},{1,9},{9,1},{17,25},{25,17},{2,10},{10... | collective-permute-start | bytes 110600 | tf_op jit(solution)/shard_map/ppermute | solution.py:589
  9.0 0.0 collective-permute-start.3
  9.0 0.6 %collective-permute-done.message.low = f32[16,640]{1,0:T(8,128)S(1)} collective-permute-done((f32[16,640]{1,0:T(8,128)S(1)}, f32[16,640]{1,0:T(8,128)S(1)}, u32[]{:S(2)}, u32[]{:S(2)}) %collective-permute-start) | collective-permute-done | bytes 40992 | tf_op jit(solution)/shard_map/ppermute | solution.py:601
  9.6 0.3 %weights.1.low_weights = f32[24,128]{1,0:T(8,128)S(1)} custom-call(f32[128,128]{1,0:T(8,128)S(1)} %get-tuple-element.22.columns.masses, f32[16,640]{1,0:T(8,128)S(1)} %collective-permute-done.message.low), custom_call_target="tpu_custom_call" | custom-call | flops 99999997952 | bytes 30000000 | tf_op jit(solution)/shard_map/weights/pallas_call | solution.py:620
  9.9 0.3 %collective-permute-done.3.from_near_rest = f32[64,128]{1,0:T(8,128)S(1)} collective-permute-done((f32[64,128]{1,0:T(8,128)S(1)}, f32[64,128]{1,0:T(8,128)S(1)}, u32[]{:S(2)}, u32[]{:S(2)}) %collective-permute-start.3) | collective-permute-done | bytes 32800 | tf_op jit(solution)/shard_map/ppermute | solution.py:589
  10.2 0.0 collective-permute-done.2.from_near
  10.2 0.1 collective-permute-done.4.high
  10.3 0.2 %collective-permute-done.1.from_far = f32[280,128]{1,0:T(8,128)S(1)} collective-permute-done((f32[280,128]{1,0:T(8,128)S(1)}, f32[280,128]{1,0:T(8,128)S(1)}, u32[]{:S(2)}, u32[]{:S(2)}) %collective-permute-start.1) | collective-permute-done | bytes 143392 | tf_op jit(solution)/shard_map/ppermute | solution.py:589
  10.5 0.5 %second.1 = (f32[128,528]{1,0:T(8,128)S(1)}, f32[456,128]{1,0:T(8,128)S(1)}, f32[168,128]{1,0:T(8,128)S(1)}, f32[4,528]{1,0:T(4,128)S(1)}, f32[8,128]{1,0:T(8,128)S(1)}) custom-call(f32[128,528]{1,0:T(8,128)S(1)} %get-tuple-element.21.total, f32[128,128]{1,0:T(8,128)S(1)} %get-tuple-element.22.columns.masses, f32[128,128]{1,0:T(8,128)S(1)} %get-tuple-element.23.operator, ...), custom_call_target="tpu_custom_call" | custom-call | tf_op jit(solution)/shard_map/second/pallas_call | solution.py:620
  11.0 0.0 copy-start.1
  11.0 0.1 collective-permute-start.5
  11.1 1.3 %collective-permute-start.6 = (f32[168,128]{1,0:T(8,128)S(1)}, f32[168,128]{1,0:T(8,128)S(1)}, u32[]{:S(2)}, u32[]{:S(2)}) collective-permute-start(f32[168,128]{1,0:T(8,128)S(1)} %get-tuple-element.33.to_far), channel_id=1, source_target_pairs={{0,24},{8,16},{16,8},{24,0},{1,25},{9,17},{17,9},{25,1},{2,26},{10... | collective-permute-start | bytes 258056 | tf_op jit(solution)/shard_map/ppermute | solution.py:589
  12.4 0.8 %collective-permute-start.7 = (f32[4,528]{1,0:T(4,128)S(1)}, f32[4,528]{1,0:T(4,128)S(1)}, u32[]{:S(2)}, u32[]{:S(2)}) collective-permute-start(f32[4,528]{1,0:T(4,128)S(1)} %get-tuple-element.34), channel_id=1, source_target_pairs={{0,16},{8,24},{16,0},{24,8},{1,17},{9,25},{17,1},{25,9},{2,18},{10... | collective-permute-start | bytes 25352 | tf_op jit(solution)/shard_map/ppermute | solution.py:589
  13.2 0.0 copy-done.1
  13.2 0.0 copy-start
  13.2 0.1 base.1
  13.3 0.0 collective-permute-done.5.refs_1_.from_near
  13.3 0.5 %copy-done = s32[4,32]{1,0:T(4,128)S(1)} copy-done((s32[4,32]{1,0:T(4,128)S(1)}, s32[4,32]{1,0:T(4,128)}, u32[]{:S(2)}) %copy-start) | copy-done | bytes 536
  13.9 0.7 %factors.1 = f32[320,128]{1,0:T(8,128)S(1)} custom-call(s32[4,32]{1,0:T(4,128)S(1)} %copy-done, f32[456,128]{1,0:T(8,128)S(1)} %get-tuple-element.32.refs_0_.to_near, f32[456,128]{1,0:T(8,128)S(1)} %collective-permute-done.5.refs_1_.from_near), custom_call_target="tpu_custom_call" | custom-call | tf_op jit(solution)/shard_map/factors/pallas_call | solution.py:620
  14.6 1.6 %collective-permute-done.7.ends_near.ends_far = f32[4,528]{1,0:T(4,128)S(1)} collective-permute-done((f32[4,528]{1,0:T(4,128)S(1)}, f32[4,528]{1,0:T(4,128)S(1)}, u32[]{:S(2)}, u32[]{:S(2)}) %collective-permute-start.7) | collective-permute-done | bytes 8480 | tf_op jit(solution)/shard_map/ppermute | solution.py:589
  16.2 0.0 collective-permute-done.6.from_far
  16.2 1.4 %third.1 = f32[4,32,528]{2,1,0:T(8,128)} custom-call(f32[1,528]{1,0:T(1,128)S(1)} %reshape.3.hyper, f32[128,528]{1,0:T(8,128)S(1)} %base.1, f32[128,128]{1,0:T(8,128)S(1)} %get-tuple-element.22.columns.masses, f32[8,128]{1,0:T(8,128)S(1)} %get-tuple-element.31.inner, f32[320,128]{1,0:T(8,128)S(1)} %factors.1, ...), custom_call_target="tpu_custom_call" | custom-call | tf_op jit(solution)/shard_map/third/pallas_call | solution.py:620
  (1 shorter events, 0.0 us)
Async XLA Ops:
  1.5 8.1 %collective-permute-start = (f32[16,640]{1,0:T(8,128)S(1)}, f32[16,640]{1,0:T(8,128)S(1)}, u32[]{:S(2)}, u32[]{:S(2)}) collective-permute-start(f32[16,640]{1,0:T(8,128)S(1)} %get-tuple-element.25), channel_id=1, source_target_pairs={{0,1},{1,2},{2,3},{3,4},{4,5},{5,6},{6,7},{7,0},{8,9},{9,10},{10,1... | collective-permute-start | bytes 122888 | tf_op jit(solution)/shard_map/ppermute | solution.py:601
  4.5 6.0 %collective-permute-start.1 = (f32[280,128]{1,0:T(8,128)S(1)}, f32[280,128]{1,0:T(8,128)S(1)}, u32[]{:S(2)}, u32[]{:S(2)}) collective-permute-start(f32[280,128]{1,0:T(8,128)S(1)} %get-tuple-element.26), channel_id=1, source_target_pairs={{0,24},{8,16},{16,8},{24,0},{1,25},{9,17},{17,9},{25,1},{2,26},{10... | collective-permute-start | bytes 430088 | tf_op jit(solution)/shard_map/ppermute | solution.py:589
  5.1 5.1 %collective-permute-start.4 = (f32[16,640]{1,0:T(8,128)S(1)}, f32[16,640]{1,0:T(8,128)S(1)}, u32[]{:S(2)}, u32[]{:S(2)}) collective-permute-start(f32[16,640]{1,0:T(8,128)S(1)} %get-tuple-element.29), channel_id=1, source_target_pairs={{0,7},{1,0},{2,1},{3,2},{4,3},{5,4},{6,5},{7,6},{8,15},{9,8},{10,9... | collective-permute-start | bytes 122888 | tf_op jit(solution)/shard_map/ppermute | solution.py:601
  8.5 1.7 %collective-permute-start.2 = (f32[72,128]{1,0:T(8,128)S(1)}, f32[72,128]{1,0:T(8,128)S(1)}, u32[]{:S(2)}, u32[]{:S(2)}) collective-permute-start(f32[72,128]{1,0:T(8,128)S(1)} %get-tuple-element.27), channel_id=1, source_target_pairs={{0,8},{8,0},{16,24},{24,16},{1,9},{9,1},{17,25},{25,17},{2,10},{10... | collective-permute-start | bytes 110600 | tf_op jit(solution)/shard_map/ppermute | solution.py:589
  9.0 1.2 %collective-permute-start.3 = (f32[64,128]{1,0:T(8,128)S(1)}, f32[64,128]{1,0:T(8,128)S(1)}, u32[]{:S(2)}, u32[]{:S(2)}) collective-permute-start(f32[64,128]{1,0:T(8,128)S(1)} %get-tuple-element.28), channel_id=1, source_target_pairs={{0,8},{8,0},{16,24},{24,16},{1,9},{9,1},{17,25},{25,17},{2,10},{10... | collective-permute-start | bytes 98312 | tf_op jit(solution)/shard_map/ppermute | solution.py:589
  11.0 2.2 %copy-start.1 = (f32[528]{0:T(1024)S(1)}, f32[528]{0:T(1024)}, u32[]{:S(2)}) copy-start(f32[528]{0:T(1024)} %param.9) | copy-start | bytes 6340
  11.0 2.3 %collective-permute-start.5 = (f32[456,128]{1,0:T(8,128)S(1)}, f32[456,128]{1,0:T(8,128)S(1)}, u32[]{:S(2)}, u32[]{:S(2)}) collective-permute-start(f32[456,128]{1,0:T(8,128)S(1)} %get-tuple-element.32.refs_0_.to_near), channel_id=1, source_target_pairs={{0,8},{8,0},{16,24},{24,16},{1,9},{9,1},{17,25},{25,17},{2,10},{10... | collective-permute-start | bytes 700424 | tf_op jit(solution)/shard_map/ppermute | solution.py:589
  11.1 5.1 %collective-permute-start.6 = (f32[168,128]{1,0:T(8,128)S(1)}, f32[168,128]{1,0:T(8,128)S(1)}, u32[]{:S(2)}, u32[]{:S(2)}) collective-permute-start(f32[168,128]{1,0:T(8,128)S(1)} %get-tuple-element.33.to_far), channel_id=1, source_target_pairs={{0,24},{8,16},{16,8},{24,0},{1,25},{9,17},{17,9},{25,1},{2,26},{10... | collective-permute-start | bytes 258056 | tf_op jit(solution)/shard_map/ppermute | solution.py:589
  12.4 3.8 %collective-permute-start.7 = (f32[4,528]{1,0:T(4,128)S(1)}, f32[4,528]{1,0:T(4,128)S(1)}, u32[]{:S(2)}, u32[]{:S(2)}) collective-permute-start(f32[4,528]{1,0:T(4,128)S(1)} %get-tuple-element.34), channel_id=1, source_target_pairs={{0,16},{8,24},{16,0},{24,8},{1,17},{9,25},{17,1},{25,9},{2,18},{10... | collective-permute-start | bytes 25352 | tf_op jit(solution)/shard_map/ppermute | solution.py:589
  13.2 0.7 %copy-start = (s32[4,32]{1,0:T(4,128)S(1)}, s32[4,32]{1,0:T(4,128)}, u32[]{:S(2)}) copy-start(s32[4,32]{1,0:T(4,128)} %slots.1) | copy-start | bytes 1540

commit v13 on v12

--- a/solution.py
+++ b/solution.py
@@ -286,17 +286,22 @@
     work,
     at_near,
     at_far,
-    near_rows,
 ):
     size_y, width = total.shape[0] // size_x, total.shape[1]
     depth = size_y + 8
     second = second_table()
     near, far = x_starts(size_x * size_y, size_y)
     work[...] = total[...]
-    rest = from_near_rest.shape[0]
-    near_rows[:rest, :] = from_near_rest[...]
-    near_rows[rest:, :] = from_near[...]
-    add_packed(work, near, near_rows, size_y)
+    half, left = from_near_rest.shape[0] // size_y, width % 128
+    for message, first in ((from_near_rest, 0), (from_near, half)):
+        for i in range(half):
+            lanes = slice((first + i) * 128, (first + i + 1) * 128)
+            rows = pl.ds(pl.multiple_of(near, size_y), size_y)
+            work[rows, lanes] += message[i * size_y : (i + 1) * size_y, :]
+    for i in range(size_y // 8):
+        rows = pl.ds(pl.multiple_of(near + i * 8, 8), 8)
+        value = from_near[half * size_y :, i * left : (i + 1) * left]
+        work[rows, width - left :] += value
     add_packed(work, far, from_far, size_y)
     sides = ((low, 0, 3, 0), (high, size_y - 1, 0, size_y - 8))
     beyond = []
@@ -695,7 +700,6 @@
             scratch(columns, width),
             scratch(size_y + 8, width),
             scratch(size_y + 8, width),
-            scratch(first_rows, 128),
         ],
         total,
         masses,

time: 17.8 us -> 17.8 us (level)
  no operation moved by 1% of the time
where the time goes in v13:
time: 17.8 us; the launch traced here: 17.6 us
  starting transfers between devices  9.74 us (55%)
  Pallas kernels  4.4 us (25%)
  waiting for transfers between devices  2.88 us (16%)
  local copies, waits for them, and re-layouts  0.56 us (3%)
    ppermute x2, starting transfers between devices, shifted(): lax.ppermute(value, axis, [(i, (i + step) % size) for i in range(size)])  6.41 us
    pallas_call x6, Pallas kernels, call(): pl.pallas_call(kernel, out_shape=outs, in_specs=[spec] * len(operands), o...  4.4 us
    ppermute x6, starting transfers between devices, swapped(): lax.ppermute(value, axis, [(i, partner(i)) for i in range(lax.axis_size(a...  3.33 us
    ppermute x6, waiting for transfers between devices, swapped(): lax.ppermute(value, axis, [(i, partner(i)) for i in range(lax.axis_size(a...  2.25 us
    ppermute x2, waiting for transfers between devices, shifted(): lax.ppermute(value, axis, [(i, (i + step) % size) for i in range(size)])  0.63 us
    unnamed x4, local copies, waits for them, and re-layouts  0.55 us
  transfers between devices with their start and end apart: 8, of which 5 were waited for; matrix products, arithmetic and copies ran while one was open for 0% of the time, Pallas kernels for 6%

profile of v13, /device:TPU:0, one launch (start us, length us, event | category | flops | bytes accessed | tf_op | source)
XLA Modules:
  0.0 17.6 jit_solution(10197472233925376648)
XLA Ops:
  0.0 1.4 %start.1 = (f32[4,32,528]{2,1,0:T(8,128)S(1)}, f32[128,528]{1,0:T(8,128)S(1)}, f32[72,128]{1,0:T(8,128)S(1)}, f32[64,128]{1,0:T(8,128)S(1)}, f32[280,128]{1,0:T(...) custom-call(f32[4,32,528]{2,1,0:T(8,128)} %state.1, ...), custom_call_target="tpu_custom_call" | custom-call | tf_op jit(solution)/shard_map/start/pallas_call | solution.py:625
  1.5 3.0 %collective-permute-start = (f32[16,640]{1,0:T(8,128)S(1)}, f32[16,640]{1,0:T(8,128)S(1)}, u32[]{:S(2)}, u32[]{:S(2)}) collective-permute-start(f32[16,640]{1,0:T(8,128)S(1)} %get-tuple-element.25), channel_id=1, source_target_pairs={{0,1},{1,2},{2,3},{3,4},{4,5},{5,6},{6,7},{7,0},{8,9},{9,10},{10,1... | collective-permute-start | bytes 122888 | tf_op jit(solution)/shard_map/ppermute | solution.py:606
  4.5 0.7 %collective-permute-start.1 = (f32[280,128]{1,0:T(8,128)S(1)}, f32[280,128]{1,0:T(8,128)S(1)}, u32[]{:S(2)}, u32[]{:S(2)}) collective-permute-start(f32[280,128]{1,0:T(8,128)S(1)} %get-tuple-element.26), channel_id=1, source_target_pairs={{0,24},{8,16},{16,8},{24,0},{1,25},{9,17},{17,9},{25,1},{2,26},{10... | collective-permute-start | bytes 430088 | tf_op jit(solution)/shard_map/ppermute | solution.py:594
  5.1 3.4 %collective-permute-start.4 = (f32[16,640]{1,0:T(8,128)S(1)}, f32[16,640]{1,0:T(8,128)S(1)}, u32[]{:S(2)}, u32[]{:S(2)}) collective-permute-start(f32[16,640]{1,0:T(8,128)S(1)} %get-tuple-element.29), channel_id=1, source_target_pairs={{0,7},{1,0},{2,1},{3,2},{4,3},{5,4},{6,5},{7,6},{8,15},{9,8},{10,9... | collective-permute-start | bytes 122888 | tf_op jit(solution)/shard_map/ppermute | solution.py:606
  8.5 0.5 %collective-permute-start.2 = (f32[72,128]{1,0:T(8,128)S(1)}, f32[72,128]{1,0:T(8,128)S(1)}, u32[]{:S(2)}, u32[]{:S(2)}) collective-permute-start(f32[72,128]{1,0:T(8,128)S(1)} %get-tuple-element.27), channel_id=1, source_target_pairs={{0,8},{8,0},{16,24},{24,16},{1,9},{9,1},{17,25},{25,17},{2,10},{10... | collective-permute-start | bytes 110600 | tf_op jit(solution)/shard_map/ppermute | solution.py:594
  9.0 0.0 collective-permute-start.3
  9.0 0.6 %collective-permute-done.message.low = f32[16,640]{1,0:T(8,128)S(1)} collective-permute-done((f32[16,640]{1,0:T(8,128)S(1)}, f32[16,640]{1,0:T(8,128)S(1)}, u32[]{:S(2)}, u32[]{:S(2)}) %collective-permute-start) | collective-permute-done | bytes 40992 | tf_op jit(solution)/shard_map/ppermute | solution.py:606
  9.6 0.3 %weights.1.low_weights = f32[24,128]{1,0:T(8,128)S(1)} custom-call(f32[128,128]{1,0:T(8,128)S(1)} %get-tuple-element.22.columns.masses, f32[16,640]{1,0:T(8,128)S(1)} %collective-permute-done.message.low), custom_call_target="tpu_custom_call" | custom-call | flops 99999997952 | bytes 30000000 | tf_op jit(solution)/shard_map/weights/pallas_call | solution.py:625
  9.9 0.3 %collective-permute-done.3.from_near_rest = f32[64,128]{1,0:T(8,128)S(1)} collective-permute-done((f32[64,128]{1,0:T(8,128)S(1)}, f32[64,128]{1,0:T(8,128)S(1)}, u32[]{:S(2)}, u32[]{:S(2)}) %collective-permute-start.3) | collective-permute-done | bytes 32800 | tf_op jit(solution)/shard_map/ppermute | solution.py:594
  10.2 0.0 collective-permute-done.2.from_near
  10.2 0.1 collective-permute-done.4.high
  10.3 0.2 %collective-permute-done.1.from_far = f32[280,128]{1,0:T(8,128)S(1)} collective-permute-done((f32[280,128]{1,0:T(8,128)S(1)}, f32[280,128]{1,0:T(8,128)S(1)}, u32[]{:S(2)}, u32[]{:S(2)}) %collective-permute-start.1) | collective-permute-done | bytes 143392 | tf_op jit(solution)/shard_map/ppermute | solution.py:594
  10.5 0.5 %second.1 = (f32[128,528]{1,0:T(8,128)S(1)}, f32[456,128]{1,0:T(8,128)S(1)}, f32[168,128]{1,0:T(8,128)S(1)}, f32[4,528]{1,0:T(4,128)S(1)}, f32[8,128]{1,0:T(8,128)S(1)}) custom-call(f32[128,528]{1,0:T(8,128)S(1)} %get-tuple-element.21.total, f32[128,128]{1,0:T(8,128)S(1)} %get-tuple-element.22.columns.masses, f32[128,128]{1,0:T(8,128)S(1)} %get-tuple-element.23.operator, ...), custom_call_target="tpu_custom_call" | custom-call | tf_op jit(solution)/shard_map/second/pallas_call | solution.py:625
  11.0 0.0 copy-start.1
  11.0 0.1 collective-permute-start.5
  11.1 1.3 %collective-permute-start.6 = (f32[168,128]{1,0:T(8,128)S(1)}, f32[168,128]{1,0:T(8,128)S(1)}, u32[]{:S(2)}, u32[]{:S(2)}) collective-permute-start(f32[168,128]{1,0:T(8,128)S(1)} %get-tuple-element.33.to_far), channel_id=1, source_target_pairs={{0,24},{8,16},{16,8},{24,0},{1,25},{9,17},{17,9},{25,1},{2,26},{10... | collective-permute-start | bytes 258056 | tf_op jit(solution)/shard_map/ppermute | solution.py:594
  12.4 0.7 %collective-permute-start.7 = (f32[4,528]{1,0:T(4,128)S(1)}, f32[4,528]{1,0:T(4,128)S(1)}, u32[]{:S(2)}, u32[]{:S(2)}) collective-permute-start(f32[4,528]{1,0:T(4,128)S(1)} %get-tuple-element.34), channel_id=1, source_target_pairs={{0,16},{8,24},{16,0},{24,8},{1,17},{9,25},{17,1},{25,9},{2,18},{10... | collective-permute-start | bytes 25352 | tf_op jit(solution)/shard_map/ppermute | solution.py:594
  13.2 0.0 copy-done.1
  13.2 0.0 copy-start
  13.2 0.1 base.1
  13.3 0.0 collective-permute-done.5.refs_1_.from_near
  13.3 0.5 %copy-done = s32[4,32]{1,0:T(4,128)S(1)} copy-done((s32[4,32]{1,0:T(4,128)S(1)}, s32[4,32]{1,0:T(4,128)}, u32[]{:S(2)}) %copy-start) | copy-done | bytes 536
  13.8 0.7 %factors.1 = f32[320,128]{1,0:T(8,128)S(1)} custom-call(s32[4,32]{1,0:T(4,128)S(1)} %copy-done, f32[456,128]{1,0:T(8,128)S(1)} %get-tuple-element.32.refs_0_.to_near, f32[456,128]{1,0:T(8,128)S(1)} %collective-permute-done.5.refs_1_.from_near), custom_call_target="tpu_custom_call" | custom-call | tf_op jit(solution)/shard_map/factors/pallas_call | solution.py:625
  14.5 1.7 %collective-permute-done.7.ends_near.ends_far = f32[4,528]{1,0:T(4,128)S(1)} collective-permute-done((f32[4,528]{1,0:T(4,128)S(1)}, f32[4,528]{1,0:T(4,128)S(1)}, u32[]{:S(2)}, u32[]{:S(2)}) %collective-permute-start.7) | collective-permute-done | bytes 8480 | tf_op jit(solution)/shard_map/ppermute | solution.py:594
  16.2 0.0 collective-permute-done.6.from_far
  16.2 1.4 %third.1 = f32[4,32,528]{2,1,0:T(8,128)} custom-call(f32[1,528]{1,0:T(1,128)S(1)} %reshape.3.hyper, f32[128,528]{1,0:T(8,128)S(1)} %base.1, f32[128,128]{1,0:T(8,128)S(1)} %get-tuple-element.22.columns.masses, f32[8,128]{1,0:T(8,128)S(1)} %get-tuple-element.31.inner, f32[320,128]{1,0:T(8,128)S(1)} %factors.1, ...), custom_call_target="tpu_custom_call" | custom-call | tf_op jit(solution)/shard_map/third/pallas_call | solution.py:625
  (1 shorter events, 0.0 us)
Async XLA Ops:
  1.5 8.1 %collective-permute-start = (f32[16,640]{1,0:T(8,128)S(1)}, f32[16,640]{1,0:T(8,128)S(1)}, u32[]{:S(2)}, u32[]{:S(2)}) collective-permute-start(f32[16,640]{1,0:T(8,128)S(1)} %get-tuple-element.25), channel_id=1, source_target_pairs={{0,1},{1,2},{2,3},{3,4},{4,5},{5,6},{6,7},{7,0},{8,9},{9,10},{10,1... | collective-permute-start | bytes 122888 | tf_op jit(solution)/shard_map/ppermute | solution.py:606
  4.5 6.0 %collective-permute-start.1 = (f32[280,128]{1,0:T(8,128)S(1)}, f32[280,128]{1,0:T(8,128)S(1)}, u32[]{:S(2)}, u32[]{:S(2)}) collective-permute-start(f32[280,128]{1,0:T(8,128)S(1)} %get-tuple-element.26), channel_id=1, source_target_pairs={{0,24},{8,16},{16,8},{24,0},{1,25},{9,17},{17,9},{25,1},{2,26},{10... | collective-permute-start | bytes 430088 | tf_op jit(solution)/shard_map/ppermute | solution.py:594
  5.1 5.1 %collective-permute-start.4 = (f32[16,640]{1,0:T(8,128)S(1)}, f32[16,640]{1,0:T(8,128)S(1)}, u32[]{:S(2)}, u32[]{:S(2)}) collective-permute-start(f32[16,640]{1,0:T(8,128)S(1)} %get-tuple-element.29), channel_id=1, source_target_pairs={{0,7},{1,0},{2,1},{3,2},{4,3},{5,4},{6,5},{7,6},{8,15},{9,8},{10,9... | collective-permute-start | bytes 122888 | tf_op jit(solution)/shard_map/ppermute | solution.py:606
  8.5 1.7 %collective-permute-start.2 = (f32[72,128]{1,0:T(8,128)S(1)}, f32[72,128]{1,0:T(8,128)S(1)}, u32[]{:S(2)}, u32[]{:S(2)}) collective-permute-start(f32[72,128]{1,0:T(8,128)S(1)} %get-tuple-element.27), channel_id=1, source_target_pairs={{0,8},{8,0},{16,24},{24,16},{1,9},{9,1},{17,25},{25,17},{2,10},{10... | collective-permute-start | bytes 110600 | tf_op jit(solution)/shard_map/ppermute | solution.py:594
  9.0 1.2 %collective-permute-start.3 = (f32[64,128]{1,0:T(8,128)S(1)}, f32[64,128]{1,0:T(8,128)S(1)}, u32[]{:S(2)}, u32[]{:S(2)}) collective-permute-start(f32[64,128]{1,0:T(8,128)S(1)} %get-tuple-element.28), channel_id=1, source_target_pairs={{0,8},{8,0},{16,24},{24,16},{1,9},{9,1},{17,25},{25,17},{2,10},{10... | collective-permute-start | bytes 98312 | tf_op jit(solution)/shard_map/ppermute | solution.py:594
  11.0 2.2 %copy-start.1 = (f32[528]{0:T(1024)S(1)}, f32[528]{0:T(1024)}, u32[]{:S(2)}) copy-start(f32[528]{0:T(1024)} %param.9) | copy-start | bytes 6340
  11.0 2.3 %collective-permute-start.5 = (f32[456,128]{1,0:T(8,128)S(1)}, f32[456,128]{1,0:T(8,128)S(1)}, u32[]{:S(2)}, u32[]{:S(2)}) collective-permute-start(f32[456,128]{1,0:T(8,128)S(1)} %get-tuple-element.32.refs_0_.to_near), channel_id=1, source_target_pairs={{0,8},{8,0},{16,24},{24,16},{1,9},{9,1},{17,25},{25,17},{2,10},{10... | collective-permute-start | bytes 700424 | tf_op jit(solution)/shard_map/ppermute | solution.py:594
  11.1 5.1 %collective-permute-start.6 = (f32[168,128]{1,0:T(8,128)S(1)}, f32[168,128]{1,0:T(8,128)S(1)}, u32[]{:S(2)}, u32[]{:S(2)}) collective-permute-start(f32[168,128]{1,0:T(8,128)S(1)} %get-tuple-element.33.to_far), channel_id=1, source_target_pairs={{0,24},{8,16},{16,8},{24,0},{1,25},{9,17},{17,9},{25,1},{2,26},{10... | collective-permute-start | bytes 258056 | tf_op jit(solution)/shard_map/ppermute | solution.py:594
  12.4 3.8 %collective-permute-start.7 = (f32[4,528]{1,0:T(4,128)S(1)}, f32[4,528]{1,0:T(4,128)S(1)}, u32[]{:S(2)}, u32[]{:S(2)}) collective-permute-start(f32[4,528]{1,0:T(4,128)S(1)} %get-tuple-element.34), channel_id=1, source_target_pairs={{0,16},{8,24},{16,0},{24,8},{1,17},{9,25},{17,1},{25,9},{2,18},{10... | collective-permute-start | bytes 25352 | tf_op jit(solution)/shard_map/ppermute | solution.py:594
  13.2 0.7 %copy-start = (s32[4,32]{1,0:T(4,128)S(1)}, s32[4,32]{1,0:T(4,128)}, u32[]{:S(2)}) copy-start(s32[4,32]{1,0:T(4,128)} %slots.1) | copy-start | bytes 1540
